TPU v7x, 128 devices: a whole 4x4x4 slice. The times are simulated.
128 devices in a mesh: section: 2 (over core), replica: 32 (over z, y, x_lo), tensor: 2 (over x_hi).
Axes of the slice: x: 4 (x_hi: 2, x_lo: 2; x = x_hi * 2 + x_lo), y: 4, z: 4, core: 2. Of those that a mesh axis runs over, the one named last changes fastest.
Arguments:
- source_slot: int32 [192], replicated, may hold values from 0 to 191, as said below
- lengths: int32 [192], replicated, may hold values from 1 to 1280, as said below
- block_table: int32 [192, 80], P('replica'), may hold values from 0 to 479, as said below
- queries: bfloat16 [2, 192, 8192], P('section', 'replica', 'tensor'), may hold values from -32 to 32
- kv_pool: bfloat16 [2, 2, 15360, 16, 1024], P('section', None, 'replica', None, 'tensor'), may hold values from -8 to 8
- new_kv: bfloat16 [2, 2, 192, 1024], P('section', None, 'replica', 'tensor'), may hold values from -8 to 8
- ssm_state: float32 [2, 192, 16, 16384], P('section', 'replica', None, 'tensor'), may hold values from -6 to 6
- conv_out: bfloat16 [2, 192, 16384], P('section', 'replica', 'tensor'), may hold values from -6 to 6
- dt_raw: bfloat16 [2, 192, 16384], P('section', 'replica', 'tensor'), may hold values from -6 to 6
- x_proj: bfloat16 [2, 32, 16384], P('section', None, 'tensor'), may hold values from -0.046875 to 0.046875
- a_log: float32 [2, 16, 16384], P('section', None, 'tensor'), may hold values from -3 to 1.5
- dt_bias: float32 [2, 16384], P('section', 'tensor'), may hold values from -4 to 0
- skip_gain: float32 [2, 16384], P('section', 'tensor'), may hold values from 0.5 to 1.5
Outputs:
- handed_mamba: bfloat16 [2, 192, 16384], P('section', 'replica', 'tensor')
- handed_attention: bfloat16 [2, 192, 8192], P('section', 'replica', 'tensor')
- new_state: float32 [2, 192, 16, 16384], P('section', 'replica', None, 'tensor')
Inputs may be any that keep to these rules, and one draw needn't show every extreme that they name: `source_slot`: slot g belongs to replica g // 6; the entries form a permutation of the slots; for every bit b below 5, each replica gives exactly one request to the replica whose index differs from its own in bit b and takes exactly one request from it; the other slots keep their requests. `lengths`: some slot holds exactly 1280 tokens. `block_table`: the rows of one replica's 6 slots together name each of its pages once.
All inputs are finite; a program needn't handle non-finite values.
Results may differ from a plain program's by a relative error of at most 0.0055.
Values may be sent and summed in bfloat16 or wider, within the bound.
No kernel may reach another device: no remote copies, remote signals or barrier semaphores. Data moves between devices by JAX's collectives and lax.ppermute only.
A program may use at most 192 MiB of HBM per device.

v0:
```python
import jax
import jax.numpy as jnp
from jax import lax
from jax.sharding import PartitionSpec as P

HEADS = 64
KVH = 8
HD = 128


masked_score = -1e30


def swapped(value, axis, bit):
    mask = 2**bit
    pairs = [(source, source ^ mask) for source in range(lax.axis_size(axis))]
    return lax.ppermute(value, axis, pairs)


def from_behind(value, axis, steps):
    count = lax.axis_size(axis)
    pairs = [(source, (source + steps) % count) for source in range(count)]
    return lax.ppermute(value, axis, pairs)


def cache_partial(head_rows, key_rows, value_rows, allowed):
    row_count, kv_local, group_size, head_size = head_rows.shape
    token_count = key_rows.shape[0]
    diagonal = jnp.eye(kv_local, dtype=head_rows.dtype)
    spread = (head_rows[:, :, :, None, :] * diagonal[None, :, None, :, None]).reshape(
        row_count * kv_local * group_size, kv_local * head_size
    )
    scores = lax.dot_general(
        spread, key_rows, (((1,), (1,)), ((), ())), preferred_element_type=jnp.float32
    ) * head_size ** (-0.5)
    scores = scores.reshape(row_count, kv_local * group_size, token_count)
    usable = allowed[:, None, :]
    masked = jnp.where(usable, scores, masked_score)
    cache_peak = jnp.max(masked, axis=-1)
    weights = jnp.where(usable, jnp.exp(masked - cache_peak[..., None]), 0.0)
    cache_total = jnp.sum(weights, axis=-1)
    rounded = weights.astype(jnp.bfloat16).reshape(row_count * kv_local * group_size, token_count)
    full = jnp.dot(rounded, value_rows, preferred_element_type=jnp.float32)
    full = full.reshape(row_count, kv_local, group_size, kv_local, head_size)
    gathered = jnp.sum(full * diagonal.astype(jnp.float32)[None, :, None, :, None], axis=3)
    return (
        cache_peak.reshape(row_count, kv_local, group_size),
        cache_total.reshape(row_count, kv_local, group_size),
        gathered,
    )


def combine_own(cache_peak, cache_total, gathered, head_rows, fresh_rows):
    row_count, kv_local, group_size, head_size = head_rows.shape
    own_keys = fresh_rows[0].reshape(row_count, kv_local, head_size)
    own_values = fresh_rows[1].reshape(row_count, kv_local, head_size).astype(jnp.float32)
    own_score = jnp.einsum(
        "nkgd,nkd->nkg", head_rows, own_keys, preferred_element_type=jnp.float32
    ) * head_size ** (-0.5)
    joint_peak = jnp.maximum(cache_peak, own_score)
    cache_weight = jnp.exp(cache_peak - joint_peak)
    own_weight = jnp.exp(own_score - joint_peak)
    numerator = (
        cache_weight[..., None] * gathered + own_weight[..., None] * own_values[:, :, None, :]
    )
    attended = numerator / (cache_weight * cache_total + own_weight)[..., None]
    return attended.reshape(row_count, kv_local * group_size * head_size).astype(jnp.bfloat16)


def per_device(
    source_slot,
    lengths,
    block_table,
    queries,
    kv_pool,
    new_kv,
    ssm_state,
    conv_out,
    dt_raw,
    x_proj,
    a_log,
    dt_bias,
    skip_gain,
):
    slot_count = ssm_state.shape[1]
    replica_count = lax.axis_size("replica")
    bit_count = replica_count.bit_length() - 1
    own_index = lax.axis_index("replica")
    slot_plan = source_slot.reshape(replica_count, slot_count)
    incoming = lax.dynamic_index_in_dim(slot_plan, own_index, 0, keepdims=False)
    anchor = incoming // slot_count
    moved_in = anchor != own_index
    slot_ids = jnp.arange(slot_count, dtype=jnp.int32)
    leave_slots = []
    ask_slots = []
    served_list = []
    for bit in range(bit_count):
        partner = jnp.bitwise_xor(own_index, 1 << bit)
        partner_row = lax.dynamic_index_in_dim(slot_plan, partner, 0, keepdims=False)
        giving = partner_row // slot_count == own_index
        position = jnp.argmax(giving.astype(jnp.int32))
        leave_slots.append(partner_row[position] % slot_count)
        served_list.append(lengths[partner * slot_count + position])
        ask_slots.append(jnp.argmax((anchor == partner).astype(jnp.int32)))
    states_here = ssm_state[0]
    previous = states_here
    for bit in range(bit_count):
        arrived = swapped(states_here[leave_slots[bit]], "replica", bit)
        taken = slot_ids == ask_slots[bit]
        previous = jnp.where(taken[:, None, None], arrived[None], previous)
    mixer_in = conv_out[0]
    step_size = jax.nn.softplus(dt_raw[0].astype(jnp.float32) + dt_bias[0])
    partial_gain = jnp.einsum("sc,nc->sn", mixer_in, x_proj[0], preferred_element_type=jnp.float32)
    coupled = lax.psum(partial_gain, "tensor")
    state_count = x_proj.shape[1] // 2
    input_gain = coupled[:, :state_count]
    read_gain = coupled[:, state_count:]
    mixer_float = mixer_in.astype(jnp.float32)
    decay_rate = jnp.exp(-step_size[:, None, :] * jnp.exp(a_log[0])[None, :, :])
    updated = decay_rate * previous + (step_size * mixer_float)[:, None, :] * input_gain[:, :, None]
    mixed_rows = (
        jnp.sum(read_gain[:, :, None] * updated, axis=1) + skip_gain[0] * mixer_float
    ).astype(jnp.bfloat16)
    pool_here = kv_pool[0]
    fresh_rows = new_kv[0]
    page_total = pool_here.shape[1]
    page_size = pool_here.shape[2]
    row_width = pool_here.shape[-1]
    pages_each = block_table.shape[1]
    kv_local = row_width // HD
    group_size = HEADS // KVH
    head_rows = queries[0].reshape(slot_count, kv_local, group_size, HD)
    own_lengths = lax.dynamic_slice_in_dim(lengths, own_index * slot_count, slot_count)
    pool_keys = pool_here[0].reshape(page_total * page_size, row_width)
    pool_values = pool_here[1].reshape(page_total * page_size, row_width)
    flat_pages = block_table.reshape(-1)
    page_owner = (
        jnp.zeros((page_total,), jnp.int32).at[flat_pages].set(jnp.repeat(slot_ids, pages_each))
    )
    page_place = (
        jnp.zeros((page_total,), jnp.int32)
        .at[flat_pages]
        .set(jnp.tile(jnp.arange(pages_each, dtype=jnp.int32), slot_count))
    )
    token_owner = jnp.broadcast_to(page_owner[:, None], (page_total, page_size)).reshape(-1)
    token_place = (
        page_place[:, None] * page_size + jnp.arange(page_size, dtype=jnp.int32)[None, :]
    ).reshape(-1)
    near_allowed = (
        (token_owner[None, :] == slot_ids[:, None])
        & (token_place[None, :] < own_lengths[:, None])
        & jnp.logical_not(moved_in)[:, None]
    )
    cache_peak, cache_total, gathered = cache_partial(
        head_rows, pool_keys, pool_values, near_allowed
    )
    for bit in range(bit_count):
        leaving = pool_here[:, block_table[leave_slots[bit]]]
        carried = swapped(leaving, "replica", bit)
        taker = ask_slots[bit]
        far_keys = carried[0].reshape(pages_each * page_size, row_width)
        far_values = carried[1].reshape(pages_each * page_size, row_width)
        far_allowed = (jnp.arange(pages_each * page_size, dtype=jnp.int32) < own_lengths[taker])[
            None, :
        ]
        far_peak, far_total, far_gathered = cache_partial(
            head_rows[taker][None], far_keys, far_values, far_allowed
        )
        taken = slot_ids == taker
        cache_peak = jnp.where(taken[:, None, None], far_peak, cache_peak)
        cache_total = jnp.where(taken[:, None, None], far_total, cache_total)
        gathered = jnp.where(taken[:, None, None, None], far_gathered, gathered)
    attended = combine_own(cache_peak, cache_total, gathered, head_rows, fresh_rows)
    handed = from_behind((mixed_rows[None], attended[None]), "section", 1)
    return (handed[0], handed[1], updated[None])


def solution(mesh):
    in_specs = (
        P(),
        P(),
        P("replica", None),
        P("section", "replica", "tensor"),
        P("section", None, "replica", None, "tensor"),
        P("section", None, "replica", "tensor"),
        P("section", "replica", None, "tensor"),
        P("section", "replica", "tensor"),
        P("section", "replica", "tensor"),
        P("section", None, "tensor"),
        P("section", None, "tensor"),
        P("section", "tensor"),
        P("section", "tensor"),
    )
    out_specs = (
        P("section", "replica", "tensor"),
        P("section", "replica", "tensor"),
        P("section", "replica", None, "tensor"),
    )
    return jax.shard_map(
        per_device, mesh=mesh, in_specs=in_specs, out_specs=out_specs, check_vma=False
    )
```

profile of v0, /device:TPU:1, one launch (start us, length us, event | category | flops | bytes accessed | tf_op | source)
XLA Modules:
  0.0 313.4 jit_solution(825722809073287214)
XLA Ops:
  18.6 3.3 %dynamic-slice_bitcast_fusion.4 = (f32[16,8192]{1,0:T(8,128)}, f32[16,8192]{1,0:T(8,128)}, f32[16,8192]{1,0:T(8,128)}, f32[16,8192]{1,0:T(8,128)}, f32[16,8192]{1,0:T(8,128)}) fusion(f32[1,6,16,8192]{3,2,1,0:T(8,128)} %param.19, s32[]{:T(128)S(6)} %select_n.430, s32[]{:T(128)S(6)} %select_n.458, s32[]{:T(128)S(6)} %select_n.451, s32[]{:T(128)S(6)} %select_n.444, ...), kind=kLoop, calls=%fused_computation.51 | loop fusion | bytes 5242900 | tf_op jit(solution)/shard_map/squeeze | solution.py:108
  21.9 4.4 %collective-permute-start = (f32[16,8192]{1,0:T(8,128)}, f32[16,8192]{1,0:T(8,128)}, u32[]{:S(2)}, u32[]{:S(2)}) collective-permute-start(f32[16,8192]{1,0:T(8,128)} %get-tuple-element.32), channel_id=1, source_target_pairs={{0,32},{2,34},{4,36},{6,38},{8,40},{10,42},{12,44},{14,46},{16,48}... | collective-permute-start | bytes 1572872 | tf_op jit(solution)/shard_map/ppermute | solution.py:17
  28.8 2.6 collective-permute-start.2
  46.3 6.3 %psum.7 = f32[6,32]{1,0:T(8,128)} all-reduce(f32[6,32]{1,0:T(8,128)S(1)} %fusion.22), channel_id=1, replica_groups=mesh['section'=2,'replica'=32,'tensor'=2] {'tensor'}, use_global_device_ids=true, to_apply=%region_0.1 | all-reduce | flops 192 | bytes 1536 | tf_op jit(solution)/shard_map/psum | solution.py:114
  52.7 2.9 scatter_custom_fusion.1
  55.7 3.1 scatter_custom_fusion
  71.0 11.3 %fusion.120 = (bf16[1,1,480,16,512]{4,3,2,1,0:T(8,128)(2,1)}, bf16[1,1,480,16,512]{4,3,2,1,0:T(8,128)(2,1)}) fusion(bf16[1,2,480,16,512]{4,3,2,1,0:T(8,128)(2,1)} %param.17), kind=kLoop, calls=%fused_computation.222 | loop fusion | bytes 31457280 | tf_op jit(solution)/shard_map/slice | solution.py:135
  82.3 7.9 %gather_fusion.2 = bf16[80,2,16,512]{3,2,1,0:T(8,128)(2,1)} fusion(bf16[2,480,16,512]{3,2,1,0:T(8,128)(2,1)} %bitcast.324, s32[1024]{0:T(1024)S(1)} %get-tuple-element.94), kind=kCustom, calls=%fused_computation.2 | custom fusion | bytes 5243200 | tf_op jit(solution)/shard_map/gather | solution.py:158
  90.2 7.8 %gather_fusion.4 = bf16[80,2,16,512]{3,2,1,0:T(8,128)(2,1)} fusion(bf16[2,480,16,512]{3,2,1,0:T(8,128)(2,1)} %bitcast.325, s32[1024]{0:T(1024)S(1)} %get-tuple-element.92), kind=kCustom, calls=%fused_computation.4 | custom fusion | bytes 5243200 | tf_op jit(solution)/shard_map/gather | solution.py:158
  98.0 7.9 %gather_fusion = bf16[80,2,16,512]{3,2,1,0:T(8,128)(2,1)} fusion(bf16[2,480,16,512]{3,2,1,0:T(8,128)(2,1)} %bitcast.326, s32[1024]{0:T(1024)S(1)} %pad_clamp_fusion.4), kind=kCustom, calls=%fused_computation | custom fusion | bytes 5243200 | tf_op jit(solution)/shard_map/gather | solution.py:158
  106.0 7.8 %gather_fusion.1 = bf16[80,2,16,512]{3,2,1,0:T(8,128)(2,1)} fusion(bf16[2,480,16,512]{3,2,1,0:T(8,128)(2,1)} %bitcast.327, s32[1024]{0:T(1024)S(1)} %get-tuple-element.95), kind=kCustom, calls=%fused_computation.1 | custom fusion | bytes 5243200 | tf_op jit(solution)/shard_map/gather | solution.py:158
  113.8 7.8 %gather_fusion.3 = bf16[80,2,16,512]{3,2,1,0:T(8,128)(2,1)} fusion(bf16[2,480,16,512]{3,2,1,0:T(8,128)(2,1)} %bitcast.328, s32[1024]{0:T(1024)S(1)} %get-tuple-element.93), kind=kCustom, calls=%fused_computation.3 | custom fusion | bytes 5243200 | tf_op jit(solution)/shard_map/gather | solution.py:158
  121.6 10.5 %copy.27 = bf16[7680,512]{0,1:T(8,128)(2,1)} copy(bf16[7680,512]{1,0:T(8,128)(2,1)} %bitcast.330) | data formatting | bytes 15728640 | tf_op jit(solution)/shard_map/reshape;squeeze | solution.py:135
  132.7 8.7 %fusion.129 = (f32[192]{0:T(256)S(1)}, f32[192,7680]{1,0:T(8,128)}) fusion(pred[192,7680]{1,0:T(32,128)(4,1)S(1)} %bitcast.331, bf16[7680,512]{1,0:T(8,128)(2,1)} %bitcast.329, bf16[24,8,4,128]{3,2,1,0:T(4,128)(2,1)S(1)} %bitcast.351), kind=kOutput, calls=%fused_computation.231 | convolution fusion | flops 1514372864 | bytes 15434496 | tf_op jit(solution)/shard_map/dot_general | solution.py:33
  141.4 6.1 %fusion.2 = (bf16[192,7680]{1,0:T(8,128)(2,1)}, f32[192]{0:T(256)S(1)}) fusion(f32[192,7680]{1,0:T(8,128)} %get-tuple-element.77, f32[192]{0:T(256)S(1)} %get-tuple-element.76, pred[6,7680]{1,0:T(8,128)(4,1)S(1)} %fusion.32, pred[192,7680]{1,0:T(32,128)(4,1)S(1)} %bitcast.332), kind=kLoop, calls=%fused_computation.11 | loop fusion | flops 7372608 | bytes 10369536 | tf_op jit(solution)/shard_map/convert_element_type | solution.py:42
  148.3 7.0 %fusion.16 = f32[6,4,8,128]{3,2,1,0:T(8,128)S(1)} fusion(bf16[6,4,8,7680,1]{3,2,4,1,0:T(8,128)(2,1)} %bitcast.349, bf16[4,128,7680,1,1]{2,1,0,4,3:T(8,128)(2,1)} %bitcast.333, f32[4,4]{1,0:T(4,128)S(1)} %fusion.112), kind=kOutput, calls=%fused_computation.33 | convolution fusion | flops 1510121472 | bytes 10911808 | tf_op jit(solution)/shard_map/dot_general | solution.py:43
  163.9 4.7 %fusion.10 = f32[6,8192]{1,0:T(8,128)S(1)} fusion(f32[1,6,16,8192]{3,2,1,0:T(8,128)} %param.19, f32[6,16]{1,0:T(8,128)S(1)} %get-tuple-element.65, f32[6,8192]{1,0:T(8,128)S(1)} %get-tuple-element.48, f32[16,8192]{1,0:T(8,128)} %collective-permute-done.4, f32[16,8192]{1,0:T(8,128)} %collective-permute-done.3, f32[16,8192]{1,0:T(8,128)} %collective-permute-done.2, ...), kind=kLoop, calls=%fused_computation.20 | loop fusion | flops 8601600 | bytes 6882078 | tf_op jit(solution)/shard_map/reduce_sum | solution.py:122
  169.4 46.9 %collective-permute-done.9 = bf16[2,80,16,512]{3,2,0,1:T(8,128)(2,1)S(1)} collective-permute-done((bf16[2,80,16,512]{3,2,0,1:T(8,128)(2,1)S(1)}, bf16[2,80,16,512]{3,2,0,1:T(8,128)(2,1)S(1)}, u32[]{:S(2)}, u32[]{:S(2)}) %collective-permute-start.9) | collective-permute-done | bytes 2621472 | tf_op jit(solution)/shard_map/ppermute | solution.py:17
  216.2 7.0 %collective-permute-start.5 = (bf16[1,6,8192]{2,1,0:T(8,128)(2,1)}, bf16[1,6,8192]{2,1,0:T(8,128)(2,1)S(1)}, u32[]{:S(2)}, u32[]{:S(2)}) collective-permute-start(bf16[1,6,8192]{2,1,0:T(8,128)(2,1)} %fusion.30), channel_id=1, source_target_pairs={{0,64},{64,0},{1,65},{65,1},{2,66},{66,2},{3,67},{67,3},{4,68},{68... | collective-permute-start | bytes 294920 | tf_op jit(solution)/shard_map/ppermute | solution.py:23
  232.8 40.3 %collective-permute-done.6 = bf16[2,80,16,512]{3,2,0,1:T(8,128)(2,1)} collective-permute-done((bf16[2,80,16,512]{3,2,0,1:T(8,128)(2,1)}, bf16[2,80,16,512]{3,2,0,1:T(8,128)(2,1)}, u32[]{:S(2)}, u32[]{:S(2)}) %collective-permute-start.6) | collective-permute-done | bytes 2621472 | tf_op jit(solution)/shard_map/ppermute | solution.py:17
  283.4 2.5 fusion.130
  288.0 2.6 fusion.20
  302.6 3.7 %collective-permute-start.11 = (bf16[1,6,4096]{2,1,0:T(8,128)(2,1)S(1)}, bf16[1,6,4096]{2,1,0:T(8,128)(2,1)S(1)}, u32[]{:S(2)}, u32[]{:S(2)}) collective-permute-start(bf16[1,6,4096]{2,1,0:T(8,128)(2,1)S(1)} %divide_convert_fusion), channel_id=1, source_target_pairs={{0,64},{64,0},{1,65},{65,1},{2,66},{66,2},{3,67},{67,3},{4,68},{68... | collective-permute-start | bytes 147464 | tf_op jit(solution)/shard_map/ppermute | solution.py:23
  306.3 5.8 %multiply_add_fusion = f32[1,6,16,8192]{3,2,1,0:T(8,128)} fusion(f32[1,6,16,8192]{3,2,1,0:T(8,128)} %param.19, f32[6,16]{1,0:T(8,128)S(1)} %copy-done.27, f32[6,8192]{1,0:T(8,128)S(1)} %copy-done.9, f32[16,8192]{1,0:T(8,128)} %collective-permute-done.4, f32[16,8192]{1,0:T(8,128)} %collective-permute-done.3, f32[16,8192]{1,0:T(8,128)} %collective-permute-done.2, ...), kind=kLoop, calls=%fused_computation.21 | loop fusion | flops 7077888 | bytes 9830814 | tf_op jit(solution)/shard_map/add | solution.py:120
  (235 shorter events, 70.2 us)
Async XLA Ops:
  0.6 45.4 %copy-start = (bf16[1,32,8192]{2,1,0:T(8,128)(2,1)S(1)}, bf16[1,32,8192]{2,1,0:T(8,128)(2,1)}, u32[]{:S(2)}) copy-start(bf16[1,32,8192]{2,1,0:T(8,128)(2,1)} %param.22) | copy-start | bytes 1572868
  18.5 27.3 %copy-start.43 = (s32[6,80]{1,0:T(8,128)S(1)}, s32[6,80]{1,0:T(8,128)}, u32[]{:S(2)}) copy-start(s32[6,80]{1,0:T(8,128)} %param.15) | copy-start | bytes 5764
  18.5 27.4 %copy-start.57 = (s32[192]{0:T(256)S(1)}, s32[192]{0:T(256)}, u32[]{:S(2)}) copy-start(s32[192]{0:T(256)} %param.14) | copy-start | bytes 2308
  18.6 27.5 %copy-start.11 = (bf16[1,6,8192]{2,1,0:T(8,128)(2,1)S(1)}, bf16[1,6,8192]{2,1,0:T(8,128)(2,1)}, u32[]{:S(2)}) copy-start(bf16[1,6,8192]{2,1,0:T(8,128)(2,1)} %param.20) | copy-start | bytes 294916
  18.6 50.2 %copy-start.23 = (bf16[1,6,4096]{2,1,0:T(8,128)(2,1)S(1)}, bf16[1,6,4096]{2,1,0:T(8,128)(2,1)}, u32[]{:S(2)}) copy-start(bf16[1,6,4096]{2,1,0:T(8,128)(2,1)} %param.16) | copy-start | bytes 147460
  18.6 50.9 %copy-start.42 = (bf16[1,2,6,512]{3,1,2,0:T(2,128)(2,1)S(1)}, bf16[1,2,6,512]{3,1,2,0:T(2,128)(2,1)}, u32[]{:S(2)}) copy-start(bf16[1,2,6,512]{3,1,2,0:T(2,128)(2,1)} %param.18) | copy-start | bytes 36868
  18.6 52.3 %copy-start.12 = (f32[1,16,8192]{2,1,0:T(8,128)S(1)}, f32[1,16,8192]{2,1,0:T(8,128)}, u32[]{:S(2)}) copy-start(f32[1,16,8192]{2,1,0:T(8,128)} %param.23) | copy-start | bytes 1572868
  21.9 138.6 %collective-permute-start = (f32[16,8192]{1,0:T(8,128)}, f32[16,8192]{1,0:T(8,128)}, u32[]{:S(2)}, u32[]{:S(2)}) collective-permute-start(f32[16,8192]{1,0:T(8,128)} %get-tuple-element.32), channel_id=1, source_target_pairs={{0,32},{2,34},{4,36},{6,38},{8,40},{10,42},{12,44},{14,46},{16,48}... | collective-permute-start | bytes 1572872 | tf_op jit(solution)/shard_map/ppermute | solution.py:17
  26.3 135.1 %collective-permute-start.4 = (f32[16,8192]{1,0:T(8,128)}, f32[16,8192]{1,0:T(8,128)}, u32[]{:S(2)}, u32[]{:S(2)}) collective-permute-start(f32[16,8192]{1,0:T(8,128)} %get-tuple-element.33), channel_id=1, source_target_pairs={{0,2},{2,0},{4,6},{6,4},{8,10},{10,8},{12,14},{14,12},{16,18},{18,... | collective-permute-start | bytes 1572872 | tf_op jit(solution)/shard_map/ppermute | solution.py:17
  27.5 134.6 %collective-permute-start.3 = (f32[16,8192]{1,0:T(8,128)}, f32[16,8192]{1,0:T(8,128)}, u32[]{:S(2)}, u32[]{:S(2)}) collective-permute-start(f32[16,8192]{1,0:T(8,128)} %get-tuple-element.34), channel_id=1, source_target_pairs={{0,4},{2,6},{4,0},{6,2},{8,12},{10,14},{12,8},{14,10},{16,20},{18,... | collective-permute-start | bytes 1572872 | tf_op jit(solution)/shard_map/ppermute | solution.py:17
  28.8 133.6 %collective-permute-start.2 = (f32[16,8192]{1,0:T(8,128)}, f32[16,8192]{1,0:T(8,128)}, u32[]{:S(2)}, u32[]{:S(2)}) collective-permute-start(f32[16,8192]{1,0:T(8,128)} %get-tuple-element.35), channel_id=1, source_target_pairs={{0,8},{2,10},{4,12},{6,14},{8,0},{10,2},{12,4},{14,6},{16,24},{18,... | collective-permute-start | bytes 1572872 | tf_op jit(solution)/shard_map/ppermute | solution.py:17
  31.5 131.2 %collective-permute-start.1 = (f32[16,8192]{1,0:T(8,128)}, f32[16,8192]{1,0:T(8,128)}, u32[]{:S(2)}, u32[]{:S(2)}) collective-permute-start(f32[16,8192]{1,0:T(8,128)} %get-tuple-element.36), channel_id=1, source_target_pairs={{0,16},{2,18},{4,20},{6,22},{8,24},{10,26},{12,28},{14,30},{16,0},... | collective-permute-start | bytes 1572872 | tf_op jit(solution)/shard_map/ppermute | solution.py:17
  32.2 50.1 %copy-start.58 = (bf16[4,4]{1,0:T(4,128)(2,1)}, bf16[4,4]{1,0:T(4,128)(2,1)S(1)}, u32[]{:S(2)}) copy-start(bf16[4,4]{1,0:T(4,128)(2,1)S(1)} %fusion.87) | copy-start | bytes 100
  71.0 92.9 %copy-start.5 = (f32[16,8192]{1,0:T(8,128)}, f32[16,8192]{1,0:T(8,128)S(1)}, u32[]{:S(2)}) copy-start(f32[16,8192]{1,0:T(8,128)S(1)} %exponential_bitcast_fusion) | copy-start | bytes 1572868
  148.3 12.3 %copy-start.7 = (bf16[80,2,16,512]{3,2,1,0:T(8,128)(2,1)S(1)}, bf16[80,2,16,512]{3,2,1,0:T(8,128)(2,1)}, u32[]{:S(2)}) copy-start(bf16[80,2,16,512]{3,2,1,0:T(8,128)(2,1)} %gather_fusion.3) | copy-start | bytes 7864324
  157.0 11.6 %copy-start.8 = (f32[6,8192]{1,0:T(8,128)}, f32[6,8192]{1,0:T(8,128)S(1)}, u32[]{:S(2)}) copy-start(f32[6,8192]{1,0:T(8,128)S(1)} %get-tuple-element.48) | copy-start | bytes 589828
  160.5 55.7 %collective-permute-start.9 = (bf16[2,80,16,512]{3,2,0,1:T(8,128)(2,1)S(1)}, bf16[2,80,16,512]{3,2,0,1:T(8,128)(2,1)S(1)}, u32[]{:S(2)}, u32[]{:S(2)}) collective-permute-start(bf16[2,80,16,512]{3,2,0,1:T(8,128)(2,1)S(1)} %bitcast.350), channel_id=1, source_target_pairs={{0,4},{2,6},{4,0},{6,2},{8,12},{10,14},{12,8},{14,10},{16,20},{18,... | collective-permute-start | bytes 7864328 | tf_op jit(solution)/shard_map/ppermute | solution.py:17
  161.4 64.8 %collective-permute-start.7 = (bf16[2,80,16,512]{3,2,0,1:T(8,128)(2,1)}, bf16[2,80,16,512]{3,2,0,1:T(8,128)(2,1)}, u32[]{:S(2)}, u32[]{:S(2)}) collective-permute-start(bf16[2,80,16,512]{3,2,0,1:T(8,128)(2,1)} %bitcast.41), channel_id=1, source_target_pairs={{0,16},{2,18},{4,20},{6,22},{8,24},{10,26},{12,28},{14,30},{16,0},... | collective-permute-start | bytes 7864328 | tf_op jit(solution)/shard_map/ppermute | solution.py:17
  162.2 110.9 %collective-permute-start.6 = (bf16[2,80,16,512]{3,2,0,1:T(8,128)(2,1)}, bf16[2,80,16,512]{3,2,0,1:T(8,128)(2,1)}, u32[]{:S(2)}, u32[]{:S(2)}) collective-permute-start(bf16[2,80,16,512]{3,2,0,1:T(8,128)(2,1)} %bitcast.35), channel_id=1, source_target_pairs={{0,32},{2,34},{4,36},{6,38},{8,40},{10,42},{12,44},{14,46},{16,48}... | collective-permute-start | bytes 7864328 | tf_op jit(solution)/shard_map/ppermute | solution.py:17
  162.4 117.6 %collective-permute-start.10 = (bf16[2,80,16,512]{3,2,0,1:T(8,128)(2,1)}, bf16[2,80,16,512]{3,2,0,1:T(8,128)(2,1)}, u32[]{:S(2)}, u32[]{:S(2)}) collective-permute-start(bf16[2,80,16,512]{3,2,0,1:T(8,128)(2,1)} %bitcast.59), channel_id=1, source_target_pairs={{0,2},{2,0},{4,6},{6,4},{8,10},{10,8},{12,14},{14,12},{16,18},{18,... | collective-permute-start | bytes 7864328 | tf_op jit(solution)/shard_map/ppermute | solution.py:17
  162.7 132.6 %collective-permute-start.8 = (bf16[2,80,16,512]{3,2,0,1:T(8,128)(2,1)}, bf16[2,80,16,512]{3,2,0,1:T(8,128)(2,1)}, u32[]{:S(2)}, u32[]{:S(2)}) collective-permute-start(bf16[2,80,16,512]{3,2,0,1:T(8,128)(2,1)} %bitcast.47), channel_id=1, source_target_pairs={{0,8},{2,10},{4,12},{6,14},{8,0},{10,2},{12,4},{14,6},{16,24},{18,... | collective-permute-start | bytes 7864328 | tf_op jit(solution)/shard_map/ppermute | solution.py:17
  216.2 95.8 %collective-permute-start.5 = (bf16[1,6,8192]{2,1,0:T(8,128)(2,1)}, bf16[1,6,8192]{2,1,0:T(8,128)(2,1)S(1)}, u32[]{:S(2)}, u32[]{:S(2)}) collective-permute-start(bf16[1,6,8192]{2,1,0:T(8,128)(2,1)} %fusion.30), channel_id=1, source_target_pairs={{0,64},{64,0},{1,65},{65,1},{2,66},{66,2},{3,67},{67,3},{4,68},{68... | collective-permute-start | bytes 294920 | tf_op jit(solution)/shard_map/ppermute | solution.py:23
  231.2 43.8 %copy-start.45 = (f32[32]{0:T(128)}, f32[32]{0:T(128)S(1)}, u32[]{:S(2)}) copy-start(f32[32]{0:T(128)S(1)} %get-tuple-element.84) | copy-start | bytes 388
  302.6 9.5 %collective-permute-start.11 = (bf16[1,6,4096]{2,1,0:T(8,128)(2,1)S(1)}, bf16[1,6,4096]{2,1,0:T(8,128)(2,1)S(1)}, u32[]{:S(2)}, u32[]{:S(2)}) collective-permute-start(bf16[1,6,4096]{2,1,0:T(8,128)(2,1)S(1)} %divide_convert_fusion), channel_id=1, source_target_pairs={{0,64},{64,0},{1,65},{65,1},{2,66},{66,2},{3,67},{67,3},{4,68},{68... | collective-permute-start | bytes 147464 | tf_op jit(solution)/shard_map/ppermute | solution.py:23
  (47 other events, 210.5 us)
where the time goes:
time: 315 us; the launch traced here: 313 us
  local copies, waits for them, and re-layouts  98.9 us (31%)
  waiting for transfers between devices  87.2 us (28%)
  other arithmetic  42.1 us (13%)
  matrix products  31.3 us (10%)
  between operations  24.2 us (8%)
  starting transfers between devices  23.4 us (7%)
  blocking collectives  6.27 us (2%)
    ppermute x10, waiting for transfers between devices, swapped(): return lax.ppermute(value, axis, pairs)  87.2 us
    gather x5, local copies, waits for them, and re-layouts, per_device(): leaving = pool_here[:, block_table[leave_slots[bit]]]  39.3 us
    dot_general x6, matrix products, cache_partial(): full = jnp.dot(rounded, value_rows, preferred_element_type=jnp.float32)  16 us
    dot_general x6, matrix products, cache_partial(): lax.dot_general(spread, key_rows, (((1,), (1,)), ((), ())), preferred_ele...  14.2 us
    ppermute x10, starting transfers between devices, swapped(): return lax.ppermute(value, axis, pairs)  12.8 us
    slice x1, local copies, waits for them, and re-layouts, per_device(): pool_values = pool_here[1].reshape(page_total * page_size, row_width)  11.3 us
    ppermute x2, starting transfers between devices, from_behind(): return lax.ppermute(value, axis, pairs)  10.7 us
    another operation x1, local copies, waits for them, and re-layouts, per_device(): pool_values = pool_here[1].reshape(page_total * page_size, row_width)  10.5 us
  transfers between devices with their start and end apart: 12, of which 2 were waited for; matrix products, arithmetic and copies ran while one was open for 52% of the time, Pallas kernels for 0%

commit v1 on v0

v1 whole, which is shorter than its diff:
```python
import jax
import jax.numpy as jnp
from jax import lax
from jax.experimental import pallas as pl
from jax.experimental.pallas import tpu as pltpu
from jax.sharding import PartitionSpec as P

HEADS = 64
KVH = 8
HD = 128

SLOTS = 6
BITS = 5
SEND_ORDER = (4, 2, 0, 3, 1)
BLOCK = 256

masked_score = -1e30
f32 = jnp.float32
bf16 = jnp.bfloat16


def swapped(value, axis, bit):
    mask = 2**bit
    pairs = [(source, source ^ mask) for source in range(lax.axis_size(axis))]
    return lax.ppermute(value, axis, pairs)


def across(value, bit):
    sections, replicas = lax.axis_size("section"), lax.axis_size("replica")
    mask = 0 if bit is None else 2**bit
    pairs = [
        (s * replicas + r, ((s + 1) % sections) * replicas + (r ^ mask))
        for s in range(sections)
        for r in range(replicas)
    ]
    return lax.ppermute(value, ("section", "replica"), pairs)


def whole(space):
    return pl.BlockSpec(memory_space=space)


def write_plan(own, src, lens, plan):
    first = own * SLOTS
    for entry in range(24):
        plan[entry] = 0
    for bit in range(BITS):
        partner = jnp.bitwise_xor(own, 1 << bit) * SLOTS
        leave = jnp.int32(0)
        served = jnp.int32(1)
        ask = jnp.int32(0)
        for j in range(SLOTS):
            there = src[partner + j] - first
            gives = (there >= 0) & (there < SLOTS)
            leave = jnp.where(gives, there, leave)
            served = jnp.where(gives, lens[partner + j], served)
            here = src[first + j] - partner
            ask = jnp.where((here >= 0) & (here < SLOTS), j, ask)
        plan[bit] = leave
        plan[8 + bit] = ask
        plan[16 + bit] = served
    kept_old = jnp.int32(0)
    kept_new = jnp.int32(0)
    for j in range(SLOTS):
        here = src[first + j] - first
        stays = (here >= 0) & (here < SLOTS)
        kept_old = jnp.where(stays, here, kept_old)
        kept_new = jnp.where(stays, j, kept_new)
    plan[5] = kept_old
    plan[13] = kept_new
    plan[21] = lens[first + kept_new]


def pack_kernel(
    src, lens, state, queries, fresh, conv, x_proj,
    plan, gains, kept, p0, p1, p2, p3, p4,
    state_buf, q_buf, fresh_buf, conv_buf, x_buf, head_rows, own_rows, sems,
):
    packs = (p0, p1, p2, p3, p4)
    width = state.shape[-1]
    small = [
        pltpu.make_async_copy(queries, q_buf, sems.at[5]),
        pltpu.make_async_copy(fresh, fresh_buf, sems.at[6]),
        pltpu.make_async_copy(conv, conv_buf, sems.at[7]),
        pltpu.make_async_copy(x_proj, x_buf, sems.at[8]),
    ]
    write_plan(lax.axis_index("replica"), src, lens, plan)
    copies = {}
    for bit in SEND_ORDER:
        copies[bit] = pltpu.make_async_copy(state.at[plan[bit]], state_buf.at[bit], sems.at[bit])
        copies[bit].start()
    for copy in small:
        copy.start()
    for copy in small:
        copy.wait()
    gains[...] = lax.dot_general(
        x_buf[...], conv_buf[...], (((1,), (1,)), ((), ())), preferred_element_type=f32
    )
    own_rows[...] = jnp.zeros_like(own_rows)
    heads = head_rows.shape[1]
    keys = fresh_buf.shape[-1] // HD
    for h in range(heads):
        column = q_buf[:, h * HD : (h + 1) * HD].astype(f32)
        for slot in range(SLOTS):
            head_rows[slot, h : h + 1, :] = column[slot : slot + 1]

    def heads_of(slot):
        pair = fresh_buf[slot].astype(f32)
        for k in range(keys):
            own_rows[k : k + 1, :] = pair[0:1, k * HD : (k + 1) * HD]
            own_rows[keys + k : keys + k + 1, :] = pair[1:2, k * HD : (k + 1) * HD]
        half = heads // 2
        return jnp.concatenate(
            [head_rows[slot, 0:half], head_rows[slot, half:heads], own_rows[...]], axis=1
        ).astype(bf16)

    for bit in SEND_ORDER:
        packs[bit][:, width:] = heads_of(plan[8 + bit])
        copies[bit].wait()
        packs[bit][:, :width] = state_buf[bit].astype(bf16)
    kept[...] = heads_of(plan[13])


def pack(source_slot, lengths, states, queries, fresh, conv, x_proj):
    n, width = states.shape[1:]
    heads = queries.shape[1] // HD
    half = heads // 2
    packed = jax.ShapeDtypeStruct((half, width + 3 * HD), bf16)
    return pl.pallas_call(
        pack_kernel,
        out_shape=(
            jax.ShapeDtypeStruct((24,), jnp.int32),
            pltpu.VMEM((x_proj.shape[0], SLOTS), f32),
            pltpu.VMEM((half, 3 * HD), bf16),
        )
        + (pltpu.VMEM(packed.shape, bf16),) * BITS,
        in_specs=[whole(pltpu.SMEM)] * 2 + [whole(pl.ANY)] * 5,
        out_specs=(whole(pltpu.SMEM),) + (whole(pltpu.VMEM),) * (2 + BITS),
        scratch_shapes=[
            pltpu.VMEM((BITS, n, width), f32),
            pltpu.VMEM(queries.shape, bf16),
            pltpu.VMEM(fresh.shape, bf16),
            pltpu.VMEM(conv.shape, bf16),
            pltpu.VMEM(x_proj.shape, bf16),
            pltpu.VMEM((SLOTS, heads, HD), f32),
            pltpu.VMEM((half, HD), f32),
            pltpu.SemaphoreType.DMA((9,)),
        ],
        compiler_params=pltpu.CompilerParams(vmem_limit_bytes=24 * 2**20),
        cost_estimate=pl.CostEstimate(
            flops=2 * 32 * 8 * width, transcendentals=0, bytes_accessed=5 * n * width * 6
        ),
    )(source_slot, lengths, states, queries, fresh, conv, x_proj)


def attend_kernel(items, plan, table, pool, *refs):
    extras, outs = refs[: len(items)], refs[len(items) :]
    page = pool.shape[2]
    pages = table.shape[1]
    tokens = page * pages
    per_block = BLOCK // page
    blocks = pages // per_block
    width = pool.shape[3]
    pair_width = 2 * HD
    pairs = width // pair_width
    group = HEADS // KVH
    rows = 2 * group
    scale = HD ** (-0.5)
    row_id = lax.broadcasted_iota(jnp.int32, (rows, pair_width), 0)
    lane_id = lax.broadcasted_iota(jnp.int32, (rows, pair_width), 1)
    own_block = (row_id < group) == (lane_id < HD)
    token_id = lax.broadcasted_iota(jnp.int32, (rows * pairs, BLOCK), 1)
    for item, extra, out in zip(items, extras, outs):
        slot = plan[item]
        length = plan[16 + item]
        base = extra.shape[1] - 3 * HD
        halves = [extra[:, base + i * HD : base + (i + 1) * HD].astype(f32) for i in range(2)]
        own = extra[:, base + 2 * HD :].astype(f32)
        spread = [
            jnp.where(own_block, jnp.concatenate([half, half], axis=1), 0.0).astype(bf16)
            for half in halves
        ]
        places = [table[slot, p] for p in range(pages)]

        def block_of(which, j):
            return jnp.concatenate(
                [pool[which, places[j * per_block + u]] for u in range(per_block)], axis=0
            )

        scores = []
        for j in range(blocks):
            keys = block_of(0, j)
            parts = [
                lax.dot_general(
                    spread[i],
                    keys[:, i * pair_width : (i + 1) * pair_width],
                    (((1,), (1,)), ((), ())),
                    preferred_element_type=f32,
                )
                for i in range(pairs)
            ]
            score = jnp.concatenate(parts, axis=0) * scale
            scores.append(jnp.where(token_id < length - j * BLOCK, score, masked_score))
        top = scores[0]
        for score in scores[1:]:
            top = jnp.maximum(top, score)
        cache_peak = jnp.max(top, axis=1, keepdims=True)
        weights = [jnp.exp(score - cache_peak) for score in scores]
        summed = weights[0]
        for weight in weights[1:]:
            summed = summed + weight
        cache_total = jnp.sum(summed, axis=1, keepdims=True)
        full = [None] * pairs
        for j in range(blocks):
            values = block_of(1, j)
            rounded = weights[j].astype(bf16)
            for i in range(pairs):
                part = jnp.dot(
                    rounded[i * rows : (i + 1) * rows],
                    values[:, i * pair_width : (i + 1) * pair_width],
                    preferred_element_type=f32,
                )
                full[i] = part if full[i] is None else full[i] + part
        gathered = jnp.concatenate(
            [
                full[k // 2][(k % 2) * group : (k % 2 + 1) * group, (k % 2) * HD : (k % 2 + 1) * HD]
                for k in range(2 * pairs)
            ],
            axis=0,
        )
        kv_heads = 2 * pairs
        own_keys = jnp.concatenate(
            [jnp.broadcast_to(own[k : k + 1], (group, HD)) for k in range(kv_heads)], axis=0
        )
        own_values = jnp.concatenate(
            [jnp.broadcast_to(own[kv_heads + k : kv_heads + k + 1], (group, HD)) for k in range(kv_heads)],
            axis=0,
        )
        head_rows = jnp.concatenate(halves, axis=0)
        own_score = jnp.sum(head_rows * own_keys, axis=1, keepdims=True) * scale
        joint_peak = jnp.maximum(cache_peak, own_score)
        cache_weight = jnp.exp(cache_peak - joint_peak)
        own_weight = jnp.exp(own_score - joint_peak)
        numerator = cache_weight * gathered + own_weight * own_values
        attended = numerator / (cache_weight * cache_total + own_weight)
        out[...] = attended.astype(bf16)


def attend(items, plan, table, pool, extras):
    heads = pool.shape[-1] // HD * (HEADS // KVH)
    pool = pltpu.with_memory_space_constraint(pool, pltpu.VMEM)
    extras = [pltpu.with_memory_space_constraint(extra, pltpu.VMEM) for extra in extras]

    def kernel(*refs):
        attend_kernel(items, *refs)

    return pl.pallas_call(
        kernel,
        out_shape=(pltpu.VMEM((heads, HD), bf16),) * len(items),
        in_specs=[whole(pltpu.SMEM)] * 2 + [whole(pltpu.VMEM)] * (1 + len(items)),
        out_specs=(whole(pltpu.VMEM),) * len(items),
        compiler_params=pltpu.CompilerParams(vmem_limit_bytes=16 * 2**20),
        cost_estimate=pl.CostEstimate(
            flops=len(items) * 4 * 1280 * 32 * 512,
            transcendentals=len(items) * 1280 * 32,
            bytes_accessed=len(items) * 2 * 80 * 16 * 1024,
        ),
    )(plan, table, pool, *extras)


def update_kernel(
    plan, gains, gains_far, state, conv, dt, a_log, bias, skip, r0, r1, r2, r3, r4,
    new_state, mixed,
    state_buf, a_buf, rate, step_rows, drive_rows, mixer_rows, mixed_rows, out_buf, sems,
):
    moved = (r0, r1, r2, r3, r4)
    n, width = a_buf.shape
    states_in = pltpu.make_async_copy(state.at[plan[5]], state_buf, sems.at[6])
    states_in.start()
    rates_in = pltpu.make_async_copy(a_log, a_buf, sems.at[7])
    rates_in.start()
    mixer = conv[...].astype(f32)
    step_in = dt[...].astype(f32) + bias[...]
    step = jnp.maximum(step_in, 0.0) + jnp.log1p(jnp.exp(-jnp.abs(step_in)))
    drive = step * mixer
    mixer_rows[...] = skip[...] * mixer
    for row in range(SLOTS):
        step_rows[row] = step[row : row + 1]
        drive_rows[row] = drive[row : row + 1]
    coupled = gains[...] + gains_far[...]
    lane = lax.broadcasted_iota(jnp.int32, coupled.shape, 1)
    rates_in.wait()
    rate[...] = -jnp.exp(a_buf[...])
    outs = []
    chunk = 512
    for item in SEND_ORDER + (5,):
        slot = plan[8 + item]
        column = jnp.sum(jnp.where(lane == slot, coupled, 0.0), axis=1, keepdims=True)
        input_gain = jnp.broadcast_to(column[0:n], (n, 128))
        read_gain = jnp.broadcast_to(column[n : 2 * n], (n, 128))
        if item == 5:
            states_in.wait()
        target = out_buf.at[item]

        def body(c, _, item=item, slot=slot, input_gain=input_gain, read_gain=read_gain, target=target):
            for u in range(chunk // 128):
                at = pl.ds(pl.multiple_of(c * chunk + u * 128, 128), 128)
                if item == 5:
                    previous = state_buf[:, at]
                else:
                    previous = moved[item][:, at].astype(f32)
                step_row = jnp.broadcast_to(step_rows[slot, :, at], (n, 128))
                drive_row = jnp.broadcast_to(drive_rows[slot, :, at], (n, 128))
                updated = jnp.exp(step_row * rate[:, at]) * previous + drive_row * input_gain
                target[:, at] = updated
                mixed_rows[slot, :, at] = jnp.sum(read_gain * updated, axis=0, keepdims=True)
            return 0

        lax.fori_loop(0, width // chunk, body, 0)
        copy = pltpu.make_async_copy(target, new_state.at[slot], sems.at[item])
        copy.start()
        outs.append(copy)
    for row in range(SLOTS):
        mixer_rows[row : row + 1, :] += mixed_rows[row]
    mixed[...] = mixer_rows[...].astype(bf16)
    for copy in outs:
        copy.wait()


def update(plan, gains, gains_far, states, conv, dt, a_log, bias, skip, moved):
    slots, n, width = states.shape
    moved = [pltpu.with_memory_space_constraint(value, pltpu.VMEM) for value in moved]
    rows = pltpu.VMEM((slots, 1, width), f32)
    return pl.pallas_call(
        update_kernel,
        out_shape=(
            jax.ShapeDtypeStruct(states.shape, f32),
            pltpu.VMEM(conv.shape, bf16),
        ),
        in_specs=[whole(pltpu.SMEM)]
        + [whole(pltpu.VMEM)] * 2
        + [whole(pl.ANY)]
        + [whole(pltpu.VMEM)] * 2
        + [whole(pl.ANY)]
        + [whole(pltpu.VMEM)] * (2 + BITS),
        out_specs=(whole(pl.ANY), whole(pltpu.VMEM)),
        scratch_shapes=[
            pltpu.VMEM((n, width), f32),
            pltpu.VMEM((n, width), f32),
            pltpu.VMEM((n, width), f32),
            rows,
            rows,
            pltpu.VMEM((slots, width), f32),
            rows,
            pltpu.VMEM((slots, n, width), f32),
            pltpu.SemaphoreType.DMA((8,)),
        ],
        compiler_params=pltpu.CompilerParams(vmem_limit_bytes=24 * 2**20),
        cost_estimate=pl.CostEstimate(
            flops=slots * n * width * 8,
            transcendentals=slots * n * width,
            bytes_accessed=slots * n * width * 6 + 2 * n * width * 4,
        ),
    )(plan, gains, gains_far, states, conv, dt, a_log, bias, skip, *moved)


def place_kernel(plan, a0, a1, a2, a3, a4, a5, out, head_rows, rows):
    for item, value in enumerate((a0, a1, a2, a3, a4, a5)):
        head_rows[plan[8 + item]] = value[...].astype(f32)
    for slot in range(SLOTS):
        for h in range(head_rows.shape[1]):
            rows[slot : slot + 1, h * HD : (h + 1) * HD] = head_rows[slot, h : h + 1, :]
    out[...] = rows[...].astype(bf16)


def place(plan, parts):
    heads = parts[0].shape[0]
    return pl.pallas_call(
        place_kernel,
        out_shape=jax.ShapeDtypeStruct((SLOTS, heads * HD), bf16),
        in_specs=[whole(pltpu.SMEM)] + [whole(pltpu.VMEM)] * (BITS + 1),
        out_specs=whole(pltpu.VMEM),
        scratch_shapes=[pltpu.VMEM((SLOTS, heads, HD), f32), pltpu.VMEM((SLOTS, heads * HD), f32)],
    )(plan, *parts)


def per_device(
    source_slot,
    lengths,
    block_table,
    queries,
    kv_pool,
    new_kv,
    ssm_state,
    conv_out,
    dt_raw,
    x_proj,
    a_log,
    dt_bias,
    skip_gain,
):
    fresh = jnp.transpose(new_kv[0], (1, 0, 2))
    plan, gains, kept, *packs = pack(
        source_slot, lengths, ssm_state[0], queries[0], fresh, conv_out[0], x_proj[0]
    )
    moved = [None] * BITS
    for bit in SEND_ORDER:
        moved[bit] = swapped(packs[bit], "replica", bit)
    gains_far = swapped(gains, "tensor", 0)
    items = SEND_ORDER + (5,)
    extras = [moved[bit] for bit in SEND_ORDER] + [kept]
    attended = attend(items, plan, block_table, kv_pool[0], extras)
    back = [None] * (BITS + 1)
    for item, value in zip(items, attended):
        back[item] = across(value, item if item < BITS else None)
    new_state, mixed = update(
        plan, gains, gains_far, ssm_state[0], conv_out[0], dt_raw[0], a_log[0], dt_bias, skip_gain, moved
    )
    handed_mamba = across(mixed, None)
    handed_attention = place(plan, back)
    return handed_mamba[None], handed_attention[None], new_state[None]


def solution(mesh):
    in_specs = (
        P(),
        P(),
        P("replica", None),
        P("section", "replica", "tensor"),
        P("section", None, "replica", None, "tensor"),
        P("section", None, "replica", "tensor"),
        P("section", "replica", None, "tensor"),
        P("section", "replica", "tensor"),
        P("section", "replica", "tensor"),
        P("section", None, "tensor"),
        P("section", None, "tensor"),
        P("section", "tensor"),
        P("section", "tensor"),
    )
    out_specs = (
        P("section", "replica", "tensor"),
        P("section", "replica", "tensor"),
        P("section", "replica", None, "tensor"),
    )
    return jax.shard_map(
        per_device, mesh=mesh, in_specs=in_specs, out_specs=out_specs, check_vma=False
    )
```

time: 315 us -> 63.9 us (0.20)
  local copies, waits for them, and re-layouts: 98.9 us -> 15 us
  waiting for transfers between devices: 87.2 us -> 15.5 us
  other arithmetic: 42.1 us -> 0 us
  matrix products: 31.3 us -> 0 us
  between operations: 24.2 us -> 0.78 us
  Pallas kernels: 0 us -> 13.7 us
  blocking collectives: 6.27 us -> 0 us
  starting transfers between devices: 23.4 us -> 18.6 us
    ppermute x10 -> x6, waiting for transfers between devices: 87.2 us -> 10.7 us  [swapped(): return lax.ppermute(value, axis, pairs)]
    gather x5 -> x0, local copies, waits for them, and re-layouts: 39.3 us -> none  [per_device(): leaving = pool_here[:, block_table[leave_slots[bit]]]]
    dot_general x14 -> x0, matrix products: 31.3 us -> none  [the longest x6 16 us: cache_partial(): full = jnp.dot(rounded, value_rows, preferred_element_type=jnp.float32)]
    slice x7 -> x0, local copies, waits for them, and re-layouts: 20.2 us -> none  [the longest x1 11.3 us: per_device(): pool_values = pool_here[1].reshape(page_total * page_size, row_width)]
    another operation x8 -> x0, local copies, waits for them, and re-layouts: 17.9 us -> none  [the longest x1 10.5 us: per_device(): pool_values = pool_here[1].reshape(page_total * page_size, row_width)]
    pallas_call x0 -> x4, Pallas kernels: none -> 13.7 us  [the longest x1 5.07 us: update(): pl.pallas_call(update_kernel, out_shape=(jax.ShapeDtypeStruct(states.shap...]
    unnamed x121 -> x45, local copies, waits for them, and re-layouts: 1.56 us -> 15 us
    convert_element_type x6 -> x0, other arithmetic: 8.31 us -> none  [the longest x1 6.13 us: cache_partial(): weights.astype(jnp.bfloat16)]
  transfers between devices with their start and end apart: 12 -> 13, of which waited for: 2 -> 6; matrix products, arithmetic and copies ran while one was open for 52% -> 0% of each run, Pallas kernels for 0% -> 10%
where the time goes in v1:
time: 63.9 us; the launch traced here: 63.5 us
  starting transfers between devices  18.6 us (29%)
  waiting for transfers between devices  15.5 us (24%)
  local copies, waits for them, and re-layouts  15 us (23%)
  Pallas kernels  13.7 us (21%)
  between operations  0.78 us (1%)
    unnamed x45, local copies, waits for them, and re-layouts  15 us
    ppermute x6, starting transfers between devices, swapped(): return lax.ppermute(value, axis, pairs)  12.8 us
    ppermute x6, waiting for transfers between devices, swapped(): return lax.ppermute(value, axis, pairs)  10.7 us
    ppermute x7, starting transfers between devices, across(): return lax.ppermute(value, ('section', 'replica'), pairs)  5.74 us
    pallas_call x1, Pallas kernels, update(): pl.pallas_call(update_kernel, out_shape=(jax.ShapeDtypeStruct(states.shap...  5.07 us
    pallas_call x1, Pallas kernels, attend(): pl.pallas_call(kernel, out_shape=(pltpu.VMEM((heads, HD), bf16),) * len(i...  4.81 us
    ppermute x7, waiting for transfers between devices, across(): return lax.ppermute(value, ('section', 'replica'), pairs)  4.78 us
    pallas_call x1, Pallas kernels, pack(): pl.pallas_call(pack_kernel, out_shape=(jax.ShapeDtypeStruct((24,), jnp.in...  2.35 us
  transfers between devices with their start and end apart: 13, of which 6 were waited for; matrix products, arithmetic and copies ran while one was open for 0% of the time, Pallas kernels for 10%

profile of v1, /device:TPU:1, one launch (start us, length us, event | category | flops | bytes accessed | tf_op | source)
XLA Modules:
  0.0 63.5 jit_solution(15010730233485833033)
XLA Ops:
  0.6 1.9 %copy-done.1 = f32[1,6,16,8192]{3,2,1,0:T(8,128)S(1)} copy-done((f32[1,6,16,8192]{3,2,1,0:T(8,128)S(1)}, f32[1,6,16,8192]{3,2,1,0:T(8,128)}, u32[]{:S(2)}) %copy-start.1) | copy-done | bytes 3145752
  2.5 1.0 %copy-done.3 = bf16[1,32,8192]{2,1,0:T(8,128)(2,1)S(1)} copy-done((bf16[1,32,8192]{2,1,0:T(8,128)(2,1)S(1)}, bf16[1,32,8192]{2,1,0:T(8,128)(2,1)}, u32[]{:S(2)}) %copy-start.3) | copy-done | bytes 524312
  3.6 0.9 %copy-done.5 = bf16[1,6,8192]{2,1,0:T(8,128)(2,1)S(1)} copy-done((bf16[1,6,8192]{2,1,0:T(8,128)(2,1)S(1)}, bf16[1,6,8192]{2,1,0:T(8,128)(2,1)}, u32[]{:S(2)}) %copy-start.5) | copy-done | bytes 98328
  4.5 0.8 %copy-done.8 = bf16[1,6,4096]{2,1,0:T(8,128)(2,1)S(1)} copy-done((bf16[1,6,4096]{2,1,0:T(8,128)(2,1)S(1)}, bf16[1,6,4096]{2,1,0:T(8,128)(2,1)}, u32[]{:S(2)}) %copy-start.8) | copy-done | bytes 49176
  5.3 0.7 %copy-done.11 = bf16[1,2,6,512]{3,1,2,0:T(2,128)(2,1)S(1)} copy-done((bf16[1,2,6,512]{3,1,2,0:T(2,128)(2,1)S(1)}, bf16[1,2,6,512]{3,1,2,0:T(2,128)(2,1)}, u32[]{:S(2)}) %copy-start.11) | copy-done | bytes 12312
  7.4 2.3 %shard_map.148 = (s32[24]{0:T(128)S(1)}, f32[32,6]{1,0:T(8,128)S(1)}, bf16[16,384]{1,0:T(8,128)(2,1)S(1)}, bf16[16,8576]{1,0:T(8,128)(2,1)S(1)}, bf16[16,8576]{1...) custom-call(s32[192]{0:T(256)S(1)} %copy-done.14, ...), custom_call_target="tpu_custom_call" | custom-call | flops 4194304 | bytes 3932160 | tf_op jit(solution)/shard_map/pallas_call | solution.py:129
  9.8 3.7 %collective-permute-start = (f32[32,6]{1,0:T(8,128)S(1)}, f32[32,6]{1,0:T(8,128)S(1)}, u32[]{:S(2)}, u32[]{:S(2)}) collective-permute-start(f32[32,6]{1,0:T(8,128)S(1)} %get-tuple-element.20.gains), channel_id=1, source_target_pairs={{0,1},{1,0},{2,3},{3,2},{4,5},{5,4},{6,7},{7,6},{8,9},{9,8},{10,11... | collective-permute-start | bytes 2312 | tf_op jit(solution)/shard_map/ppermute | solution.py:25
  13.7 1.3 %collective-permute-start.2 = (bf16[16,8576]{1,0:T(8,128)(2,1)S(1)}, bf16[16,8576]{1,0:T(8,128)(2,1)S(1)}, u32[]{:S(2)}, u32[]{:S(2)}) collective-permute-start(bf16[16,8576]{1,0:T(8,128)(2,1)S(1)} %get-tuple-element.22), channel_id=1, source_target_pairs={{0,4},{2,6},{4,0},{6,2},{8,12},{10,14},{12,8},{14,10},{16,20},{18,... | collective-permute-start | bytes 823304 | tf_op jit(solution)/shard_map/ppermute | solution.py:25
  15.0 2.6 %collective-permute-start.3 = (bf16[16,8576]{1,0:T(8,128)(2,1)S(1)}, bf16[16,8576]{1,0:T(8,128)(2,1)S(1)}, u32[]{:S(2)}, u32[]{:S(2)}) collective-permute-start(bf16[16,8576]{1,0:T(8,128)(2,1)S(1)} %get-tuple-element.23), channel_id=1, source_target_pairs={{0,8},{2,10},{4,12},{6,14},{8,0},{10,2},{12,4},{14,6},{16,24},{18,... | collective-permute-start | bytes 823304 | tf_op jit(solution)/shard_map/ppermute | solution.py:25
  17.7 1.6 %collective-permute-start.4 = (bf16[16,8576]{1,0:T(8,128)(2,1)S(1)}, bf16[16,8576]{1,0:T(8,128)(2,1)S(1)}, u32[]{:S(2)}, u32[]{:S(2)}) collective-permute-start(bf16[16,8576]{1,0:T(8,128)(2,1)S(1)} %get-tuple-element.24), channel_id=1, source_target_pairs={{0,16},{2,18},{4,20},{6,22},{8,24},{10,26},{12,28},{14,30},{16,0},... | collective-permute-start | bytes 823304 | tf_op jit(solution)/shard_map/ppermute | solution.py:25
  19.3 3.3 %collective-permute-start.5 = (bf16[16,8576]{1,0:T(8,128)(2,1)S(1)}, bf16[16,8576]{1,0:T(8,128)(2,1)S(1)}, u32[]{:S(2)}, u32[]{:S(2)}) collective-permute-start(bf16[16,8576]{1,0:T(8,128)(2,1)S(1)} %get-tuple-element.25), channel_id=1, source_target_pairs={{0,32},{2,34},{4,36},{6,38},{8,40},{10,42},{12,44},{14,46},{16,48}... | collective-permute-start | bytes 823304 | tf_op jit(solution)/shard_map/ppermute | solution.py:25
  22.6 6.3 %collective-permute-done.3.r2.refs_4_ = bf16[16,8576]{1,0:T(8,128)(2,1)S(1)} collective-permute-done((bf16[16,8576]{1,0:T(8,128)(2,1)S(1)}, bf16[16,8576]{1,0:T(8,128)(2,1)S(1)}, u32[]{:S(2)}, u32[]{:S(2)}) %collective-permute-start.3) | collective-permute-done | bytes 274464 | tf_op jit(solution)/shard_map/ppermute | solution.py:25
  28.9 4.4 %collective-permute-done.5.r4.refs_3_ = bf16[16,8576]{1,0:T(8,128)(2,1)S(1)} collective-permute-done((bf16[16,8576]{1,0:T(8,128)(2,1)S(1)}, bf16[16,8576]{1,0:T(8,128)(2,1)S(1)}, u32[]{:S(2)}, u32[]{:S(2)}) %collective-permute-start.5) | collective-permute-done | bytes 274464 | tf_op jit(solution)/shard_map/ppermute | solution.py:25
  33.3 0.9 %copy-done.7 = bf16[1,6,8192]{2,1,0:T(8,128)(2,1)S(1)} copy-done((bf16[1,6,8192]{2,1,0:T(8,128)(2,1)S(1)}, bf16[1,6,8192]{2,1,0:T(8,128)(2,1)}, u32[]{:S(2)}) %copy-start.7) | copy-done | bytes 98328
  34.2 5.1 %shard_map.149 = (f32[6,16,8192]{2,1,0:T(8,128)}, bf16[6,8192]{1,0:T(8,128)(2,1)S(1)}) custom-call(s32[24]{0:T(128)S(1)} %get-tuple-element.19.plan.refs_0_, f32[32,6]{1,0:T(8,128)S(1)} %get-tuple-element.20.gains, f32[32,6]{1,0:T(8,128)S(1)} %collective-permute-done.gains_far, f32[6,16,8192]{2,1,0:T(8,128)S(1)} %bitcast.15, bf16[6,8192]{1,0:T(8,128)(2,1)S(1)} %bitcast.19, ...), custom_call_target="tpu_custom_call" | custom-call | flops 6291456 | bytes 5767168 | tf_op jit(solution)/shard_map/pallas_call | solution.py:334
  39.3 2.8 %collective-permute-start.6 = (bf16[6,8192]{1,0:T(8,128)(2,1)S(1)}, bf16[6,8192]{1,0:T(8,128)(2,1)S(1)}, u32[]{:S(2)}, u32[]{:S(2)}) collective-permute-start(bf16[6,8192]{1,0:T(8,128)(2,1)S(1)} %get-tuple-element.26), channel_id=1, source_target_pairs={{0,64},{2,66},{4,68},{6,70},{8,72},{10,74},{12,76},{14,78},{16,80}... | collective-permute-start | bytes 294920 | tf_op jit(solution)/shard_map/ppermute | solution.py:36
  42.1 5.5 %copy-done = bf16[1,2,480,16,512]{4,3,2,1,0:T(8,128)(2,1)S(1)} copy-done((bf16[1,2,480,16,512]{4,3,2,1,0:T(8,128)(2,1)S(1)}, bf16[1,2,480,16,512]{4,3,2,1,0:T(8,128)(2,1)}, u32[]{:S(2)}) %copy-start) | copy-done | bytes 15728664
  47.6 4.8 %shard_map.150 = (bf16[32,128]{1,0:T(8,128)(2,1)S(1)}, bf16[32,128]{1,0:T(8,128)(2,1)S(1)}, bf16[32,128]{1,0:T(8,128)(2,1)S(1)}, bf16[32,128]{1,0:T(8,128)(2,1)S...) custom-call(s32[24]{0:T(128)S(1)} %get-tuple-element.19.plan.refs_0_, s32[6,80]{1,0:T(8,128)S(1)} %copy-done.13, ...), custom_call_target="tpu_custom_call" | custom-call | flops 503316480 | bytes 15728640 | tf_op jit(solution)/shard_map/pallas_call | solution.py:257
  52.4 1.1 %collective-permute-start.7 = (bf16[32,128]{1,0:T(8,128)(2,1)S(1)}, bf16[32,128]{1,0:T(8,128)(2,1)S(1)}, u32[]{:S(2)}, u32[]{:S(2)}) collective-permute-start(bf16[32,128]{1,0:T(8,128)(2,1)S(1)} %get-tuple-element.28), channel_id=1, source_target_pairs={{0,66},{2,64},{4,70},{6,68},{8,74},{10,72},{12,78},{14,76},{16,82}... | collective-permute-start | bytes 24584 | tf_op jit(solution)/shard_map/ppermute | solution.py:36
  53.8 1.2 %collective-permute-start.9 = (bf16[32,128]{1,0:T(8,128)(2,1)S(1)}, bf16[32,128]{1,0:T(8,128)(2,1)S(1)}, u32[]{:S(2)}, u32[]{:S(2)}) collective-permute-start(bf16[32,128]{1,0:T(8,128)(2,1)S(1)} %get-tuple-element.30), channel_id=1, source_target_pairs={{0,72},{2,74},{4,76},{6,78},{8,64},{10,66},{12,68},{14,70},{16,88}... | collective-permute-start | bytes 24584 | tf_op jit(solution)/shard_map/ppermute | solution.py:36
  55.6 1.1 %collective-permute-done.8.a1 = bf16[32,128]{1,0:T(8,128)(2,1)S(1)} collective-permute-done((bf16[32,128]{1,0:T(8,128)(2,1)S(1)}, bf16[32,128]{1,0:T(8,128)(2,1)S(1)}, u32[]{:S(2)}, u32[]{:S(2)}) %collective-permute-start.8) | collective-permute-done | bytes 8224 | tf_op jit(solution)/shard_map/ppermute | solution.py:36
  57.1 1.2 %collective-permute-done.9.a2 = bf16[32,128]{1,0:T(8,128)(2,1)S(1)} collective-permute-done((bf16[32,128]{1,0:T(8,128)(2,1)S(1)}, bf16[32,128]{1,0:T(8,128)(2,1)S(1)}, u32[]{:S(2)}, u32[]{:S(2)}) %collective-permute-start.9) | collective-permute-done | bytes 8224 | tf_op jit(solution)/shard_map/ppermute | solution.py:36
  58.4 1.8 %collective-permute-done.11.a4 = bf16[32,128]{1,0:T(8,128)(2,1)S(1)} collective-permute-done((bf16[32,128]{1,0:T(8,128)(2,1)S(1)}, bf16[32,128]{1,0:T(8,128)(2,1)S(1)}, u32[]{:S(2)}, u32[]{:S(2)}) %collective-permute-start.11) | collective-permute-done | bytes 8224 | tf_op jit(solution)/shard_map/ppermute | solution.py:36
  61.3 1.5 %shard_map.151 = bf16[6,4096]{1,0:T(8,128)(2,1)} custom-call(s32[24]{0:T(128)} %copy-done.12, bf16[32,128]{1,0:T(8,128)(2,1)} %copy-done.16, bf16[32,128]{1,0:T(8,128)(2,1)} %copy-done.17, bf16[32,128]{1,0:T(8,128)(2,1)} %copy-done.18, bf16[32,128]{1,0:T(8,128)(2,1)} %copy-done.19, bf16[32,128]{1,0:T(8,128)(2,1)} %copy-done.20, bf16[32,128]{1,0:T(8,128)(2,1)} %copy-done.21), custom_call_target="tpu_custom_call" | custom-call | tf_op jit(solution)/shard_map/pallas_call | solution.py:378
  (51 shorter events, 4.8 us)
Async XLA Ops:
  0.6 1.9 %copy-start.1 = (f32[1,6,16,8192]{3,2,1,0:T(8,128)S(1)}, f32[1,6,16,8192]{3,2,1,0:T(8,128)}, u32[]{:S(2)}) copy-start(f32[1,6,16,8192]{3,2,1,0:T(8,128)} %param.19) | copy-start | bytes 9437188
  7.4 25.9 %copy-start.2 = (f32[1,6,16,8192]{3,2,1,0:T(8,128)S(1)}, f32[1,6,16,8192]{3,2,1,0:T(8,128)}, u32[]{:S(2)}) copy-start(f32[1,6,16,8192]{3,2,1,0:T(8,128)} %param.19) | copy-start | bytes 9437188
  7.4 25.9 %copy-start.4 = (f32[1,16,8192]{2,1,0:T(8,128)S(1)}, f32[1,16,8192]{2,1,0:T(8,128)}, u32[]{:S(2)}) copy-start(f32[1,16,8192]{2,1,0:T(8,128)} %param.23) | copy-start | bytes 1572868
  7.4 25.9 %copy-start.6 = (bf16[1,6,8192]{2,1,0:T(8,128)(2,1)S(1)}, bf16[1,6,8192]{2,1,0:T(8,128)(2,1)}, u32[]{:S(2)}) copy-start(bf16[1,6,8192]{2,1,0:T(8,128)(2,1)} %param.20) | copy-start | bytes 294916
  7.4 25.9 %copy-start.9 = (f32[1,8192]{1,0:T(1,128)S(1)}, f32[1,8192]{1,0:T(1,128)}, u32[]{:S(2)}) copy-start(f32[1,8192]{1,0:T(1,128)} %bias.1) | copy-start | bytes 98308
  7.4 25.9 %copy-start.10 = (f32[1,8192]{1,0:T(1,128)S(1)}, f32[1,8192]{1,0:T(1,128)}, u32[]{:S(2)}) copy-start(f32[1,8192]{1,0:T(1,128)} %skip.1) | copy-start | bytes 98308
  9.8 42.6 %copy-start.12 = (s32[24]{0:T(128)}, s32[24]{0:T(128)S(1)}, u32[]{:S(2)}) copy-start(s32[24]{0:T(128)S(1)} %get-tuple-element.19.plan.refs_0_) | copy-start | bytes 292
  9.8 32.3 %copy-start.13 = (s32[6,80]{1,0:T(8,128)S(1)}, s32[6,80]{1,0:T(8,128)}, u32[]{:S(2)}) copy-start(s32[6,80]{1,0:T(8,128)} %refs_1_.1) | copy-start | bytes 5764
  9.8 9.5 %collective-permute-start = (f32[32,6]{1,0:T(8,128)S(1)}, f32[32,6]{1,0:T(8,128)S(1)}, u32[]{:S(2)}, u32[]{:S(2)}) collective-permute-start(f32[32,6]{1,0:T(8,128)S(1)} %get-tuple-element.20.gains), channel_id=1, source_target_pairs={{0,1},{1,0},{2,3},{3,2},{4,5},{5,4},{6,7},{7,6},{8,9},{9,8},{10,11... | collective-permute-start | bytes 2312 | tf_op jit(solution)/shard_map/ppermute | solution.py:25
  13.4 9.2 %collective-permute-start.1 = (bf16[16,8576]{1,0:T(8,128)(2,1)S(1)}, bf16[16,8576]{1,0:T(8,128)(2,1)S(1)}, u32[]{:S(2)}, u32[]{:S(2)}) collective-permute-start(bf16[16,8576]{1,0:T(8,128)(2,1)S(1)} %get-tuple-element.21), channel_id=1, source_target_pairs={{0,2},{2,0},{4,6},{6,4},{8,10},{10,8},{12,14},{14,12},{16,18},{18,... | collective-permute-start | bytes 823304 | tf_op jit(solution)/shard_map/ppermute | solution.py:25
  13.7 8.9 %collective-permute-start.2 = (bf16[16,8576]{1,0:T(8,128)(2,1)S(1)}, bf16[16,8576]{1,0:T(8,128)(2,1)S(1)}, u32[]{:S(2)}, u32[]{:S(2)}) collective-permute-start(bf16[16,8576]{1,0:T(8,128)(2,1)S(1)} %get-tuple-element.22), channel_id=1, source_target_pairs={{0,4},{2,6},{4,0},{6,2},{8,12},{10,14},{12,8},{14,10},{16,20},{18,... | collective-permute-start | bytes 823304 | tf_op jit(solution)/shard_map/ppermute | solution.py:25
  15.0 13.9 %collective-permute-start.3 = (bf16[16,8576]{1,0:T(8,128)(2,1)S(1)}, bf16[16,8576]{1,0:T(8,128)(2,1)S(1)}, u32[]{:S(2)}, u32[]{:S(2)}) collective-permute-start(bf16[16,8576]{1,0:T(8,128)(2,1)S(1)} %get-tuple-element.23), channel_id=1, source_target_pairs={{0,8},{2,10},{4,12},{6,14},{8,0},{10,2},{12,4},{14,6},{16,24},{18,... | collective-permute-start | bytes 823304 | tf_op jit(solution)/shard_map/ppermute | solution.py:25
  17.7 11.2 %collective-permute-start.4 = (bf16[16,8576]{1,0:T(8,128)(2,1)S(1)}, bf16[16,8576]{1,0:T(8,128)(2,1)S(1)}, u32[]{:S(2)}, u32[]{:S(2)}) collective-permute-start(bf16[16,8576]{1,0:T(8,128)(2,1)S(1)} %get-tuple-element.24), channel_id=1, source_target_pairs={{0,16},{2,18},{4,20},{6,22},{8,24},{10,26},{12,28},{14,30},{16,0},... | collective-permute-start | bytes 823304 | tf_op jit(solution)/shard_map/ppermute | solution.py:25
  19.3 14.0 %collective-permute-start.5 = (bf16[16,8576]{1,0:T(8,128)(2,1)S(1)}, bf16[16,8576]{1,0:T(8,128)(2,1)S(1)}, u32[]{:S(2)}, u32[]{:S(2)}) collective-permute-start(bf16[16,8576]{1,0:T(8,128)(2,1)S(1)} %get-tuple-element.25), channel_id=1, source_target_pairs={{0,32},{2,34},{4,36},{6,38},{8,40},{10,42},{12,44},{14,46},{16,48}... | collective-permute-start | bytes 823304 | tf_op jit(solution)/shard_map/ppermute | solution.py:25
  39.3 23.6 %collective-permute-start.6 = (bf16[6,8192]{1,0:T(8,128)(2,1)S(1)}, bf16[6,8192]{1,0:T(8,128)(2,1)S(1)}, u32[]{:S(2)}, u32[]{:S(2)}) collective-permute-start(bf16[6,8192]{1,0:T(8,128)(2,1)S(1)} %get-tuple-element.26), channel_id=1, source_target_pairs={{0,64},{2,66},{4,68},{6,70},{8,72},{10,74},{12,76},{14,78},{16,80}... | collective-permute-start | bytes 294920 | tf_op jit(solution)/shard_map/ppermute | solution.py:36
  42.1 5.5 %copy-start = (bf16[1,2,480,16,512]{4,3,2,1,0:T(8,128)(2,1)S(1)}, bf16[1,2,480,16,512]{4,3,2,1,0:T(8,128)(2,1)}, u32[]{:S(2)}) copy-start(bf16[1,2,480,16,512]{4,3,2,1,0:T(8,128)(2,1)} %param.17) | copy-start | bytes 47185924
  52.4 3.2 %collective-permute-start.7 = (bf16[32,128]{1,0:T(8,128)(2,1)S(1)}, bf16[32,128]{1,0:T(8,128)(2,1)S(1)}, u32[]{:S(2)}, u32[]{:S(2)}) collective-permute-start(bf16[32,128]{1,0:T(8,128)(2,1)S(1)} %get-tuple-element.28), channel_id=1, source_target_pairs={{0,66},{2,64},{4,70},{6,68},{8,74},{10,72},{12,78},{14,76},{16,82}... | collective-permute-start | bytes 24584 | tf_op jit(solution)/shard_map/ppermute | solution.py:36
  53.5 3.2 %collective-permute-start.8 = (bf16[32,128]{1,0:T(8,128)(2,1)S(1)}, bf16[32,128]{1,0:T(8,128)(2,1)S(1)}, u32[]{:S(2)}, u32[]{:S(2)}) collective-permute-start(bf16[32,128]{1,0:T(8,128)(2,1)S(1)} %get-tuple-element.29), channel_id=1, source_target_pairs={{0,68},{2,70},{4,64},{6,66},{8,76},{10,78},{12,72},{14,74},{16,84}... | collective-permute-start | bytes 24584 | tf_op jit(solution)/shard_map/ppermute | solution.py:36
  53.8 4.6 %collective-permute-start.9 = (bf16[32,128]{1,0:T(8,128)(2,1)S(1)}, bf16[32,128]{1,0:T(8,128)(2,1)S(1)}, u32[]{:S(2)}, u32[]{:S(2)}) collective-permute-start(bf16[32,128]{1,0:T(8,128)(2,1)S(1)} %get-tuple-element.30), channel_id=1, source_target_pairs={{0,72},{2,74},{4,76},{6,78},{8,64},{10,66},{12,68},{14,70},{16,88}... | collective-permute-start | bytes 24584 | tf_op jit(solution)/shard_map/ppermute | solution.py:36
  55.0 3.4 %collective-permute-start.10 = (bf16[32,128]{1,0:T(8,128)(2,1)S(1)}, bf16[32,128]{1,0:T(8,128)(2,1)S(1)}, u32[]{:S(2)}, u32[]{:S(2)}) collective-permute-start(bf16[32,128]{1,0:T(8,128)(2,1)S(1)} %get-tuple-element.31), channel_id=1, source_target_pairs={{0,80},{2,82},{4,84},{6,86},{8,88},{10,90},{12,92},{14,94},{16,64}... | collective-permute-start | bytes 24584 | tf_op jit(solution)/shard_map/ppermute | solution.py:36
  55.6 4.6 %copy-start.16 = (bf16[32,128]{1,0:T(8,128)(2,1)}, bf16[32,128]{1,0:T(8,128)(2,1)S(1)}, u32[]{:S(2)}) copy-start(bf16[32,128]{1,0:T(8,128)(2,1)S(1)} %collective-permute-done.7.a0) | copy-start | bytes 24580
  55.6 4.6 %collective-permute-start.11 = (bf16[32,128]{1,0:T(8,128)(2,1)S(1)}, bf16[32,128]{1,0:T(8,128)(2,1)S(1)}, u32[]{:S(2)}, u32[]{:S(2)}) collective-permute-start(bf16[32,128]{1,0:T(8,128)(2,1)S(1)} %get-tuple-element.32), channel_id=1, source_target_pairs={{0,96},{2,98},{4,100},{6,102},{8,104},{10,106},{12,108},{14,110},{... | collective-permute-start | bytes 24584 | tf_op jit(solution)/shard_map/ppermute | solution.py:36
  56.7 3.4 %copy-start.17 = (bf16[32,128]{1,0:T(8,128)(2,1)}, bf16[32,128]{1,0:T(8,128)(2,1)S(1)}, u32[]{:S(2)}) copy-start(bf16[32,128]{1,0:T(8,128)(2,1)S(1)} %collective-permute-done.8.a1) | copy-start | bytes 24580
  56.7 3.4 %collective-permute-start.12 = (bf16[32,128]{1,0:T(8,128)(2,1)S(1)}, bf16[32,128]{1,0:T(8,128)(2,1)S(1)}, u32[]{:S(2)}, u32[]{:S(2)}) collective-permute-start(bf16[32,128]{1,0:T(8,128)(2,1)S(1)} %get-tuple-element.33), channel_id=1, source_target_pairs={{0,64},{2,66},{4,68},{6,70},{8,72},{10,74},{12,76},{14,78},{16,80}... | collective-permute-start | bytes 24584 | tf_op jit(solution)/shard_map/ppermute | solution.py:36
  (11 other events, 10.6 us)

commit v2 on v1

v2 whole, which is shorter than its diff:
```python
import jax
import jax.numpy as jnp
from jax import lax
from jax.experimental import pallas as pl
from jax.experimental.pallas import tpu as pltpu
from jax.sharding import PartitionSpec as P

HEADS = 64
KVH = 8
HD = 128

SLOTS = 6
BITS = 5
SEND_ORDER = (4, 2, 0, 3, 1)
FIRST = (5, 4, 2)
LAST = (0, 3, 1)
BLOCK = 256
LOG2E = 1.4426950408889634
PACK_WEIGHT = 10000

masked_score = -1e30
f32 = jnp.float32
bf16 = jnp.bfloat16


def swapped(value, axis, bit):
    mask = 2**bit
    pairs = [(source, source ^ mask) for source in range(lax.axis_size(axis))]
    return lax.ppermute(value, axis, pairs)


def across(value, bit):
    sections, replicas = lax.axis_size("section"), lax.axis_size("replica")
    mask = 2**bit if bit < BITS else 0
    pairs = [
        (s * replicas + r, ((s + 1) % sections) * replicas + (r ^ mask))
        for s in range(sections)
        for r in range(replicas)
    ]
    return lax.ppermute(value, ("section", "replica"), pairs)


def whole(space):
    return pl.BlockSpec(memory_space=space)


def in_hbm(*values):
    return [pltpu.with_memory_space_constraint(value, pltpu.HBM) for value in values]


def in_vmem(*values):
    return [pltpu.with_memory_space_constraint(value, pltpu.VMEM) for value in values]


def write_plan(own, src, lens, plan):
    first = own * SLOTS
    for entry in range(24):
        plan[entry] = 0
    for bit in range(BITS):
        partner = jnp.bitwise_xor(own, 1 << bit) * SLOTS
        leave = jnp.int32(0)
        served = jnp.int32(1)
        ask = jnp.int32(0)
        for j in range(SLOTS):
            there = src[partner + j] - first
            gives = (there >= 0) & (there < SLOTS)
            leave = jnp.where(gives, there, leave)
            served = jnp.where(gives, lens[partner + j], served)
            here = src[first + j] - partner
            ask = jnp.where((here >= 0) & (here < SLOTS), j, ask)
        plan[bit] = leave
        plan[8 + bit] = ask
        plan[16 + bit] = served
    kept_old = jnp.int32(0)
    kept_new = jnp.int32(0)
    for j in range(SLOTS):
        here = src[first + j] - first
        stays = (here >= 0) & (here < SLOTS)
        kept_old = jnp.where(stays, here, kept_old)
        kept_new = jnp.where(stays, j, kept_new)
    plan[5] = kept_old
    plan[13] = kept_new
    plan[21] = lens[first + kept_new]


def load_kernel(
    src_in, lens_in, state, queries, fresh, plan, held, heads_out,
    src, lens, q_buf, fresh_buf, head_rows, own_rows, sems,
):
    copies = [
        pltpu.make_async_copy(source, target, sems.at[i])
        for i, (source, target) in enumerate(
            ((src_in, src), (lens_in, lens), (queries, q_buf), (fresh, fresh_buf), (state, held))
        )
    ]
    for copy in copies:
        copy.start()
    copies[0].wait()
    copies[1].wait()
    write_plan(lax.axis_index("replica"), src, lens, plan)
    copies[2].wait()
    copies[3].wait()
    heads = head_rows.shape[1]
    half = heads // 2
    keys = fresh_buf.shape[-1] // HD
    own_rows[...] = jnp.zeros_like(own_rows)
    for h in range(heads):
        column = q_buf[:, h * HD : (h + 1) * HD].astype(f32)
        for slot in range(SLOTS):
            head_rows[slot, h : h + 1, :] = column[slot : slot + 1]
    for item in range(BITS + 1):
        slot = plan[8 + item]
        pair = fresh_buf[slot].astype(f32)
        for k in range(keys):
            own_rows[k : k + 1, :] = pair[0:1, k * HD : (k + 1) * HD]
            own_rows[keys + k : keys + k + 1, :] = pair[1:2, k * HD : (k + 1) * HD]
        heads_out[item] = jnp.concatenate(
            [head_rows[slot, 0:half], head_rows[slot, half:heads], own_rows[...]], axis=1
        ).astype(bf16)
    copies[4].wait()


def load(source_slot, lengths, states, queries, fresh):
    heads = queries.shape[1] // HD
    half = heads // 2
    return pl.pallas_call(
        load_kernel,
        out_shape=(
            pltpu.SMEM((24,), jnp.int32),
            pltpu.VMEM(states.shape, f32),
            pltpu.VMEM((BITS + 1, half, 3 * HD), bf16),
        ),
        in_specs=[whole(pl.ANY)] * 5,
        out_specs=(whole(pltpu.SMEM), whole(pltpu.VMEM), whole(pltpu.VMEM)),
        scratch_shapes=[
            pltpu.SMEM(source_slot.shape, jnp.int32),
            pltpu.SMEM(lengths.shape, jnp.int32),
            pltpu.VMEM(queries.shape, bf16),
            pltpu.VMEM(fresh.shape, bf16),
            pltpu.VMEM((SLOTS, heads, HD), f32),
            pltpu.VMEM((half, HD), f32),
            pltpu.SemaphoreType.DMA((5,)),
        ],
        compiler_params=pltpu.CompilerParams(vmem_limit_bytes=4 * 2**20),
        cost_estimate=pl.CostEstimate(flops=0, transcendentals=0, bytes_accessed=states.size * 4),
    )(*in_hbm(source_slot, lengths, states, queries, fresh))


def pack_kernel(plan, held, heads, *packs):
    width = held.shape[-1]
    for bit, out in zip(SEND_ORDER, packs):
        out[:, :width] = held[plan[bit]].astype(bf16)
        out[:, width:] = heads[bit]


def pack(plan, held, heads):
    n, width = held.shape[1:]
    packs = pl.pallas_call(
        pack_kernel,
        out_shape=(pltpu.VMEM((n, width + heads.shape[-1]), bf16),) * BITS,
        in_specs=[whole(pltpu.SMEM)] + [whole(pltpu.VMEM)] * 2,
        out_specs=(whole(pltpu.VMEM),) * BITS,
        compiler_params=pltpu.CompilerParams(vmem_limit_bytes=4 * 2**20),
        cost_estimate=pl.CostEstimate(
            flops=PACK_WEIGHT * held.size, transcendentals=0, bytes_accessed=held.size * 6
        ),
    )(plan, *in_vmem(held, heads))
    return dict(zip(SEND_ORDER, packs))


def attend_kernel(items, arrived, plan, table, pool, *refs):
    refs = list(refs)
    extras = [refs.pop(0) for _ in items]
    backs = [refs.pop(0) for _ in arrived]
    later = refs.pop(0)
    outs = [refs.pop(0) for _ in items]
    for entry in range(24):
        later[entry] = plan[entry]
    if arrived:
        placed = refs.pop(0)
        placed[...] = jnp.zeros_like(placed)
        for item, back in zip(arrived, backs):
            placed[plan[8 + item]] = back[...].astype(f32)
    page = pool.shape[2]
    pages = table.shape[1]
    tokens = page * pages
    per_block = BLOCK // page
    blocks = pages // per_block
    width = pool.shape[3]
    pair_width = 2 * HD
    pairs = width // pair_width
    group = HEADS // KVH
    rows = 2 * group
    scale = HD ** (-0.5)
    row_id = lax.broadcasted_iota(jnp.int32, (rows, pair_width), 0)
    lane_id = lax.broadcasted_iota(jnp.int32, (rows, pair_width), 1)
    own_block = (row_id < group) == (lane_id < HD)
    token_id = lax.broadcasted_iota(jnp.int32, (rows * pairs, BLOCK), 1)
    for item, extra, out in zip(items, extras, outs):
        slot = plan[item]
        length = plan[16 + item]
        if item == BITS:
            extra = extra.at[BITS]
        base = extra.shape[1] - 3 * HD
        halves = [extra[:, base + i * HD : base + (i + 1) * HD].astype(f32) for i in range(2)]
        own = extra[:, base + 2 * HD :].astype(f32)
        spread = [
            jnp.where(own_block, jnp.concatenate([half, half], axis=1), 0.0).astype(bf16)
            for half in halves
        ]
        places = [table[slot, p] for p in range(pages)]

        def block_of(which, j):
            return jnp.concatenate(
                [pool[which, places[j * per_block + u]] for u in range(per_block)], axis=0
            )

        scores = []
        for j in range(blocks):
            keys = block_of(0, j)
            parts = [
                lax.dot_general(
                    spread[i],
                    keys[:, i * pair_width : (i + 1) * pair_width],
                    (((1,), (1,)), ((), ())),
                    preferred_element_type=f32,
                )
                for i in range(pairs)
            ]
            score = jnp.concatenate(parts, axis=0) * scale
            scores.append(jnp.where(token_id < length - j * BLOCK, score, masked_score))
        top = scores[0]
        for score in scores[1:]:
            top = jnp.maximum(top, score)
        cache_peak = jnp.max(top, axis=1, keepdims=True)
        weights = [jnp.exp(score - cache_peak) for score in scores]
        summed = weights[0]
        for weight in weights[1:]:
            summed = summed + weight
        cache_total = jnp.sum(summed, axis=1, keepdims=True)
        full = [None] * pairs
        for j in range(blocks):
            values = block_of(1, j)
            rounded = weights[j].astype(bf16)
            for i in range(pairs):
                part = jnp.dot(
                    rounded[i * rows : (i + 1) * rows],
                    values[:, i * pair_width : (i + 1) * pair_width],
                    preferred_element_type=f32,
                )
                full[i] = part if full[i] is None else full[i] + part
        gathered = jnp.concatenate(
            [
                full[k // 2][(k % 2) * group : (k % 2 + 1) * group, (k % 2) * HD : (k % 2 + 1) * HD]
                for k in range(2 * pairs)
            ],
            axis=0,
        )
        kv_heads = 2 * pairs
        own_keys = jnp.concatenate(
            [jnp.broadcast_to(own[k : k + 1], (group, HD)) for k in range(kv_heads)], axis=0
        )
        own_values = jnp.concatenate(
            [jnp.broadcast_to(own[kv_heads + k : kv_heads + k + 1], (group, HD)) for k in range(kv_heads)],
            axis=0,
        )
        head_rows = jnp.concatenate(halves, axis=0)
        own_score = jnp.sum(head_rows * own_keys, axis=1, keepdims=True) * scale
        joint_peak = jnp.maximum(cache_peak, own_score)
        cache_weight = jnp.exp(cache_peak - joint_peak)
        own_weight = jnp.exp(own_score - joint_peak)
        numerator = cache_weight * gathered + own_weight * own_values
        attended = numerator / (cache_weight * cache_total + own_weight)
        out[...] = attended.astype(bf16)


def attend(items, plan, table, pool, extras, arrived, backs):
    heads = pool.shape[-1] // HD * (HEADS // KVH)

    def kernel(*refs):
        attend_kernel(items, arrived, *refs)

    result = pltpu.VMEM((heads, HD), bf16)
    out_shape = (pltpu.SMEM(plan.shape, jnp.int32),) + (result,) * len(items)
    if arrived:
        out_shape += (pltpu.VMEM((SLOTS, heads, HD), f32),)
    return pl.pallas_call(
        kernel,
        out_shape=out_shape,
        in_specs=[whole(pltpu.SMEM)] * 2 + [whole(pltpu.VMEM)] * (1 + len(items) + len(arrived)),
        out_specs=(whole(pltpu.SMEM),) + (whole(pltpu.VMEM),) * (len(out_shape) - 1),
        compiler_params=pltpu.CompilerParams(vmem_limit_bytes=8 * 2**20),
        cost_estimate=pl.CostEstimate(
            flops=len(items) * 4 * 1280 * 32 * 512,
            transcendentals=len(items) * 1280 * 32,
            bytes_accessed=len(items) * 2 * 80 * 16 * 1024,
        ),
    )(plan, table, *in_vmem(pool, *extras, *backs))


def rates_kernel(
    plan, conv, dt, a_log, bias, skip, x_proj, gains, rate, step_rows, drive_rows, direct
):
    gains[...] = lax.dot_general(
        x_proj[...], conv[...], (((1,), (1,)), ((), ())), preferred_element_type=f32
    )
    mixer = conv[...].astype(f32)
    step_in = dt[...].astype(f32) + bias[...]
    step = jnp.maximum(step_in, 0.0) + jnp.log1p(jnp.exp(-jnp.abs(step_in)))
    drive = step * mixer
    direct[...] = skip[...] * mixer
    for row in range(SLOTS):
        step_rows[row] = step[row : row + 1]
        drive_rows[row] = drive[row : row + 1]
    rate[...] = jnp.exp(a_log[...]) * (-LOG2E)


def rates(plan, conv, dt, a_log, bias, skip, x_proj):
    slots, width = conv.shape
    rows = pltpu.VMEM((slots, 1, width), f32)
    return pl.pallas_call(
        rates_kernel,
        out_shape=(pltpu.VMEM((x_proj.shape[0], slots), f32), pltpu.VMEM(a_log.shape, f32), rows, rows, pltpu.VMEM((slots, width), f32)),
        in_specs=[whole(pltpu.SMEM)] + [whole(pltpu.VMEM)] * 6,
        out_specs=(whole(pltpu.VMEM),) * 5,
        compiler_params=pltpu.CompilerParams(vmem_limit_bytes=8 * 2**20),
        cost_estimate=pl.CostEstimate(
            flops=10 * slots * width,
            transcendentals=a_log.size + 2 * slots * width,
            bytes_accessed=a_log.size * 4,
        ),
    )(plan, conv, dt, a_log, bias, skip, x_proj)


def update_kernel(
    plan, gains, gains_far, held, rate, step_rows, drive_rows, direct, r0, r1, r2, r3, r4,
    later, new_state, mixed,
    mixed_rows, mixed_all, out_buf, sems,
):
    moved = (r0, r1, r2, r3, r4)
    n, width = rate.shape
    for entry in range(24):
        later[entry] = plan[entry]
    coupled = gains[...] + gains_far[...]
    lane = lax.broadcasted_iota(jnp.int32, coupled.shape, 1)
    outs = []
    chunk = 1024
    for item in SEND_ORDER + (5,):
        slot = plan[8 + item]
        column = jnp.sum(jnp.where(lane == slot, coupled, 0.0), axis=1, keepdims=True)
        input_gain = jnp.broadcast_to(column[0:n], (n, 128))
        read_gain = jnp.broadcast_to(column[n : 2 * n], (n, 128))
        target = out_buf.at[item]

        def body(c, _, item=item, slot=slot, input_gain=input_gain, read_gain=read_gain, target=target):
            for u in range(chunk // 128):
                at = pl.ds(pl.multiple_of(c * chunk + u * 128, 128), 128)
                if item == 5:
                    previous = held[plan[5], :, at]
                else:
                    previous = moved[item][:, at].astype(f32)
                step_row = jnp.broadcast_to(step_rows[slot, :, at], (n, 128))
                drive_row = jnp.broadcast_to(drive_rows[slot, :, at], (n, 128))
                updated = jnp.exp2(step_row * rate[:, at]) * previous + drive_row * input_gain
                target[:, at] = updated
                mixed_rows[slot, :, at] = jnp.sum(read_gain * updated, axis=0, keepdims=True)
            return 0

        lax.fori_loop(0, width // chunk, body, 0)
        copy = pltpu.make_async_copy(target, new_state.at[slot], sems.at[item])
        copy.start()
        outs.append(copy)
    for row in range(SLOTS):
        mixed_all[row : row + 1, :] = mixed_rows[row]
    mixed[...] = (mixed_all[...] + direct[...]).astype(bf16)
    for copy in outs:
        copy.wait()


def update(plan, gains, gains_far, held, made, moved):
    slots, n, width = held.shape
    return pl.pallas_call(
        update_kernel,
        out_shape=(
            pltpu.SMEM(plan.shape, jnp.int32),
            pltpu.HBM(held.shape, f32),
            pltpu.VMEM((slots, width), bf16),
        ),
        in_specs=[whole(pltpu.SMEM)] + [whole(pltpu.VMEM)] * (7 + BITS),
        out_specs=(whole(pltpu.SMEM), whole(pl.ANY), whole(pltpu.VMEM)),
        scratch_shapes=[
            pltpu.VMEM((slots, 1, width), f32),
            pltpu.VMEM((slots, width), f32),
            pltpu.VMEM((slots, n, width), f32),
            pltpu.SemaphoreType.DMA((slots,)),
        ],
        compiler_params=pltpu.CompilerParams(vmem_limit_bytes=8 * 2**20),
        cost_estimate=pl.CostEstimate(
            flops=held.size * 8, transcendentals=held.size, bytes_accessed=held.size * 6
        ),
    )(plan, *in_vmem(gains, gains_far, held, *made, *moved))


def place_kernel(plan, placed, *refs):
    backs, (mixed, attended, handed, head_rows, rows, rounded, sems) = refs[: len(LAST)], refs[len(LAST) :]
    through = pltpu.make_async_copy(mixed, handed, sems.at[0])
    through.start()
    head_rows[...] = placed[...]
    for item, back in zip(LAST, backs):
        head_rows[plan[8 + item]] = back[...].astype(f32)
    for slot in range(SLOTS):
        for h in range(head_rows.shape[1]):
            rows[slot : slot + 1, h * HD : (h + 1) * HD] = head_rows[slot, h : h + 1, :]
    rounded[...] = rows[...].astype(bf16)
    out = pltpu.make_async_copy(rounded, attended, sems.at[1])
    out.start()
    through.wait()
    out.wait()


def place(plan, placed, backs, mixed):
    heads = placed.shape[1]
    shape = (SLOTS, heads * HD)
    return pl.pallas_call(
        place_kernel,
        out_shape=(pltpu.HBM(shape, bf16), pltpu.HBM(mixed.shape, bf16)),
        in_specs=[whole(pltpu.SMEM)] + [whole(pltpu.VMEM)] * (len(backs) + 2),
        out_specs=(whole(pl.ANY),) * 2,
        scratch_shapes=[
            pltpu.VMEM(placed.shape, f32),
            pltpu.VMEM(shape, f32),
            pltpu.VMEM(shape, bf16),
            pltpu.SemaphoreType.DMA((2,)),
        ],
    )(plan, *in_vmem(placed, *backs, mixed))


def per_device(
    source_slot,
    lengths,
    block_table,
    queries,
    kv_pool,
    new_kv,
    ssm_state,
    conv_out,
    dt_raw,
    x_proj,
    a_log,
    dt_bias,
    skip_gain,
):
    fresh = jnp.transpose(new_kv[0], (1, 0, 2))
    plan, held, heads = load(source_slot, lengths, ssm_state[0], queries[0], fresh)
    packs = pack(plan, held, heads)
    moved = [None] * BITS
    for bit in SEND_ORDER:
        moved[bit] = swapped(packs[bit], "replica", bit)
    gains, *made = rates(
        plan, conv_out[0], dt_raw[0], a_log[0], dt_bias, skip_gain, x_proj[0]
    )
    gains_far = swapped(gains, "tensor", 0)
    extras = moved + [heads]
    pool = kv_pool[0]
    plan, *attended = attend(FIRST, plan, block_table, pool, [extras[i] for i in FIRST], (), ())
    backs = [across(value, item) for item, value in zip(FIRST, attended)]
    plan, new_state, mixed = update(plan, gains, gains_far, held, made, moved)
    handed_mamba = across(mixed, BITS)
    plan, *attended, placed = attend(
        LAST, plan, block_table, pool, [extras[i] for i in LAST], FIRST, backs
    )
    backs = [across(value, item) for item, value in zip(LAST, attended)]
    handed_attention, handed_mamba = place(plan, placed, backs, handed_mamba)
    return handed_mamba[None], handed_attention[None], new_state[None]


def solution(mesh):
    in_specs = (
        P(),
        P(),
        P("replica", None),
        P("section", "replica", "tensor"),
        P("section", None, "replica", None, "tensor"),
        P("section", None, "replica", "tensor"),
        P("section", "replica", None, "tensor"),
        P("section", "replica", "tensor"),
        P("section", "replica", "tensor"),
        P("section", None, "tensor"),
        P("section", None, "tensor"),
        P("section", "tensor"),
        P("section", "tensor"),
    )
    out_specs = (
        P("section", "replica", "tensor"),
        P("section", "replica", "tensor"),
        P("section", "replica", None, "tensor"),
    )
    return jax.shard_map(
        per_device, mesh=mesh, in_specs=in_specs, out_specs=out_specs, check_vma=False
    )
```

time: 63.9 us -> 42 us (0.66)
  local copies, waits for them, and re-layouts: 15 us -> 0.07 us
  waiting for transfers between devices: 15.5 us -> 6.69 us
  starting transfers between devices: 18.6 us -> 21.8 us
  Pallas kernels: 13.7 us -> 12.4 us
    unnamed x45 -> x22, local copies, waits for them, and re-layouts: 15 us -> 0.07 us
    ppermute x6, waiting for transfers between devices: 10.7 us -> 3.37 us  [swapped(): return lax.ppermute(value, axis, pairs)]
    ppermute x7, starting transfers between devices: 5.74 us -> 9.29 us  [across(): return lax.ppermute(value, ('section', 'replica'), pairs)]
    ppermute x7, waiting for transfers between devices: 4.78 us -> 3.32 us  [across(): return lax.ppermute(value, ('section', 'replica'), pairs)]
    pallas_call x4 -> x7, Pallas kernels: 13.7 us -> 12.4 us  [the longest x2 5.57 us: attend(): pl.pallas_call(kernel, out_shape=out_shape, in_specs=[whole(pltpu.SMEM)]...]
  transfers between devices with their start and end apart: 13 -> 13, of which waited for: 6 -> 7; matrix products, arithmetic and copies ran while one was open for 0% -> 0% of each run, Pallas kernels for 10% -> 15%
where the time goes in v2:
time: 42 us; the launch traced here: 41.8 us
  starting transfers between devices  21.8 us (52%)
  Pallas kernels  12.4 us (30%)
  waiting for transfers between devices  6.69 us (16%)
  between operations  0.83 us (2%)
    ppermute x6, starting transfers between devices, swapped(): return lax.ppermute(value, axis, pairs)  12.5 us
    ppermute x7, starting transfers between devices, across(): return lax.ppermute(value, ('section', 'replica'), pairs)  9.29 us
    pallas_call x2, Pallas kernels, attend(): pl.pallas_call(kernel, out_shape=out_shape, in_specs=[whole(pltpu.SMEM)]...  5.57 us
    pallas_call x1, Pallas kernels, update(): pl.pallas_call(update_kernel, out_shape=(pltpu.SMEM(plan.shape, jnp.int32...  3.42 us
    ppermute x6, waiting for transfers between devices, swapped(): return lax.ppermute(value, axis, pairs)  3.37 us
    ppermute x7, waiting for transfers between devices, across(): return lax.ppermute(value, ('section', 'replica'), pairs)  3.32 us
    pallas_call x1, Pallas kernels, load(): pl.pallas_call(load_kernel, out_shape=(pltpu.SMEM((24,), jnp.int32), pltp...  1.99 us
  transfers between devices with their start and end apart: 13, of which 7 were waited for; matrix products, arithmetic and copies ran while one was open for 0% of the time, Pallas kernels for 15%

profile of v2, /device:TPU:1, one launch (start us, length us, event | category | flops | bytes accessed | tf_op | source)
XLA Modules:
  0.0 41.8 jit_solution(14372381056483955913)
XLA Ops:
  0.6 2.0 %shard_map.148 = (s32[24]{0:T(128)S(4)}, f32[6,16,8192]{2,1,0:T(8,128)S(1)}, bf16[6,16,384]{2,1,0:T(8,128)(2,1)S(1)}) custom-call(s32[192]{0:T(256)} %src_in.1, s32[192]{0:T(256)} %lens_in.1, f32[6,16,8192]{2,1,0:T(8,128)} %bitcast.21, bf16[6,4096]{1,0:T(8,128)(2,1)} %bitcast.22, bf16[6,2,512]{2,1,0:T(2,128)(2,1)} %bitcast.23), custom_call_target="tpu_custom_call" | custom-call | bytes 3145728 | tf_op jit(solution)/shard_map/pallas_call | solution.py:126
  2.9 4.5 %collective-permute-start = (bf16[16,8576]{1,0:T(8,128)(2,1)S(1)}, bf16[16,8576]{1,0:T(8,128)(2,1)S(1)}, u32[]{:S(2)}, u32[]{:S(2)}) collective-permute-start(bf16[16,8576]{1,0:T(8,128)(2,1)S(1)} %get-tuple-element.33), channel_id=1, source_target_pairs={{0,32},{2,34},{4,36},{6,38},{8,40},{10,42},{12,44},{14,46},{16,48}... | collective-permute-start | bytes 823304 | tf_op jit(solution)/shard_map/ppermute | solution.py:29
  7.4 2.9 %collective-permute-start.1 = (bf16[16,8576]{1,0:T(8,128)(2,1)S(1)}, bf16[16,8576]{1,0:T(8,128)(2,1)S(1)}, u32[]{:S(2)}, u32[]{:S(2)}) collective-permute-start(bf16[16,8576]{1,0:T(8,128)(2,1)S(1)} %get-tuple-element.34), channel_id=1, source_target_pairs={{0,8},{2,10},{4,12},{6,14},{8,0},{10,2},{12,4},{14,6},{16,24},{18,... | collective-permute-start | bytes 823304 | tf_op jit(solution)/shard_map/ppermute | solution.py:29
  10.3 1.2 %collective-permute-start.3 = (bf16[16,8576]{1,0:T(8,128)(2,1)S(1)}, bf16[16,8576]{1,0:T(8,128)(2,1)S(1)}, u32[]{:S(2)}, u32[]{:S(2)}) collective-permute-start(bf16[16,8576]{1,0:T(8,128)(2,1)S(1)} %get-tuple-element.41), channel_id=1, source_target_pairs={{0,2},{2,0},{4,6},{6,4},{8,10},{10,8},{12,14},{14,12},{16,18},{18,... | collective-permute-start | bytes 823304 | tf_op jit(solution)/shard_map/ppermute | solution.py:29
  11.5 0.4 collective-permute-start.4
  11.9 0.7 %collective-permute-start.5 = (bf16[16,8576]{1,0:T(8,128)(2,1)S(1)}, bf16[16,8576]{1,0:T(8,128)(2,1)S(1)}, u32[]{:S(2)}, u32[]{:S(2)}) collective-permute-start(bf16[16,8576]{1,0:T(8,128)(2,1)S(1)} %get-tuple-element.43), channel_id=1, source_target_pairs={{0,16},{2,18},{4,20},{6,22},{8,24},{10,26},{12,28},{14,30},{16,0},... | collective-permute-start | bytes 823304 | tf_op jit(solution)/shard_map/ppermute | solution.py:29
  12.7 0.6 %shard_map.151 = (f32[32,6]{1,0:T(8,128)S(1)}, f32[16,8192]{1,0:T(8,128)S(1)}, f32[6,1,8192]{2,1,0:T(1,128)S(1)}, f32[6,1,8192]{2,1,0:T(1,128)S(1)}, f32[6,8192]{1,0:T(8,128)S(1)}) custom-call(s32[24]{0:T(128)S(4)} %get-tuple-element.30.plan.refs_0_, bf16[6,8192]{1,0:T(8,128)(2,1)S(1)} %bitcast.19, bf16[6,8192]{1,0:T(8,128)(2,1)S(1)} %bitcast.20, ...), custom_call_target="tpu_custom_call" | custom-call | flops 491520 | bytes 524288 | tf_op jit(solution)/shard_map/pallas_call | solution.py:321
  13.3 0.4 collective-permute-done.refs_4_.r4
  13.7 2.7 %collective-permute-start.2 = (f32[32,6]{1,0:T(8,128)S(1)}, f32[32,6]{1,0:T(8,128)S(1)}, u32[]{:S(2)}, u32[]{:S(2)}) collective-permute-start(f32[32,6]{1,0:T(8,128)S(1)} %get-tuple-element.36.gains), channel_id=1, source_target_pairs={{0,1},{1,0},{2,3},{3,2},{4,5},{5,4},{6,7},{7,6},{8,9},{9,8},{10,11... | collective-permute-start | bytes 2312 | tf_op jit(solution)/shard_map/ppermute | solution.py:29
  16.5 2.8 %shard_map.150 = (s32[24]{0:T(128)S(4)}, bf16[32,128]{1,0:T(8,128)(2,1)S(1)}, bf16[32,128]{1,0:T(8,128)(2,1)S(1)}, bf16[32,128]{1,0:T(8,128)(2,1)S(1)}) custom-call(s32[24]{0:T(128)S(4)} %get-tuple-element.30.plan.refs_0_, s32[6,80]{1,0:T(8,128)S(1)} %copy-done.6, bf16[2,480,16,512]{3,2,1,0:T(8,128)(2,1)S(1)} %bitcast.15, ...), custom_call_target="tpu_custom_call" | custom-call | flops 251658240 | bytes 7864320 | tf_op jit(solution)/shard_map/pallas_call | solution.py:287
  19.4 2.9 %collective-permute-done.4.r1.refs_5_ = bf16[16,8576]{1,0:T(8,128)(2,1)S(1)} collective-permute-done((bf16[16,8576]{1,0:T(8,128)(2,1)S(1)}, bf16[16,8576]{1,0:T(8,128)(2,1)S(1)}, u32[]{:S(2)}, u32[]{:S(2)}) %collective-permute-start.4) | collective-permute-done | bytes 274464 | tf_op jit(solution)/shard_map/ppermute | solution.py:29
  22.3 3.4 %shard_map.152 = (s32[24]{0:T(128)S(4)}, f32[6,16,8192]{2,1,0:T(8,128)}, bf16[6,8192]{1,0:T(8,128)(2,1)S(1)}) custom-call(s32[24]{0:T(128)S(4)} %get-tuple-element.35.plan, f32[32,6]{1,0:T(8,128)S(1)} %get-tuple-element.36.gains, f32[32,6]{1,0:T(8,128)S(1)} %collective-permute-done.2.gains_far, f32[6,16,8192]{2,1,0:T(8,128)S(1)} %get-tuple-element.32.held, ...), custom_call_target="tpu_custom_call" | custom-call | flops 6291456 | bytes 4718592 | tf_op jit(solution)/shard_map/pallas_call | solution.py:382
  25.7 1.9 %collective-permute-start.12 = (bf16[6,8192]{1,0:T(8,128)(2,1)S(1)}, bf16[6,8192]{1,0:T(8,128)(2,1)S(1)}, u32[]{:S(2)}, u32[]{:S(2)}) collective-permute-start(bf16[6,8192]{1,0:T(8,128)(2,1)S(1)} %get-tuple-element.53), channel_id=1, source_target_pairs={{0,64},{2,66},{4,68},{6,70},{8,72},{10,74},{12,76},{14,78},{16,80}... | collective-permute-start | bytes 294920 | tf_op jit(solution)/shard_map/ppermute | solution.py:40
  27.7 0.8 %collective-permute-start.7 = (bf16[32,128]{1,0:T(8,128)(2,1)S(1)}, bf16[32,128]{1,0:T(8,128)(2,1)S(1)}, u32[]{:S(2)}, u32[]{:S(2)}) collective-permute-start(bf16[32,128]{1,0:T(8,128)(2,1)S(1)} %get-tuple-element.46), channel_id=1, source_target_pairs={{0,96},{2,98},{4,100},{6,102},{8,104},{10,106},{12,108},{14,110},{... | collective-permute-start | bytes 24584 | tf_op jit(solution)/shard_map/ppermute | solution.py:40
  28.6 3.2 %collective-permute-start.8 = (bf16[32,128]{1,0:T(8,128)(2,1)S(1)}, bf16[32,128]{1,0:T(8,128)(2,1)S(1)}, u32[]{:S(2)}, u32[]{:S(2)}) collective-permute-start(bf16[32,128]{1,0:T(8,128)(2,1)S(1)} %get-tuple-element.47), channel_id=1, source_target_pairs={{0,72},{2,74},{4,76},{6,78},{8,64},{10,66},{12,68},{14,70},{16,88}... | collective-permute-start | bytes 24584 | tf_op jit(solution)/shard_map/ppermute | solution.py:40
  31.8 0.6 %collective-permute-done.7.refs_7_ = bf16[32,128]{1,0:T(8,128)(2,1)S(1)} collective-permute-done((bf16[32,128]{1,0:T(8,128)(2,1)S(1)}, bf16[32,128]{1,0:T(8,128)(2,1)S(1)}, u32[]{:S(2)}, u32[]{:S(2)}) %collective-permute-start.7) | collective-permute-done | bytes 8224 | tf_op jit(solution)/shard_map/ppermute | solution.py:40
  32.3 0.8 %collective-permute-done.8.refs_8_ = bf16[32,128]{1,0:T(8,128)(2,1)S(1)} collective-permute-done((bf16[32,128]{1,0:T(8,128)(2,1)S(1)}, bf16[32,128]{1,0:T(8,128)(2,1)S(1)}, u32[]{:S(2)}, u32[]{:S(2)}) %collective-permute-start.8) | collective-permute-done | bytes 8224 | tf_op jit(solution)/shard_map/ppermute | solution.py:40
  33.2 2.8 %shard_map.153 = (s32[24]{0:T(128)S(4)}, bf16[32,128]{1,0:T(8,128)(2,1)S(1)}, bf16[32,128]{1,0:T(8,128)(2,1)S(1)}, bf16[32,128]{1,0:T(8,128)(2,1)S(1)}, f32[6,32,128]{2,1,0:T(8,128)S(1)}) custom-call(s32[24]{0:T(128)S(4)} %get-tuple-element.44.refs_0_, s32[6,80]{1,0:T(8,128)S(1)} %copy-done.6, bf16[2,480,16,512]{3,2,1,0:T(8,128)(2,1)S(1)} %bitcast.16, ...), custom_call_target="tpu_custom_call" | custom-call | flops 251658240 | bytes 7864320 | tf_op jit(solution)/shard_map/pallas_call | solution.py:287
  36.0 0.9 %collective-permute-start.9 = (bf16[32,128]{1,0:T(8,128)(2,1)S(1)}, bf16[32,128]{1,0:T(8,128)(2,1)S(1)}, u32[]{:S(2)}, u32[]{:S(2)}) collective-permute-start(bf16[32,128]{1,0:T(8,128)(2,1)S(1)} %get-tuple-element.50), channel_id=1, source_target_pairs={{0,66},{2,64},{4,70},{6,68},{8,74},{10,72},{12,78},{14,76},{16,82}... | collective-permute-start | bytes 24584 | tf_op jit(solution)/shard_map/ppermute | solution.py:40
  36.9 1.1 %collective-permute-start.10 = (bf16[32,128]{1,0:T(8,128)(2,1)S(1)}, bf16[32,128]{1,0:T(8,128)(2,1)S(1)}, u32[]{:S(2)}, u32[]{:S(2)}) collective-permute-start(bf16[32,128]{1,0:T(8,128)(2,1)S(1)} %get-tuple-element.51), channel_id=1, source_target_pairs={{0,80},{2,82},{4,84},{6,86},{8,88},{10,90},{12,92},{14,94},{16,64}... | collective-permute-start | bytes 24584 | tf_op jit(solution)/shard_map/ppermute | solution.py:40
  38.0 1.2 %collective-permute-start.11 = (bf16[32,128]{1,0:T(8,128)(2,1)S(1)}, bf16[32,128]{1,0:T(8,128)(2,1)S(1)}, u32[]{:S(2)}, u32[]{:S(2)}) collective-permute-start(bf16[32,128]{1,0:T(8,128)(2,1)S(1)} %get-tuple-element.52), channel_id=1, source_target_pairs={{0,68},{2,70},{4,64},{6,66},{8,76},{10,78},{12,72},{14,74},{16,84}... | collective-permute-start | bytes 24584 | tf_op jit(solution)/shard_map/ppermute | solution.py:40
  39.2 0.8 %collective-permute-done.10.refs_1_ = bf16[32,128]{1,0:T(8,128)(2,1)S(1)} collective-permute-done((bf16[32,128]{1,0:T(8,128)(2,1)S(1)}, bf16[32,128]{1,0:T(8,128)(2,1)S(1)}, u32[]{:S(2)}, u32[]{:S(2)}) %collective-permute-start.10) | collective-permute-done | bytes 8224 | tf_op jit(solution)/shard_map/ppermute | solution.py:40
  40.0 1.1 %collective-permute-done.11.refs_2_ = bf16[32,128]{1,0:T(8,128)(2,1)S(1)} collective-permute-done((bf16[32,128]{1,0:T(8,128)(2,1)S(1)}, bf16[32,128]{1,0:T(8,128)(2,1)S(1)}, u32[]{:S(2)}, u32[]{:S(2)}) %collective-permute-start.11) | collective-permute-done | bytes 8224 | tf_op jit(solution)/shard_map/ppermute | solution.py:40
  41.1 0.7 %shard_map.154 = (bf16[6,4096]{1,0:T(8,128)(2,1)}, bf16[6,8192]{1,0:T(8,128)(2,1)}) custom-call(s32[24]{0:T(128)S(4)} %get-tuple-element.48.plan, f32[6,32,128]{2,1,0:T(8,128)S(1)} %get-tuple-element.49.placed, bf16[32,128]{1,0:T(8,128)(2,1)S(1)} %collective-permute-done.9.refs_0_, bf16[32,128]{1,0:T(8,128)(2,1)S(1)} %collective-permute-done.10.refs_1_, ...), custom_call_target="tpu_custom_call" | custom-call | tf_op jit(solution)/shard_map/pallas_call | solution.py:424
  (32 shorter events, 0.4 us)
Async XLA Ops:
  2.6 13.8 %slice-start = ((s8[15728640]{0:T(1024)(128)(4,1)}), s8[4194304]{0:T(1024)(128)(4,1)S(1)}, s32[]{:S(2)}) async-start(s8[15728640]{0:T(1024)(128)(4,1)} %bitcast.13), calls=%async_computation | async-start | bytes 8388608
  2.6 10.0 %copy-start = (f32[1,16,8192]{2,1,0:T(8,128)S(1)}, f32[1,16,8192]{2,1,0:T(8,128)}, u32[]{:S(2)}) copy-start(f32[1,16,8192]{2,1,0:T(8,128)} %param.23) | copy-start | bytes 1572868
  2.7 10.0 %copy-start.1 = (bf16[1,32,8192]{2,1,0:T(8,128)(2,1)S(1)}, bf16[1,32,8192]{2,1,0:T(8,128)(2,1)}, u32[]{:S(2)}) copy-start(bf16[1,32,8192]{2,1,0:T(8,128)(2,1)} %param.22) | copy-start | bytes 1572868
  2.7 10.0 %copy-start.2 = (bf16[1,6,8192]{2,1,0:T(8,128)(2,1)S(1)}, bf16[1,6,8192]{2,1,0:T(8,128)(2,1)}, u32[]{:S(2)}) copy-start(bf16[1,6,8192]{2,1,0:T(8,128)(2,1)} %param.20) | copy-start | bytes 294916
  2.7 10.0 %copy-start.3 = (bf16[1,6,8192]{2,1,0:T(8,128)(2,1)S(1)}, bf16[1,6,8192]{2,1,0:T(8,128)(2,1)}, u32[]{:S(2)}) copy-start(bf16[1,6,8192]{2,1,0:T(8,128)(2,1)} %param.21) | copy-start | bytes 294916
  2.7 10.0 %copy-start.4 = (f32[1,8192]{1,0:T(1,128)S(1)}, f32[1,8192]{1,0:T(1,128)}, u32[]{:S(2)}) copy-start(f32[1,8192]{1,0:T(1,128)} %bias.1) | copy-start | bytes 98308
  2.7 10.0 %copy-start.5 = (f32[1,8192]{1,0:T(1,128)S(1)}, f32[1,8192]{1,0:T(1,128)}, u32[]{:S(2)}) copy-start(f32[1,8192]{1,0:T(1,128)} %skip.1) | copy-start | bytes 98308
  2.7 13.7 %slice-start.1 = ((s8[15728640]{0:T(1024)(128)(4,1)}), s8[4194304]{0:T(1024)(128)(4,1)S(1)}, s32[]{:S(2)}) async-start(s8[15728640]{0:T(1024)(128)(4,1)} %bitcast.13), calls=%async_computation.1 | async-start | bytes 8388608
  2.7 13.7 %slice-start.2 = ((s8[15728640]{0:T(1024)(128)(4,1)}), s8[4194304]{0:T(1024)(128)(4,1)S(1)}, s32[]{:S(2)}) async-start(s8[15728640]{0:T(1024)(128)(4,1)} %bitcast.13), calls=%async_computation.2 | async-start | bytes 8388608
  2.7 13.7 %slice-start.3 = ((s8[15728640]{0:T(1024)(128)(4,1)}), s8[3145728]{0:T(1024)(128)(4,1)S(1)}, s32[]{:S(2)}) async-start(s8[15728640]{0:T(1024)(128)(4,1)} %bitcast.13), calls=%async_computation.3 | async-start | bytes 6291456
  2.7 13.7 %copy-start.6 = (s32[6,80]{1,0:T(8,128)S(1)}, s32[6,80]{1,0:T(8,128)}, u32[]{:S(2)}) copy-start(s32[6,80]{1,0:T(8,128)} %refs_1_.3) | copy-start | bytes 5764
  2.9 10.8 %collective-permute-start = (bf16[16,8576]{1,0:T(8,128)(2,1)S(1)}, bf16[16,8576]{1,0:T(8,128)(2,1)S(1)}, u32[]{:S(2)}, u32[]{:S(2)}) collective-permute-start(bf16[16,8576]{1,0:T(8,128)(2,1)S(1)} %get-tuple-element.33), channel_id=1, source_target_pairs={{0,32},{2,34},{4,36},{6,38},{8,40},{10,42},{12,44},{14,46},{16,48}... | collective-permute-start | bytes 823304 | tf_op jit(solution)/shard_map/ppermute | solution.py:29
  7.4 9.0 %collective-permute-start.1 = (bf16[16,8576]{1,0:T(8,128)(2,1)S(1)}, bf16[16,8576]{1,0:T(8,128)(2,1)S(1)}, u32[]{:S(2)}, u32[]{:S(2)}) collective-permute-start(bf16[16,8576]{1,0:T(8,128)(2,1)S(1)} %get-tuple-element.34), channel_id=1, source_target_pairs={{0,8},{2,10},{4,12},{6,14},{8,0},{10,2},{12,4},{14,6},{16,24},{18,... | collective-permute-start | bytes 823304 | tf_op jit(solution)/shard_map/ppermute | solution.py:29
  10.3 9.1 %collective-permute-start.3 = (bf16[16,8576]{1,0:T(8,128)(2,1)S(1)}, bf16[16,8576]{1,0:T(8,128)(2,1)S(1)}, u32[]{:S(2)}, u32[]{:S(2)}) collective-permute-start(bf16[16,8576]{1,0:T(8,128)(2,1)S(1)} %get-tuple-element.41), channel_id=1, source_target_pairs={{0,2},{2,0},{4,6},{6,4},{8,10},{10,8},{12,14},{14,12},{16,18},{18,... | collective-permute-start | bytes 823304 | tf_op jit(solution)/shard_map/ppermute | solution.py:29
  11.5 10.7 %collective-permute-start.4 = (bf16[16,8576]{1,0:T(8,128)(2,1)S(1)}, bf16[16,8576]{1,0:T(8,128)(2,1)S(1)}, u32[]{:S(2)}, u32[]{:S(2)}) collective-permute-start(bf16[16,8576]{1,0:T(8,128)(2,1)S(1)} %get-tuple-element.42), channel_id=1, source_target_pairs={{0,4},{2,6},{4,0},{6,2},{8,12},{10,14},{12,8},{14,10},{16,20},{18,... | collective-permute-start | bytes 823304 | tf_op jit(solution)/shard_map/ppermute | solution.py:29
  11.9 10.3 %collective-permute-start.5 = (bf16[16,8576]{1,0:T(8,128)(2,1)S(1)}, bf16[16,8576]{1,0:T(8,128)(2,1)S(1)}, u32[]{:S(2)}, u32[]{:S(2)}) collective-permute-start(bf16[16,8576]{1,0:T(8,128)(2,1)S(1)} %get-tuple-element.43), channel_id=1, source_target_pairs={{0,16},{2,18},{4,20},{6,22},{8,24},{10,26},{12,28},{14,30},{16,0},... | collective-permute-start | bytes 823304 | tf_op jit(solution)/shard_map/ppermute | solution.py:29
  13.7 5.7 %collective-permute-start.2 = (f32[32,6]{1,0:T(8,128)S(1)}, f32[32,6]{1,0:T(8,128)S(1)}, u32[]{:S(2)}, u32[]{:S(2)}) collective-permute-start(f32[32,6]{1,0:T(8,128)S(1)} %get-tuple-element.36.gains), channel_id=1, source_target_pairs={{0,1},{1,0},{2,3},{3,2},{4,5},{5,4},{6,7},{7,6},{8,9},{9,8},{10,11... | collective-permute-start | bytes 2312 | tf_op jit(solution)/shard_map/ppermute | solution.py:29
  25.7 15.4 %collective-permute-start.12 = (bf16[6,8192]{1,0:T(8,128)(2,1)S(1)}, bf16[6,8192]{1,0:T(8,128)(2,1)S(1)}, u32[]{:S(2)}, u32[]{:S(2)}) collective-permute-start(bf16[6,8192]{1,0:T(8,128)(2,1)S(1)} %get-tuple-element.53), channel_id=1, source_target_pairs={{0,64},{2,66},{4,68},{6,70},{8,72},{10,74},{12,76},{14,78},{16,80}... | collective-permute-start | bytes 294920 | tf_op jit(solution)/shard_map/ppermute | solution.py:40
  27.6 4.1 %collective-permute-start.6 = (bf16[32,128]{1,0:T(8,128)(2,1)S(1)}, bf16[32,128]{1,0:T(8,128)(2,1)S(1)}, u32[]{:S(2)}, u32[]{:S(2)}) collective-permute-start(bf16[32,128]{1,0:T(8,128)(2,1)S(1)} %get-tuple-element.45), channel_id=1, source_target_pairs={{0,64},{2,66},{4,68},{6,70},{8,72},{10,74},{12,76},{14,78},{16,80}... | collective-permute-start | bytes 24584 | tf_op jit(solution)/shard_map/ppermute | solution.py:40
  27.7 4.6 %collective-permute-start.7 = (bf16[32,128]{1,0:T(8,128)(2,1)S(1)}, bf16[32,128]{1,0:T(8,128)(2,1)S(1)}, u32[]{:S(2)}, u32[]{:S(2)}) collective-permute-start(bf16[32,128]{1,0:T(8,128)(2,1)S(1)} %get-tuple-element.46), channel_id=1, source_target_pairs={{0,96},{2,98},{4,100},{6,102},{8,104},{10,106},{12,108},{14,110},{... | collective-permute-start | bytes 24584 | tf_op jit(solution)/shard_map/ppermute | solution.py:40
  28.6 4.6 %collective-permute-start.8 = (bf16[32,128]{1,0:T(8,128)(2,1)S(1)}, bf16[32,128]{1,0:T(8,128)(2,1)S(1)}, u32[]{:S(2)}, u32[]{:S(2)}) collective-permute-start(bf16[32,128]{1,0:T(8,128)(2,1)S(1)} %get-tuple-element.47), channel_id=1, source_target_pairs={{0,72},{2,74},{4,76},{6,78},{8,64},{10,66},{12,68},{14,70},{16,88}... | collective-permute-start | bytes 24584 | tf_op jit(solution)/shard_map/ppermute | solution.py:40
  36.0 3.2 %collective-permute-start.9 = (bf16[32,128]{1,0:T(8,128)(2,1)S(1)}, bf16[32,128]{1,0:T(8,128)(2,1)S(1)}, u32[]{:S(2)}, u32[]{:S(2)}) collective-permute-start(bf16[32,128]{1,0:T(8,128)(2,1)S(1)} %get-tuple-element.50), channel_id=1, source_target_pairs={{0,66},{2,64},{4,70},{6,68},{8,74},{10,72},{12,78},{14,76},{16,82}... | collective-permute-start | bytes 24584 | tf_op jit(solution)/shard_map/ppermute | solution.py:40
  36.9 3.1 %collective-permute-start.10 = (bf16[32,128]{1,0:T(8,128)(2,1)S(1)}, bf16[32,128]{1,0:T(8,128)(2,1)S(1)}, u32[]{:S(2)}, u32[]{:S(2)}) collective-permute-start(bf16[32,128]{1,0:T(8,128)(2,1)S(1)} %get-tuple-element.51), channel_id=1, source_target_pairs={{0,80},{2,82},{4,84},{6,86},{8,88},{10,90},{12,92},{14,94},{16,64}... | collective-permute-start | bytes 24584 | tf_op jit(solution)/shard_map/ppermute | solution.py:40
  38.0 3.1 %collective-permute-start.11 = (bf16[32,128]{1,0:T(8,128)(2,1)S(1)}, bf16[32,128]{1,0:T(8,128)(2,1)S(1)}, u32[]{:S(2)}, u32[]{:S(2)}) collective-permute-start(bf16[32,128]{1,0:T(8,128)(2,1)S(1)} %get-tuple-element.52), channel_id=1, source_target_pairs={{0,68},{2,70},{4,64},{6,66},{8,76},{10,78},{12,72},{14,74},{16,84}... | collective-permute-start | bytes 24584 | tf_op jit(solution)/shard_map/ppermute | solution.py:40

commit v3 on v2

v3 whole, which is shorter than its diff:
```python
import jax
import jax.numpy as jnp
from jax import lax
from jax.experimental import pallas as pl
from jax.experimental.pallas import tpu as pltpu
from jax.sharding import PartitionSpec as P

HEADS = 64
KVH = 8
HD = 128

SLOTS = 6
BITS = 5
FAR = (2, 4)
NEAR = (1, 3, 0)
FIRST = (BITS,) + FAR
BLOCK = 256
LOG2E = 1.4426950408889634
WEIGHT = 10**10

masked_score = -1e30
f32 = jnp.float32
bf16 = jnp.bfloat16


def swapped(value, axis, bit):
    mask = 2**bit
    pairs = [(source, source ^ mask) for source in range(lax.axis_size(axis))]
    return lax.ppermute(value, axis, pairs)


def across(value, bit):
    sections, replicas = lax.axis_size("section"), lax.axis_size("replica")
    mask = 2**bit if bit < BITS else 0
    pairs = [
        (s * replicas + r, ((s + 1) % sections) * replicas + (r ^ mask))
        for s in range(sections)
        for r in range(replicas)
    ]
    return lax.ppermute(value, ("section", "replica"), pairs)


def whole(space):
    return pl.BlockSpec(memory_space=space)


def in_hbm(*values):
    return [pltpu.with_memory_space_constraint(value, pltpu.HBM) for value in values]


def in_vmem(*values):
    return [pltpu.with_memory_space_constraint(value, pltpu.VMEM) for value in values]


def write_plan(own, src, lens, plan):
    first = own * SLOTS
    for entry in range(24):
        plan[entry] = 0
    for bit in range(BITS):
        partner = jnp.bitwise_xor(own, 1 << bit) * SLOTS
        leave = jnp.int32(0)
        served = jnp.int32(1)
        ask = jnp.int32(0)
        for j in range(SLOTS):
            there = src[partner + j] - first
            gives = (there >= 0) & (there < SLOTS)
            leave = jnp.where(gives, there, leave)
            served = jnp.where(gives, lens[partner + j], served)
            here = src[first + j] - partner
            ask = jnp.where((here >= 0) & (here < SLOTS), j, ask)
        plan[bit] = leave
        plan[8 + bit] = ask
        plan[16 + bit] = served
    kept_old = jnp.int32(0)
    kept_new = jnp.int32(0)
    for j in range(SLOTS):
        here = src[first + j] - first
        stays = (here >= 0) & (here < SLOTS)
        kept_old = jnp.where(stays, here, kept_old)
        kept_new = jnp.where(stays, j, kept_new)
    plan[5] = kept_old
    plan[13] = kept_new
    plan[21] = lens[first + kept_new]


def load_kernel(
    src_in, lens_in, table_in, queries, fresh, conv, x_proj, plan, table, gains, heads_out, far0, far1,
    src, lens, q_buf, fresh_buf, conv_buf, x_buf, head_rows, own_rows, sems,
):
    copies = [
        pltpu.make_async_copy(source, target, sems.at[i])
        for i, (source, target) in enumerate(
            (
                (src_in, src), (lens_in, lens), (queries, q_buf), (fresh, fresh_buf),
                (table_in, table), (conv, conv_buf), (x_proj, x_buf),
            )
        )
    ]
    for copy in copies:
        copy.start()
    copies[0].wait()
    copies[1].wait()
    write_plan(lax.axis_index("replica"), src, lens, plan)
    copies[2].wait()
    copies[3].wait()
    heads = head_rows.shape[1]
    half = heads // 2
    keys = fresh_buf.shape[-1] // HD
    own_rows[...] = jnp.zeros_like(own_rows)
    for h in range(heads):
        column = q_buf[:, h * HD : (h + 1) * HD].astype(f32)
        for slot in range(SLOTS):
            head_rows[slot, h : h + 1, :] = column[slot : slot + 1]
    for item in range(BITS + 1):
        slot = plan[8 + item]
        pair = fresh_buf[slot].astype(f32)
        for k in range(keys):
            own_rows[k : k + 1, :] = pair[0:1, k * HD : (k + 1) * HD]
            own_rows[keys + k : keys + k + 1, :] = pair[1:2, k * HD : (k + 1) * HD]
        heads_out[item] = jnp.concatenate(
            [head_rows[slot, 0:half], head_rows[slot, half:heads], own_rows[...]], axis=1
        ).astype(bf16)
    for bit, out in zip(FAR, (far0, far1)):
        out[...] = heads_out[bit]
    copies[4].wait()
    copies[5].wait()
    copies[6].wait()
    gains[...] = lax.dot_general(
        x_buf[...], conv_buf[...], (((1,), (1,)), ((), ())), preferred_element_type=f32
    )


def load(source_slot, lengths, block_table, queries, fresh, conv, x_proj):
    heads = queries.shape[1] // HD
    half = heads // 2
    return pl.pallas_call(
        load_kernel,
        out_shape=(
            pltpu.SMEM((24,), jnp.int32),
            pltpu.SMEM(block_table.shape, jnp.int32),
            pltpu.VMEM((x_proj.shape[0], SLOTS), f32),
            pltpu.VMEM((BITS + 1, half, 3 * HD), bf16),
        )
        + (pltpu.VMEM((half, 3 * HD), bf16),) * len(FAR),
        in_specs=[whole(pl.ANY)] * 7,
        out_specs=(whole(pltpu.SMEM),) * 2 + (whole(pltpu.VMEM),) * (2 + len(FAR)),
        scratch_shapes=[
            pltpu.SMEM(source_slot.shape, jnp.int32),
            pltpu.SMEM(lengths.shape, jnp.int32),
            pltpu.VMEM(queries.shape, bf16),
            pltpu.VMEM(fresh.shape, bf16),
            pltpu.VMEM(conv.shape, bf16),
            pltpu.VMEM(x_proj.shape, bf16),
            pltpu.VMEM((SLOTS, heads, HD), f32),
            pltpu.VMEM((half, HD), f32),
            pltpu.SemaphoreType.DMA((7,)),
        ],
        compiler_params=pltpu.CompilerParams(vmem_limit_bytes=4 * 2**20),
        cost_estimate=pl.CostEstimate(flops=WEIGHT, transcendentals=0, bytes_accessed=queries.size * 2),
    )(*in_hbm(source_slot, lengths, block_table, queries, fresh, conv, x_proj))


def pack_kernel(plan, held, heads, later, *packs):
    width = held.shape[-1]
    for entry in range(24):
        later[entry] = plan[entry]
    for bit, out in zip(NEAR, packs):
        out[:, :width] = held[plan[bit]].astype(bf16)
        out[:, width:] = heads[bit]


def pack(plan, held, heads):
    n, width = held.shape[1:]
    return pl.pallas_call(
        pack_kernel,
        out_shape=(pltpu.SMEM(plan.shape, jnp.int32),)
        + (pltpu.VMEM((n, width + heads.shape[-1]), bf16),) * len(NEAR),
        in_specs=[whole(pltpu.SMEM)] + [whole(pltpu.VMEM)] * 2,
        out_specs=(whole(pltpu.SMEM),) + (whole(pltpu.VMEM),) * len(NEAR),
        compiler_params=pltpu.CompilerParams(vmem_limit_bytes=4 * 2**20),
        cost_estimate=pl.CostEstimate(
            flops=0, transcendentals=0, bytes_accessed=held.size * 3
        ),
    )(plan, *in_vmem(held, heads))


def attend_items(items, plan, table, pool, extras, outs):
    page = pool.shape[2]
    pages = table.shape[1]
    per_block = BLOCK // page
    blocks = pages // per_block
    pair_width = 2 * HD
    pairs = pool.shape[3] // pair_width
    group = HEADS // KVH
    rows = 2 * group
    kv_heads = 2 * pairs
    scale = HD ** (-0.5)
    row_id = lax.broadcasted_iota(jnp.int32, (rows, pair_width), 0)
    lane_id = lax.broadcasted_iota(jnp.int32, (rows, pair_width), 1)
    own_block = (row_id < group) == (lane_id < HD)
    token_id = lax.broadcasted_iota(jnp.int32, (rows * pairs, BLOCK), 1)

    def block_of(which, places, j):
        return jnp.concatenate(
            [pool[which, places[j * per_block + u]] for u in range(per_block)], axis=0
        )

    def places_of(item):
        slot = plan[item]
        return [table[slot, p] for p in range(pages)]

    def halves_of(extra):
        base = extra.shape[1] - 3 * HD
        return [extra[:, base + i * HD : base + (i + 1) * HD] for i in range(2)]

    def score_block(spread, length, places, j):
        keys = block_of(0, places, j)
        parts = [
            lax.dot_general(
                spread[i],
                keys[:, i * pair_width : (i + 1) * pair_width],
                (((1,), (1,)), ((), ())),
                preferred_element_type=f32,
            )
            for i in range(pairs)
        ]
        score = jnp.concatenate(parts, axis=0) * scale
        return jnp.where(token_id < length - j * BLOCK, score, masked_score)

    def ready(item, extra):
        spread = [
            jnp.where(own_block, jnp.concatenate([half, half], axis=1).astype(f32), 0.0).astype(bf16)
            for half in halves_of(extra)
        ]
        return spread, plan[16 + item], places_of(item)

    current = ready(items[0], extras[0])
    scores = [score_block(*current, j) for j in range(blocks)]
    for at, (extra, out) in enumerate(zip(extras, outs)):
        places = current[2]
        top = scores[0]
        for score in scores[1:]:
            top = jnp.maximum(top, score)
        cache_peak = jnp.max(top, axis=1, keepdims=True)
        weights = [jnp.exp(score - cache_peak) for score in scores]
        summed = weights[0]
        for weight in weights[1:]:
            summed = summed + weight
        cache_total = jnp.sum(summed, axis=1, keepdims=True)
        following = at + 1 < len(items)
        if following:
            current = ready(items[at + 1], extras[at + 1])
        scores = []
        full = [None] * pairs
        for j in range(blocks):
            if following:
                scores.append(score_block(*current, j))
            values = block_of(1, places, j)
            rounded = weights[j].astype(bf16)
            for i in range(pairs):
                part = jnp.dot(
                    rounded[i * rows : (i + 1) * rows],
                    values[:, i * pair_width : (i + 1) * pair_width],
                    preferred_element_type=f32,
                )
                full[i] = part if full[i] is None else full[i] + part
        gathered = jnp.concatenate(
            [
                full[k // 2][(k % 2) * group : (k % 2 + 1) * group, (k % 2) * HD : (k % 2 + 1) * HD]
                for k in range(kv_heads)
            ],
            axis=0,
        )
        own = extra[:, extra.shape[1] - HD :].astype(f32)
        own_keys = jnp.concatenate(
            [jnp.broadcast_to(own[k : k + 1], (group, HD)) for k in range(kv_heads)], axis=0
        )
        own_values = jnp.concatenate(
            [jnp.broadcast_to(own[kv_heads + k : kv_heads + k + 1], (group, HD)) for k in range(kv_heads)],
            axis=0,
        )
        head_rows = jnp.concatenate(halves_of(extra), axis=0).astype(f32)
        own_score = jnp.sum(head_rows * own_keys, axis=1, keepdims=True) * scale
        joint_peak = jnp.maximum(cache_peak, own_score)
        cache_weight = jnp.exp(cache_peak - joint_peak)
        own_weight = jnp.exp(own_score - joint_peak)
        numerator = cache_weight * gathered + own_weight * own_values
        attended = numerator / (cache_weight * cache_total + own_weight)
        out(attended)


def rates_kernel(plan, conv, dt, a_log, bias, skip, rate, step_rows, drive_rows, direct):
    mixer = conv[...].astype(f32)
    step_in = dt[...].astype(f32) + bias[...]
    step = jnp.maximum(step_in, 0.0) + jnp.log1p(jnp.exp(-jnp.abs(step_in)))
    drive = step * mixer
    direct[...] = skip[...] * mixer
    for row in range(SLOTS):
        step_rows[row] = step[row : row + 1]
        drive_rows[row] = drive[row : row + 1]
    rate[...] = jnp.exp(a_log[...]) * (-LOG2E)


def rates(plan, conv, dt, a_log, bias, skip):
    slots, width = conv.shape
    rows = pltpu.VMEM((slots, 1, width), f32)
    return pl.pallas_call(
        rates_kernel,
        out_shape=(pltpu.VMEM(a_log.shape, f32), rows, rows, pltpu.VMEM((slots, width), f32)),
        in_specs=[whole(pltpu.SMEM)] + [whole(pltpu.VMEM)] * 5,
        out_specs=(whole(pltpu.VMEM),) * 4,
        compiler_params=pltpu.CompilerParams(vmem_limit_bytes=8 * 2**20),
        cost_estimate=pl.CostEstimate(
            flops=10 * slots * width,
            transcendentals=a_log.size + 2 * slots * width,
            bytes_accessed=a_log.size * 4,
        ),
    )(plan, conv, dt, a_log, bias, skip)


def update_items(
    items, plan, gains, rate, step_rows, drive_rows, held, moved, new_state, mixed_rows, out_buf, sems
):
    n, width = rate.shape
    coupled = gains[...]
    lane = lax.broadcasted_iota(jnp.int32, coupled.shape, 1)
    copies = []
    for i, item in enumerate(items):
        slot = plan[8 + item]
        column = jnp.sum(jnp.where(lane == slot, coupled, 0.0), axis=1, keepdims=True)
        input_gain = jnp.broadcast_to(column[0:n], (n, HD))
        read_gain = jnp.broadcast_to(column[n : 2 * n], (n, HD))
        for c in range(0, width, HD):
            at = slice(c, c + HD)
            previous = held[plan[BITS], :, at] if item == BITS else moved[i][:, at].astype(f32)
            step_row = jnp.broadcast_to(step_rows[slot, :, at], (n, HD))
            drive_row = jnp.broadcast_to(drive_rows[slot, :, at], (n, HD))
            updated = jnp.exp2(step_row * rate[:, at]) * previous + drive_row * input_gain
            out_buf[i, :, at] = updated
            mixed_rows[slot, :, at] = jnp.sum(read_gain * updated, axis=0, keepdims=True)
        copies.append(pltpu.make_async_copy(out_buf.at[i], new_state.at[slot], sems.at[i]))
        copies[-1].start()
    return copies


def first_kernel(
    plan, table, pool, held, heads, q0, q1, gains, gains_far, later, coupled, own, row0, row1
):
    width = held.shape[-1]
    coupled[...] = gains[...] + gains_far[...]
    for entry in range(24):
        later[entry] = plan[entry]

    def keep(attended):
        own[...] = attended.astype(bf16)

    def into(row):
        def put(attended):
            half = attended.shape[0] // 2
            row[:, width : width + HD] = attended[:half].astype(bf16)
            row[:, width + HD :] = attended[half:].astype(bf16)

        return put

    attend_items(FIRST, plan, table, pool, [heads.at[BITS], q0, q1], [keep, into(row0), into(row1)])
    for bit, row in zip(FAR, (row0, row1)):
        row[:, :width] = held[plan[bit]].astype(bf16)


def attention_cost(count):
    return dict(
        flops=count * 4 * 1280 * 32 * 512,
        transcendentals=count * 1280 * 32,
        bytes_accessed=count * 2 * 80 * 16 * 1024,
    )


def first(plan, table, pool, held, heads, gains, gains_far, queries):
    n, width = held.shape[1:]
    result = pltpu.VMEM((2 * n, HD), bf16)
    return pl.pallas_call(
        first_kernel,
        out_shape=(pltpu.SMEM(plan.shape, jnp.int32), pltpu.VMEM(gains.shape, f32), result)
        + (pltpu.VMEM((n, width + 2 * HD), bf16),) * len(FAR),
        in_specs=[whole(pltpu.SMEM)] * 2 + [whole(pltpu.VMEM)] * (5 + len(FAR)),
        out_specs=(whole(pltpu.SMEM),) + (whole(pltpu.VMEM),) * (2 + len(FAR)),
        compiler_params=pltpu.CompilerParams(vmem_limit_bytes=8 * 2**20),
        cost_estimate=pl.CostEstimate(**attention_cost(len(FIRST))),
    )(plan, table, *in_vmem(pool, held, heads, *queries, gains, gains_far))


def near_kernel(
    plan, table, pool, gains, rate, step_rows, drive_rows, held, x0, x1, x2,
    later, new_state, mixed_rows, a0, a1, a2,
    out_buf, sems,
):
    for entry in range(24):
        later[entry] = plan[entry]
    extras = [x0, x1, x2]
    copies = update_items(
        (BITS,) + NEAR, plan, gains, rate, step_rows, drive_rows, held, [None] + extras,
        new_state, mixed_rows, out_buf, sems,
    )

    def into(out):
        def put(attended):
            out[...] = attended.astype(bf16)

        return put

    attend_items(NEAR, plan, table, pool, extras, [into(a0), into(a1), into(a2)])
    for copy in copies:
        copy.wait()


def near(plan, table, pool, gains, made, held, extras):
    slots, n, width = held.shape
    count = 1 + len(NEAR)
    inputs = in_vmem(pool, gains, *made[:3], held, *extras)
    return pl.pallas_call(
        near_kernel,
        out_shape=(
            pltpu.SMEM(plan.shape, jnp.int32),
            pltpu.HBM(held.shape, f32),
            pltpu.VMEM((slots, 1, width), f32),
        )
        + (pltpu.VMEM((2 * n, HD), bf16),) * len(NEAR),
        in_specs=[whole(pltpu.SMEM)] * 2 + [whole(pltpu.VMEM)] * len(inputs),
        out_specs=(whole(pltpu.SMEM), whole(pl.ANY)) + (whole(pltpu.VMEM),) * (1 + len(NEAR)),
        scratch_shapes=[pltpu.VMEM((count, n, width), f32), pltpu.SemaphoreType.DMA((count,))],
        compiler_params=pltpu.CompilerParams(vmem_limit_bytes=8 * 2**20),
        cost_estimate=pl.CostEstimate(**attention_cost(len(NEAR))),
    )(plan, table, *inputs)


def last_kernel(
    plan, gains, rate, step_rows, drive_rows, direct, own, x0, x1, b0, b1, b2, state_before, rows_before,
    later, new_state, mixed_rows, final, placed,
    mixed_all, out_buf, sems,
):
    for entry in range(24):
        later[entry] = plan[entry]
    slots, width = direct.shape
    copies = update_items(
        FAR, plan, gains, rate, step_rows, drive_rows, None, [x0, x1],
        new_state, mixed_rows, out_buf, sems,
    )
    mixed_all[...] = jnp.zeros_like(mixed_all)
    for slot in range(slots):
        mixed_all[slot : slot + 1, :] = mixed_rows[slot] + direct[slot : slot + 1, :]
    final[:, :width] = mixed_all[...].astype(bf16)
    results = [own[...].astype(f32)]
    for row in (x0, x1):
        results.append(
            jnp.concatenate([row[:, width : width + HD], row[:, width + HD :]], axis=0).astype(f32)
        )
    for i, result in enumerate(results):
        for k in range(result.shape[0] // 8):
            start = width + (4 * i + k) * HD
            final[:, start : start + HD] = result[8 * k : 8 * k + 8].astype(bf16)
    for item, back in zip(NEAR, (b0, b1, b2)):
        placed[plan[8 + item]] = back[...].astype(f32)
    for copy in copies:
        copy.wait()


def last(plan, gains, made, own, extras, backs, new_state, mixed_rows):
    slots, width = made[3].shape
    n = made[0].shape[0]
    inputs = in_vmem(gains, *made, own, *extras, *backs) + in_hbm(new_state) + in_vmem(mixed_rows)
    vmem = whole(pltpu.VMEM)
    return pl.pallas_call(
        last_kernel,
        out_shape=(
            pltpu.SMEM(plan.shape, jnp.int32),
            pltpu.HBM(new_state.shape, f32),
            pltpu.VMEM(mixed_rows.shape, f32),
            pltpu.VMEM((8, width + 12 * HD), bf16),
            pltpu.VMEM((slots, 2 * n, HD), f32),
        ),
        in_specs=[whole(pltpu.SMEM)] + [vmem] * (len(inputs) - 2) + [whole(pl.ANY), vmem],
        out_specs=(whole(pltpu.SMEM), whole(pl.ANY), vmem, vmem, vmem),
        scratch_shapes=[
            pltpu.VMEM((8, width), f32),
            pltpu.VMEM((len(FAR), n, width), f32),
            pltpu.SemaphoreType.DMA((len(FAR),)),
        ],
        input_output_aliases={len(inputs) - 1: 1, len(inputs): 2},
        compiler_params=pltpu.CompilerParams(vmem_limit_bytes=8 * 2**20),
        cost_estimate=pl.CostEstimate(
            flops=16 * n * width, transcendentals=2 * n * width, bytes_accessed=12 * n * width
        ),
    )(plan, *inputs)


def place_kernel(plan, final, placed, attended, handed, head_rows, rows, rounded, mixed, sems):
    slots, width = mixed.shape
    mixed[...] = final[:, :width][0:slots]
    through = pltpu.make_async_copy(mixed, handed, sems.at[0])
    through.start()
    head_rows[...] = placed[...]
    for i, item in enumerate(FIRST):
        for k in range(head_rows.shape[1] // 8):
            start = width + (4 * i + k) * HD
            head_rows[plan[8 + item], 8 * k : 8 * k + 8] = final[:, start : start + HD].astype(f32)
    for slot in range(slots):
        for h in range(head_rows.shape[1]):
            rows[slot : slot + 1, h * HD : (h + 1) * HD] = head_rows[slot, h : h + 1, :]
    rounded[...] = rows[...].astype(bf16)
    out = pltpu.make_async_copy(rounded, attended, sems.at[1])
    out.start()
    through.wait()
    out.wait()


def place(plan, final, placed):
    heads = placed.shape[1]
    shape = (SLOTS, heads * HD)
    mixed = (SLOTS, final.shape[1] - 12 * HD)
    return pl.pallas_call(
        place_kernel,
        out_shape=(pltpu.HBM(shape, bf16), pltpu.HBM(mixed, bf16)),
        in_specs=[whole(pltpu.SMEM)] + [whole(pltpu.VMEM)] * 2,
        out_specs=(whole(pl.ANY),) * 2,
        scratch_shapes=[
            pltpu.VMEM((SLOTS, heads, HD), f32),
            pltpu.VMEM(shape, f32),
            pltpu.VMEM(shape, bf16),
            pltpu.VMEM(mixed, bf16),
            pltpu.SemaphoreType.DMA((2,)),
        ],
    )(plan, *in_vmem(final, placed))


def per_device(
    source_slot,
    lengths,
    block_table,
    queries,
    kv_pool,
    new_kv,
    ssm_state,
    conv_out,
    dt_raw,
    x_proj,
    a_log,
    dt_bias,
    skip_gain,
):
    fresh = jnp.transpose(new_kv[0], (1, 0, 2))
    held = ssm_state[0]
    pool = kv_pool[0]
    plan, table, gains, heads, *queries_far = load(
        source_slot, lengths, block_table, queries[0], fresh, conv_out[0], x_proj[0]
    )
    gains_far = swapped(gains, "tensor", 0)
    queries_far = [swapped(value, "replica", bit) for bit, value in zip(FAR, queries_far)]
    plan, *rows = pack(plan, held, heads)
    rows_near = [swapped(value, "replica", bit) for bit, value in zip(NEAR, rows)]
    plan, gains, own, *rows = first(plan, table, pool, held, heads, gains, gains_far, queries_far)
    rows_far = [swapped(value, "replica", bit) for bit, value in zip(FAR, rows)]
    made = rates(plan, conv_out[0], dt_raw[0], a_log[0], dt_bias, skip_gain)
    plan, new_state, mixed_rows, *attended = near(plan, table, pool, gains, made, held, rows_near)
    backs = [across(value, bit) for bit, value in zip(NEAR, attended)]
    plan, new_state, _, final, placed = last(
        plan, gains, made, own, rows_far, backs, new_state, mixed_rows
    )
    handed_attention, handed_mamba = place(plan, across(final, BITS), placed)
    return handed_mamba[None], handed_attention[None], new_state[None]


def solution(mesh):
    in_specs = (
        P(),
        P(),
        P("replica", None),
        P("section", "replica", "tensor"),
        P("section", None, "replica", None, "tensor"),
        P("section", None, "replica", "tensor"),
        P("section", "replica", None, "tensor"),
        P("section", "replica", "tensor"),
        P("section", "replica", "tensor"),
        P("section", None, "tensor"),
        P("section", None, "tensor"),
        P("section", "tensor"),
        P("section", "tensor"),
    )
    out_specs = (
        P("section", "replica", "tensor"),
        P("section", "replica", "tensor"),
        P("section", "replica", None, "tensor"),
    )
    return jax.shard_map(
        per_device, mesh=mesh, in_specs=in_specs, out_specs=out_specs, check_vma=False
    )
```

time: 42 us -> 34.9 us (0.83)
  Pallas kernels: 12.4 us -> 9.63 us
  waiting for transfers between devices: 6.69 us -> 4.3 us
  starting transfers between devices: 21.8 us -> 20 us
    ppermute x7 -> x4, starting transfers between devices: 9.29 us -> 5.8 us  [across(): return lax.ppermute(value, ('section', 'replica'), pairs)]
    ppermute x6 -> x8, waiting for transfers between devices: 3.37 us -> 0.8 us  [swapped(): return lax.ppermute(value, axis, pairs)]
    pallas_call x5, Pallas kernels: 9.7 us -> 7.2 us  [the longest x1 3.68 us: near(): pl.pallas_call(near_kernel, out_shape=(pltpu.SMEM(plan.shape, jnp.int32),...]
    ppermute x6 -> x8, starting transfers between devices: 12.5 us -> 14.2 us  [swapped(): return lax.ppermute(value, axis, pairs)]
    ppermute x7 -> x4, waiting for transfers between devices: 3.32 us -> 3.49 us  [across(): return lax.ppermute(value, ('section', 'replica'), pairs)]
  transfers between devices with their start and end apart: 13 -> 12, of which waited for: 7 -> 6; matrix products, arithmetic and copies ran while one was open for 0% -> 0% of each run, Pallas kernels for 15% -> 17%
where the time goes in v3:
time: 34.9 us; the launch traced here: 34.8 us
  starting transfers between devices  20 us (57%)
  Pallas kernels  9.63 us (28%)
  waiting for transfers between devices  4.3 us (12%)
  between operations  0.81 us (2%)
    ppermute x8, starting transfers between devices, swapped(): return lax.ppermute(value, axis, pairs)  14.2 us
    ppermute x4, starting transfers between devices, across(): return lax.ppermute(value, ('section', 'replica'), pairs)  5.8 us
    pallas_call x1, Pallas kernels, near(): pl.pallas_call(near_kernel, out_shape=(pltpu.SMEM(plan.shape, jnp.int32),...  3.68 us
    ppermute x4, waiting for transfers between devices, across(): return lax.ppermute(value, ('section', 'replica'), pairs)  3.49 us
    pallas_call x1, Pallas kernels, first(): pl.pallas_call(first_kernel, out_shape=(pltpu.SMEM(plan.shape, jnp.int32)...  1.86 us
    pallas_call x1, Pallas kernels, load(): pl.pallas_call(load_kernel, out_shape=(pltpu.SMEM((24,), jnp.int32), pltp...  1.68 us
    pallas_call x1, Pallas kernels, last(): pl.pallas_call(last_kernel, out_shape=(pltpu.SMEM(plan.shape, jnp.int32),...  1.23 us
    ppermute x8, waiting for transfers between devices, swapped(): return lax.ppermute(value, axis, pairs)  0.8 us
  transfers between devices with their start and end apart: 12, of which 6 were waited for; matrix products, arithmetic and copies ran while one was open for 0% of the time, Pallas kernels for 17%

profile of v3, /device:TPU:1, one launch (start us, length us, event | category | flops | bytes accessed | tf_op | source)
XLA Modules:
  0.0 34.8 jit_solution(15872812872570433478)
XLA Ops:
  0.7 1.7 %shard_map.148 = (s32[24]{0:T(128)S(4)}, s32[6,80]{1,0:T(8,128)S(4)}, f32[32,6]{1,0:T(8,128)S(1)}, bf16[6,16,384]{2,1,0:T(8,128)(2,1)S(1)}, bf16[16,384]{1,0:T(8,128)(2,1)S(1)}, /*index=5*/bf16[16,384]{1,0:T(8,128)(2,1)S(1)}) custom-call(s32[192]{0:T(256)} %src_in.1, s32[192]{0:T(256)} %lens_in.1, s32[6,80]{1,0:T(8,128)} %table_in.1, ...), custom_call_target="tpu_custom_call" | custom-call | flops 10000000000 | bytes 49152 | tf_op jit(solution)/shard_map/pallas_call | solution.py:136
  2.4 3.7 %collective-permute-start.2 = (f32[32,6]{1,0:T(8,128)S(1)}, f32[32,6]{1,0:T(8,128)S(1)}, u32[]{:S(2)}, u32[]{:S(2)}) collective-permute-start(f32[32,6]{1,0:T(8,128)S(1)} %get-tuple-element.40.gains), channel_id=1, source_target_pairs={{0,1},{1,0},{2,3},{3,2},{4,5},{5,4},{6,7},{7,6},{8,9},{9,8},{10,11... | collective-permute-start | bytes 2312 | tf_op jit(solution)/shard_map/ppermute | solution.py:29
  6.0 2.9 %collective-permute-start = (bf16[16,384]{1,0:T(8,128)(2,1)S(1)}, bf16[16,384]{1,0:T(8,128)(2,1)S(1)}, u32[]{:S(2)}, u32[]{:S(2)}) collective-permute-start(bf16[16,384]{1,0:T(8,128)(2,1)S(1)} %get-tuple-element.38), channel_id=1, source_target_pairs={{0,8},{2,10},{4,12},{6,14},{8,0},{10,2},{12,4},{14,6},{16,24},{18,... | collective-permute-start | bytes 36872 | tf_op jit(solution)/shard_map/ppermute | solution.py:29
  8.9 3.6 %collective-permute-start.1 = (bf16[16,384]{1,0:T(8,128)(2,1)S(1)}, bf16[16,384]{1,0:T(8,128)(2,1)S(1)}, u32[]{:S(2)}, u32[]{:S(2)}) collective-permute-start(bf16[16,384]{1,0:T(8,128)(2,1)S(1)} %get-tuple-element.39), channel_id=1, source_target_pairs={{0,32},{2,34},{4,36},{6,38},{8,40},{10,42},{12,44},{14,46},{16,48}... | collective-permute-start | bytes 36872 | tf_op jit(solution)/shard_map/ppermute | solution.py:29
  12.6 0.5 %collective-permute-start.3 = (bf16[16,8576]{1,0:T(8,128)(2,1)S(1)}, bf16[16,8576]{1,0:T(8,128)(2,1)S(1)}, u32[]{:S(2)}, u32[]{:S(2)}) collective-permute-start(bf16[16,8576]{1,0:T(8,128)(2,1)S(1)} %get-tuple-element.46), channel_id=1, source_target_pairs={{0,4},{2,6},{4,0},{6,2},{8,12},{10,14},{12,8},{14,10},{16,20},{18,... | collective-permute-start | bytes 823304 | tf_op jit(solution)/shard_map/ppermute | solution.py:29
  13.1 0.8 %collective-permute-start.4 = (bf16[16,8576]{1,0:T(8,128)(2,1)S(1)}, bf16[16,8576]{1,0:T(8,128)(2,1)S(1)}, u32[]{:S(2)}, u32[]{:S(2)}) collective-permute-start(bf16[16,8576]{1,0:T(8,128)(2,1)S(1)} %get-tuple-element.47), channel_id=1, source_target_pairs={{0,16},{2,18},{4,20},{6,22},{8,24},{10,26},{12,28},{14,30},{16,0},... | collective-permute-start | bytes 823304 | tf_op jit(solution)/shard_map/ppermute | solution.py:29
  13.8 0.3 collective-permute-start.5
  14.3 1.9 %shard_map.150 = (s32[24]{0:T(128)S(4)}, f32[32,6]{1,0:T(8,128)S(1)}, bf16[32,128]{1,0:T(8,128)(2,1)S(1)}, bf16[16,8448]{1,0:T(8,128)(2,1)S(1)}, bf16[16,8448]{1,0:T(8,128)(2,1)S(1)}) custom-call(s32[24]{0:T(128)S(4)} %get-tuple-element.36.plan, s32[6,80]{1,0:T(8,128)S(4)} %get-tuple-element.37.table, bf16[2,480,16,512]{3,2,1,0:T(8,128)(2,1)S(1)} %bitcast.15, ...), custom_call_target="tpu_custom_call" | custom-call | flops 251658240 | bytes 7864320 | tf_op jit(solution)/shard_map/pallas_call | solution.py:381
  16.1 1.6 %collective-permute-start.6 = (bf16[16,8448]{1,0:T(8,128)(2,1)S(1)}, bf16[16,8448]{1,0:T(8,128)(2,1)S(1)}, u32[]{:S(2)}, u32[]{:S(2)}) collective-permute-start(bf16[16,8448]{1,0:T(8,128)(2,1)S(1)} %get-tuple-element.52), channel_id=1, source_target_pairs={{0,8},{2,10},{4,12},{6,14},{8,0},{10,2},{12,4},{14,6},{16,24},{18,... | collective-permute-start | bytes 811016 | tf_op jit(solution)/shard_map/ppermute | solution.py:29
  17.7 0.9 %collective-permute-start.7 = (bf16[16,8448]{1,0:T(8,128)(2,1)S(1)}, bf16[16,8448]{1,0:T(8,128)(2,1)S(1)}, u32[]{:S(2)}, u32[]{:S(2)}) collective-permute-start(bf16[16,8448]{1,0:T(8,128)(2,1)S(1)} %get-tuple-element.53), channel_id=1, source_target_pairs={{0,32},{2,34},{4,36},{6,38},{8,40},{10,42},{12,44},{14,46},{16,48}... | collective-permute-start | bytes 811016 | tf_op jit(solution)/shard_map/ppermute | solution.py:29
  18.7 0.4 %shard_map.151 = (f32[16,8192]{1,0:T(8,128)S(1)}, f32[6,1,8192]{2,1,0:T(1,128)S(1)}, f32[6,1,8192]{2,1,0:T(1,128)S(1)}, f32[6,8192]{1,0:T(8,128)S(1)}) custom-call(s32[24]{0:T(128)S(4)} %get-tuple-element.41.plan, bf16[6,8192]{1,0:T(8,128)(2,1)S(1)} %bitcast.22, bf16[6,8192]{1,0:T(8,128)(2,1)S(1)} %bitcast.23, f32[16,8192]{1,0:T(8,128)S(1)} %bitcast.20, ...), custom_call_target="tpu_custom_call" | custom-call | flops 491520 | bytes 524288 | tf_op jit(solution)/shard_map/pallas_call | solution.py:307
  19.0 0.2 collective-permute-done.3.x0
  19.2 0.4 %collective-permute-done.4.x1 = bf16[16,8576]{1,0:T(8,128)(2,1)S(1)} collective-permute-done((bf16[16,8576]{1,0:T(8,128)(2,1)S(1)}, bf16[16,8576]{1,0:T(8,128)(2,1)S(1)}, u32[]{:S(2)}, u32[]{:S(2)}) %collective-permute-start.4) | collective-permute-done | bytes 274464 | tf_op jit(solution)/shard_map/ppermute | solution.py:29
  19.6 0.2 collective-permute-done.5.x2
  19.8 3.7 %shard_map.152 = (s32[24]{0:T(128)S(4)}, f32[6,16,8192]{2,1,0:T(8,128)}, f32[6,1,8192]{2,1,0:T(1,128)S(1)}, bf16[32,128]{1,0:T(8,128)(2,1)S(1)}, bf16[32,128]{1,...) custom-call(s32[24]{0:T(128)S(4)} %get-tuple-element.41.plan, s32[6,80]{1,0:T(8,128)S(4)} %get-tuple-element.37.table, ...), custom_call_target="tpu_custom_call" | custom-call | flops 251658240 | bytes 7864320 | tf_op jit(solution)/shard_map/pallas_call | solution.py:420
  23.5 4.0 %collective-permute-start.8 = (bf16[32,128]{1,0:T(8,128)(2,1)S(1)}, bf16[32,128]{1,0:T(8,128)(2,1)S(1)}, u32[]{:S(2)}, u32[]{:S(2)}) collective-permute-start(bf16[32,128]{1,0:T(8,128)(2,1)S(1)} %get-tuple-element.54), channel_id=1, source_target_pairs={{0,68},{2,70},{4,64},{6,66},{8,76},{10,78},{12,72},{14,74},{16,84}... | collective-permute-start | bytes 24584 | tf_op jit(solution)/shard_map/ppermute | solution.py:40
  27.6 0.7 %collective-permute-start.9 = (bf16[32,128]{1,0:T(8,128)(2,1)S(1)}, bf16[32,128]{1,0:T(8,128)(2,1)S(1)}, u32[]{:S(2)}, u32[]{:S(2)}) collective-permute-start(bf16[32,128]{1,0:T(8,128)(2,1)S(1)} %get-tuple-element.55), channel_id=1, source_target_pairs={{0,80},{2,82},{4,84},{6,86},{8,88},{10,90},{12,92},{14,94},{16,64}... | collective-permute-start | bytes 24584 | tf_op jit(solution)/shard_map/ppermute | solution.py:40
  28.2 0.6 %collective-permute-start.10 = (bf16[32,128]{1,0:T(8,128)(2,1)S(1)}, bf16[32,128]{1,0:T(8,128)(2,1)S(1)}, u32[]{:S(2)}, u32[]{:S(2)}) collective-permute-start(bf16[32,128]{1,0:T(8,128)(2,1)S(1)} %get-tuple-element.56), channel_id=1, source_target_pairs={{0,66},{2,64},{4,70},{6,68},{8,74},{10,72},{12,78},{14,76},{16,82}... | collective-permute-start | bytes 24584 | tf_op jit(solution)/shard_map/ppermute | solution.py:40
  28.9 1.7 %collective-permute-done.9.b1 = bf16[32,128]{1,0:T(8,128)(2,1)S(1)} collective-permute-done((bf16[32,128]{1,0:T(8,128)(2,1)S(1)}, bf16[32,128]{1,0:T(8,128)(2,1)S(1)}, u32[]{:S(2)}, u32[]{:S(2)}) %collective-permute-start.9) | collective-permute-done | bytes 8224 | tf_op jit(solution)/shard_map/ppermute | solution.py:40
  30.6 0.7 %collective-permute-done.10.b2 = bf16[32,128]{1,0:T(8,128)(2,1)S(1)} collective-permute-done((bf16[32,128]{1,0:T(8,128)(2,1)S(1)}, bf16[32,128]{1,0:T(8,128)(2,1)S(1)}, u32[]{:S(2)}, u32[]{:S(2)}) %collective-permute-start.10) | collective-permute-done | bytes 8224 | tf_op jit(solution)/shard_map/ppermute | solution.py:40
  31.3 1.2 %shard_map.153 = (s32[24]{0:T(128)S(4)}, f32[6,16,8192]{2,1,0:T(8,128)}, f32[6,1,8192]{2,1,0:T(1,128)S(1)}, bf16[8,9728]{1,0:T(8,128)(2,1)S(1)}, f32[6,32,128]{2,1,0:T(8,128)S(1)}) custom-call(s32[24]{0:T(128)S(4)} %get-tuple-element.49.plan, f32[32,6]{1,0:T(8,128)S(1)} %get-tuple-element.42.gains, ...), custom_call_target="tpu_custom_call", output_to_operand_aliasing={{1}: (12, {}), {2}: (13, {})} | custom-call | flops 2097152 | bytes 1572864 | tf_op jit(solution)/shard_map/pallas_call | solution.py:472
  32.6 0.5 %collective-permute-start.11 = (bf16[8,9728]{1,0:T(8,128)(2,1)S(1)}, bf16[8,9728]{1,0:T(8,128)(2,1)S(1)}, u32[]{:S(2)}, u32[]{:S(2)}) collective-permute-start(bf16[8,9728]{1,0:T(8,128)(2,1)S(1)} %get-tuple-element.60), channel_id=1, source_target_pairs={{0,64},{2,66},{4,68},{6,70},{8,72},{10,74},{12,76},{14,78},{16,80}... | collective-permute-start | bytes 466952 | tf_op jit(solution)/shard_map/ppermute | solution.py:40
  33.0 1.0 %collective-permute-done.11.final = bf16[8,9728]{1,0:T(8,128)(2,1)S(1)} collective-permute-done((bf16[8,9728]{1,0:T(8,128)(2,1)S(1)}, bf16[8,9728]{1,0:T(8,128)(2,1)S(1)}, u32[]{:S(2)}, u32[]{:S(2)}) %collective-permute-start.11) | collective-permute-done | bytes 155680 | tf_op jit(solution)/shard_map/ppermute | solution.py:40
  34.1 0.7 %shard_map.154 = (bf16[6,4096]{1,0:T(8,128)(2,1)}, bf16[6,8192]{1,0:T(8,128)(2,1)}) custom-call(s32[24]{0:T(128)S(4)} %get-tuple-element.59.plan, bf16[8,9728]{1,0:T(8,128)(2,1)S(1)} %collective-permute-done.11.final, f32[6,32,128]{2,1,0:T(8,128)S(1)} %get-tuple-element.61.placed), custom_call_target="tpu_custom_call" | custom-call | tf_op jit(solution)/shard_map/pallas_call | solution.py:520
  (28 shorter events, 0.2 us)
Async XLA Ops:
  0.6 13.5 %slice-start = ((s8[15728640]{0:T(1024)(128)(4,1)}), s8[4194304]{0:T(1024)(128)(4,1)S(1)}, s32[]{:S(2)}) async-start(s8[15728640]{0:T(1024)(128)(4,1)} %bitcast.13), calls=%async_computation | async-start | bytes 8388608
  0.6 11.9 %copy-start = (f32[1,6,16,8192]{3,2,1,0:T(8,128)S(1)}, f32[1,6,16,8192]{3,2,1,0:T(8,128)}, u32[]{:S(2)}) copy-start(f32[1,6,16,8192]{3,2,1,0:T(8,128)} %param.19) | copy-start | bytes 9437188
  0.7 13.5 %slice-start.1 = ((s8[15728640]{0:T(1024)(128)(4,1)}), s8[4194304]{0:T(1024)(128)(4,1)S(1)}, s32[]{:S(2)}) async-start(s8[15728640]{0:T(1024)(128)(4,1)} %bitcast.13), calls=%async_computation.1 | async-start | bytes 8388608
  0.7 13.5 %slice-start.2 = ((s8[15728640]{0:T(1024)(128)(4,1)}), s8[4194304]{0:T(1024)(128)(4,1)S(1)}, s32[]{:S(2)}) async-start(s8[15728640]{0:T(1024)(128)(4,1)} %bitcast.13), calls=%async_computation.2 | async-start | bytes 8388608
  0.7 13.5 %slice-start.3 = ((s8[15728640]{0:T(1024)(128)(4,1)}), s8[3145728]{0:T(1024)(128)(4,1)S(1)}, s32[]{:S(2)}) async-start(s8[15728640]{0:T(1024)(128)(4,1)} %bitcast.13), calls=%async_computation.3 | async-start | bytes 6291456
  2.4 11.5 %collective-permute-start.2 = (f32[32,6]{1,0:T(8,128)S(1)}, f32[32,6]{1,0:T(8,128)S(1)}, u32[]{:S(2)}, u32[]{:S(2)}) collective-permute-start(f32[32,6]{1,0:T(8,128)S(1)} %get-tuple-element.40.gains), channel_id=1, source_target_pairs={{0,1},{1,0},{2,3},{3,2},{4,5},{5,4},{6,7},{7,6},{8,9},{9,8},{10,11... | collective-permute-start | bytes 2312 | tf_op jit(solution)/shard_map/ppermute | solution.py:29
  6.0 8.1 %collective-permute-start = (bf16[16,384]{1,0:T(8,128)(2,1)S(1)}, bf16[16,384]{1,0:T(8,128)(2,1)S(1)}, u32[]{:S(2)}, u32[]{:S(2)}) collective-permute-start(bf16[16,384]{1,0:T(8,128)(2,1)S(1)} %get-tuple-element.38), channel_id=1, source_target_pairs={{0,8},{2,10},{4,12},{6,14},{8,0},{10,2},{12,4},{14,6},{16,24},{18,... | collective-permute-start | bytes 36872 | tf_op jit(solution)/shard_map/ppermute | solution.py:29
  8.9 5.2 %collective-permute-start.1 = (bf16[16,384]{1,0:T(8,128)(2,1)S(1)}, bf16[16,384]{1,0:T(8,128)(2,1)S(1)}, u32[]{:S(2)}, u32[]{:S(2)}) collective-permute-start(bf16[16,384]{1,0:T(8,128)(2,1)S(1)} %get-tuple-element.39), channel_id=1, source_target_pairs={{0,32},{2,34},{4,36},{6,38},{8,40},{10,42},{12,44},{14,46},{16,48}... | collective-permute-start | bytes 36872 | tf_op jit(solution)/shard_map/ppermute | solution.py:29
  12.6 6.6 %collective-permute-start.3 = (bf16[16,8576]{1,0:T(8,128)(2,1)S(1)}, bf16[16,8576]{1,0:T(8,128)(2,1)S(1)}, u32[]{:S(2)}, u32[]{:S(2)}) collective-permute-start(bf16[16,8576]{1,0:T(8,128)(2,1)S(1)} %get-tuple-element.46), channel_id=1, source_target_pairs={{0,4},{2,6},{4,0},{6,2},{8,12},{10,14},{12,8},{14,10},{16,20},{18,... | collective-permute-start | bytes 823304 | tf_op jit(solution)/shard_map/ppermute | solution.py:29
  13.1 6.5 %collective-permute-start.4 = (bf16[16,8576]{1,0:T(8,128)(2,1)S(1)}, bf16[16,8576]{1,0:T(8,128)(2,1)S(1)}, u32[]{:S(2)}, u32[]{:S(2)}) collective-permute-start(bf16[16,8576]{1,0:T(8,128)(2,1)S(1)} %get-tuple-element.47), channel_id=1, source_target_pairs={{0,16},{2,18},{4,20},{6,22},{8,24},{10,26},{12,28},{14,30},{16,0},... | collective-permute-start | bytes 823304 | tf_op jit(solution)/shard_map/ppermute | solution.py:29
  13.8 6.0 %collective-permute-start.5 = (bf16[16,8576]{1,0:T(8,128)(2,1)S(1)}, bf16[16,8576]{1,0:T(8,128)(2,1)S(1)}, u32[]{:S(2)}, u32[]{:S(2)}) collective-permute-start(bf16[16,8576]{1,0:T(8,128)(2,1)S(1)} %get-tuple-element.48), channel_id=1, source_target_pairs={{0,2},{2,0},{4,6},{6,4},{8,10},{10,8},{12,14},{14,12},{16,18},{18,... | collective-permute-start | bytes 823304 | tf_op jit(solution)/shard_map/ppermute | solution.py:29
  14.2 4.5 %copy-start.1 = (f32[1,16,8192]{2,1,0:T(8,128)S(1)}, f32[1,16,8192]{2,1,0:T(8,128)}, u32[]{:S(2)}) copy-start(f32[1,16,8192]{2,1,0:T(8,128)} %param.23) | copy-start | bytes 1572868
  14.2 4.5 %copy-start.2 = (bf16[1,6,8192]{2,1,0:T(8,128)(2,1)S(1)}, bf16[1,6,8192]{2,1,0:T(8,128)(2,1)}, u32[]{:S(2)}) copy-start(bf16[1,6,8192]{2,1,0:T(8,128)(2,1)} %param.20) | copy-start | bytes 294916
  14.2 4.5 %copy-start.3 = (bf16[1,6,8192]{2,1,0:T(8,128)(2,1)S(1)}, bf16[1,6,8192]{2,1,0:T(8,128)(2,1)}, u32[]{:S(2)}) copy-start(bf16[1,6,8192]{2,1,0:T(8,128)(2,1)} %param.21) | copy-start | bytes 294916
  14.2 4.4 %copy-start.4 = (f32[1,8192]{1,0:T(1,128)S(1)}, f32[1,8192]{1,0:T(1,128)}, u32[]{:S(2)}) copy-start(f32[1,8192]{1,0:T(1,128)} %bias.1) | copy-start | bytes 98308
  14.2 4.4 %copy-start.5 = (f32[1,8192]{1,0:T(1,128)S(1)}, f32[1,8192]{1,0:T(1,128)}, u32[]{:S(2)}) copy-start(f32[1,8192]{1,0:T(1,128)} %skip.1) | copy-start | bytes 98308
  16.1 12.7 %collective-permute-start.6 = (bf16[16,8448]{1,0:T(8,128)(2,1)S(1)}, bf16[16,8448]{1,0:T(8,128)(2,1)S(1)}, u32[]{:S(2)}, u32[]{:S(2)}) collective-permute-start(bf16[16,8448]{1,0:T(8,128)(2,1)S(1)} %get-tuple-element.52), channel_id=1, source_target_pairs={{0,8},{2,10},{4,12},{6,14},{8,0},{10,2},{12,4},{14,6},{16,24},{18,... | collective-permute-start | bytes 811016 | tf_op jit(solution)/shard_map/ppermute | solution.py:29
  17.7 11.1 %collective-permute-start.7 = (bf16[16,8448]{1,0:T(8,128)(2,1)S(1)}, bf16[16,8448]{1,0:T(8,128)(2,1)S(1)}, u32[]{:S(2)}, u32[]{:S(2)}) collective-permute-start(bf16[16,8448]{1,0:T(8,128)(2,1)S(1)} %get-tuple-element.53), channel_id=1, source_target_pairs={{0,32},{2,34},{4,36},{6,38},{8,40},{10,42},{12,44},{14,46},{16,48}... | collective-permute-start | bytes 811016 | tf_op jit(solution)/shard_map/ppermute | solution.py:29
  23.5 5.4 %collective-permute-start.8 = (bf16[32,128]{1,0:T(8,128)(2,1)S(1)}, bf16[32,128]{1,0:T(8,128)(2,1)S(1)}, u32[]{:S(2)}, u32[]{:S(2)}) collective-permute-start(bf16[32,128]{1,0:T(8,128)(2,1)S(1)} %get-tuple-element.54), channel_id=1, source_target_pairs={{0,68},{2,70},{4,64},{6,66},{8,76},{10,78},{12,72},{14,74},{16,84}... | collective-permute-start | bytes 24584 | tf_op jit(solution)/shard_map/ppermute | solution.py:40
  27.6 3.1 %collective-permute-start.9 = (bf16[32,128]{1,0:T(8,128)(2,1)S(1)}, bf16[32,128]{1,0:T(8,128)(2,1)S(1)}, u32[]{:S(2)}, u32[]{:S(2)}) collective-permute-start(bf16[32,128]{1,0:T(8,128)(2,1)S(1)} %get-tuple-element.55), channel_id=1, source_target_pairs={{0,80},{2,82},{4,84},{6,86},{8,88},{10,90},{12,92},{14,94},{16,64}... | collective-permute-start | bytes 24584 | tf_op jit(solution)/shard_map/ppermute | solution.py:40
  28.2 3.1 %collective-permute-start.10 = (bf16[32,128]{1,0:T(8,128)(2,1)S(1)}, bf16[32,128]{1,0:T(8,128)(2,1)S(1)}, u32[]{:S(2)}, u32[]{:S(2)}) collective-permute-start(bf16[32,128]{1,0:T(8,128)(2,1)S(1)} %get-tuple-element.56), channel_id=1, source_target_pairs={{0,66},{2,64},{4,70},{6,68},{8,74},{10,72},{12,78},{14,76},{16,82}... | collective-permute-start | bytes 24584 | tf_op jit(solution)/shard_map/ppermute | solution.py:40
  32.6 1.5 %collective-permute-start.11 = (bf16[8,9728]{1,0:T(8,128)(2,1)S(1)}, bf16[8,9728]{1,0:T(8,128)(2,1)S(1)}, u32[]{:S(2)}, u32[]{:S(2)}) collective-permute-start(bf16[8,9728]{1,0:T(8,128)(2,1)S(1)} %get-tuple-element.60), channel_id=1, source_target_pairs={{0,64},{2,66},{4,68},{6,70},{8,72},{10,74},{12,76},{14,78},{16,80}... | collective-permute-start | bytes 466952 | tf_op jit(solution)/shard_map/ppermute | solution.py:40

commit v4 on v3

--- a/solution.py
+++ b/solution.py
@@ -289,7 +289,9 @@
         out(attended)
 
 
-def rates_kernel(plan, conv, dt, a_log, bias, skip, rate, step_rows, drive_rows, direct):
+def rates_kernel(plan, conv, dt, a_log, bias, skip, later, rate, step_rows, drive_rows, direct):
+    for entry in range(24):
+        later[entry] = plan[entry]
     mixer = conv[...].astype(f32)
     step_in = dt[...].astype(f32) + bias[...]
     step = jnp.maximum(step_in, 0.0) + jnp.log1p(jnp.exp(-jnp.abs(step_in)))
@@ -306,9 +308,9 @@
     rows = pltpu.VMEM((slots, 1, width), f32)
     return pl.pallas_call(
         rates_kernel,
-        out_shape=(pltpu.VMEM(a_log.shape, f32), rows, rows, pltpu.VMEM((slots, width), f32)),
+        out_shape=(pltpu.SMEM(plan.shape, jnp.int32), pltpu.VMEM(a_log.shape, f32), rows, rows, pltpu.VMEM((slots, width), f32)),
         in_specs=[whole(pltpu.SMEM)] + [whole(pltpu.VMEM)] * 5,
-        out_specs=(whole(pltpu.VMEM),) * 4,
+        out_specs=(whole(pltpu.SMEM),) + (whole(pltpu.VMEM),) * 4,
         compiler_params=pltpu.CompilerParams(vmem_limit_bytes=8 * 2**20),
         cost_estimate=pl.CostEstimate(
             flops=10 * slots * width,
@@ -389,18 +391,9 @@
     )(plan, table, *in_vmem(pool, held, heads, *queries, gains, gains_far))
 
 
-def near_kernel(
-    plan, table, pool, gains, rate, step_rows, drive_rows, held, x0, x1, x2,
-    later, new_state, mixed_rows, a0, a1, a2,
-    out_buf, sems,
-):
+def near_kernel(plan, table, pool, x0, x1, x2, later, a0, a1, a2):
     for entry in range(24):
         later[entry] = plan[entry]
-    extras = [x0, x1, x2]
-    copies = update_items(
-        (BITS,) + NEAR, plan, gains, rate, step_rows, drive_rows, held, [None] + extras,
-        new_state, mixed_rows, out_buf, sems,
-    )
 
     def into(out):
         def put(attended):
@@ -408,41 +401,29 @@
 
         return put
 
-    attend_items(NEAR, plan, table, pool, extras, [into(a0), into(a1), into(a2)])
-    for copy in copies:
-        copy.wait()
-
-
-def near(plan, table, pool, gains, made, held, extras):
-    slots, n, width = held.shape
-    count = 1 + len(NEAR)
-    inputs = in_vmem(pool, gains, *made[:3], held, *extras)
+    attend_items(NEAR, plan, table, pool, [x0, x1, x2], [into(a0), into(a1), into(a2)])
+
+
+def near(plan, table, pool, extras):
+    result = pltpu.VMEM((2 * extras[0].shape[0], HD), bf16)
     return pl.pallas_call(
         near_kernel,
-        out_shape=(
-            pltpu.SMEM(plan.shape, jnp.int32),
-            pltpu.HBM(held.shape, f32),
-            pltpu.VMEM((slots, 1, width), f32),
-        )
-        + (pltpu.VMEM((2 * n, HD), bf16),) * len(NEAR),
-        in_specs=[whole(pltpu.SMEM)] * 2 + [whole(pltpu.VMEM)] * len(inputs),
-        out_specs=(whole(pltpu.SMEM), whole(pl.ANY)) + (whole(pltpu.VMEM),) * (1 + len(NEAR)),
-        scratch_shapes=[pltpu.VMEM((count, n, width), f32), pltpu.SemaphoreType.DMA((count,))],
+        out_shape=(pltpu.SMEM(plan.shape, jnp.int32),) + (result,) * len(NEAR),
+        in_specs=[whole(pltpu.SMEM)] * 2 + [whole(pltpu.VMEM)] * (1 + len(NEAR)),
+        out_specs=(whole(pltpu.SMEM),) + (whole(pltpu.VMEM),) * len(NEAR),
         compiler_params=pltpu.CompilerParams(vmem_limit_bytes=8 * 2**20),
         cost_estimate=pl.CostEstimate(**attention_cost(len(NEAR))),
-    )(plan, table, *inputs)
+    )(plan, table, *in_vmem(pool, *extras))
 
 
 def last_kernel(
-    plan, gains, rate, step_rows, drive_rows, direct, own, x0, x1, b0, b1, b2, state_before, rows_before,
-    later, new_state, mixed_rows, final, placed,
-    mixed_all, out_buf, sems,
+    plan, gains, rate, step_rows, drive_rows, direct, own, held, x0, x1, x2, x3, x4, b0, b1, b2,
+    new_state, final, placed,
+    mixed_rows, mixed_all, out_buf, sems,
 ):
-    for entry in range(24):
-        later[entry] = plan[entry]
     slots, width = direct.shape
     copies = update_items(
-        FAR, plan, gains, rate, step_rows, drive_rows, None, [x0, x1],
+        (BITS,) + NEAR + FAR, plan, gains, rate, step_rows, drive_rows, held, [None, x0, x1, x2, x3, x4],
         new_state, mixed_rows, out_buf, sems,
     )
     mixed_all[...] = jnp.zeros_like(mixed_all)
@@ -450,7 +431,7 @@
         mixed_all[slot : slot + 1, :] = mixed_rows[slot] + direct[slot : slot + 1, :]
     final[:, :width] = mixed_all[...].astype(bf16)
     results = [own[...].astype(f32)]
-    for row in (x0, x1):
+    for row in (x3, x4):
         results.append(
             jnp.concatenate([row[:, width : width + HD], row[:, width + HD :]], axis=0).astype(f32)
         )
@@ -464,31 +445,28 @@
         copy.wait()
 
 
-def last(plan, gains, made, own, extras, backs, new_state, mixed_rows):
-    slots, width = made[3].shape
-    n = made[0].shape[0]
-    inputs = in_vmem(gains, *made, own, *extras, *backs) + in_hbm(new_state) + in_vmem(mixed_rows)
+def last(plan, gains, made, own, held, extras, backs):
+    slots, n, width = held.shape
+    inputs = in_vmem(gains, *made, own, held, *extras, *backs)
     vmem = whole(pltpu.VMEM)
     return pl.pallas_call(
         last_kernel,
         out_shape=(
-            pltpu.SMEM(plan.shape, jnp.int32),
-            pltpu.HBM(new_state.shape, f32),
-            pltpu.VMEM(mixed_rows.shape, f32),
+            pltpu.HBM(held.shape, f32),
             pltpu.VMEM((8, width + 12 * HD), bf16),
             pltpu.VMEM((slots, 2 * n, HD), f32),
         ),
-        in_specs=[whole(pltpu.SMEM)] + [vmem] * (len(inputs) - 2) + [whole(pl.ANY), vmem],
-        out_specs=(whole(pltpu.SMEM), whole(pl.ANY), vmem, vmem, vmem),
+        in_specs=[whole(pltpu.SMEM)] + [vmem] * len(inputs),
+        out_specs=(whole(pl.ANY), vmem, vmem),
         scratch_shapes=[
+            pltpu.VMEM((slots, 1, width), f32),
             pltpu.VMEM((8, width), f32),
-            pltpu.VMEM((len(FAR), n, width), f32),
-            pltpu.SemaphoreType.DMA((len(FAR),)),
+            pltpu.VMEM((slots, n, width), f32),
+            pltpu.SemaphoreType.DMA((slots,)),
         ],
-        input_output_aliases={len(inputs) - 1: 1, len(inputs): 2},
         compiler_params=pltpu.CompilerParams(vmem_limit_bytes=8 * 2**20),
         cost_estimate=pl.CostEstimate(
-            flops=16 * n * width, transcendentals=2 * n * width, bytes_accessed=12 * n * width
+            flops=8 * held.size, transcendentals=held.size, bytes_accessed=6 * held.size
         ),
     )(plan, *inputs)
 
@@ -559,12 +537,10 @@
     rows_near = [swapped(value, "replica", bit) for bit, value in zip(NEAR, rows)]
     plan, gains, own, *rows = first(plan, table, pool, held, heads, gains, gains_far, queries_far)
     rows_far = [swapped(value, "replica", bit) for bit, value in zip(FAR, rows)]
-    made = rates(plan, conv_out[0], dt_raw[0], a_log[0], dt_bias, skip_gain)
-    plan, new_state, mixed_rows, *attended = near(plan, table, pool, gains, made, held, rows_near)
+    plan, *made = rates(plan, conv_out[0], dt_raw[0], a_log[0], dt_bias, skip_gain)
+    plan, *attended = near(plan, table, pool, rows_near)
     backs = [across(value, bit) for bit, value in zip(NEAR, attended)]
-    plan, new_state, _, final, placed = last(
-        plan, gains, made, own, rows_far, backs, new_state, mixed_rows
-    )
+    new_state, final, placed = last(plan, gains, made, own, held, rows_near + rows_far, backs)
     handed_attention, handed_mamba = place(plan, across(final, BITS), placed)
     return handed_mamba[None], handed_attention[None], new_state[None]
 

time: 34.9 us -> 34 us (0.974)
  Pallas kernels: 9.63 us -> 8.78 us
    pallas_call x1, Pallas kernels: 3.68 us -> 1.83 us  [near(): pl.pallas_call(near_kernel, out_shape=(pltpu.SMEM(plan.shape, jnp.int32),...]
    pallas_call x2, Pallas kernels: 1.58 us -> 2.59 us  [the longest x1 2.24 us: last(): pl.pallas_call(last_kernel, out_shape=(pltpu.HBM(held.shape, f32), pltpu....]
  transfers between devices with their start and end apart: 12 -> 12, of which waited for: 6 -> 7; matrix products, arithmetic and copies ran while one was open for 0% -> 0% of each run, Pallas kernels for 17% -> 12%
where the time goes in v4:
time: 34 us; the launch traced here: 33.9 us
  starting transfers between devices  20 us (59%)
  Pallas kernels  8.78 us (26%)
  waiting for transfers between devices  4.3 us (13%)
  between operations  0.8 us (2%)
    ppermute x8, starting transfers between devices, swapped(): return lax.ppermute(value, axis, pairs)  14.2 us
    ppermute x4, starting transfers between devices, across(): return lax.ppermute(value, ('section', 'replica'), pairs)  5.75 us
    ppermute x4, waiting for transfers between devices, across(): return lax.ppermute(value, ('section', 'replica'), pairs)  3.49 us
    pallas_call x1, Pallas kernels, last(): pl.pallas_call(last_kernel, out_shape=(pltpu.HBM(held.shape, f32), pltpu....  2.24 us
    pallas_call x1, Pallas kernels, first(): pl.pallas_call(first_kernel, out_shape=(pltpu.SMEM(plan.shape, jnp.int32)...  1.85 us
    pallas_call x1, Pallas kernels, near(): pl.pallas_call(near_kernel, out_shape=(pltpu.SMEM(plan.shape, jnp.int32),...  1.83 us
    pallas_call x1, Pallas kernels, load(): pl.pallas_call(load_kernel, out_shape=(pltpu.SMEM((24,), jnp.int32), pltp...  1.68 us
    ppermute x8, waiting for transfers between devices, swapped(): return lax.ppermute(value, axis, pairs)  0.81 us
  transfers between devices with their start and end apart: 12, of which 7 were waited for; matrix products, arithmetic and copies ran while one was open for 0% of the time, Pallas kernels for 12%

profile of v4, /device:TPU:1, one launch (start us, length us, event | category | flops | bytes accessed | tf_op | source)
XLA Modules:
  0.0 33.9 jit_solution(5443448118145486309)
XLA Ops:
  0.7 1.7 %shard_map.148 = (s32[24]{0:T(128)S(4)}, s32[6,80]{1,0:T(8,128)S(4)}, f32[32,6]{1,0:T(8,128)S(1)}, bf16[6,16,384]{2,1,0:T(8,128)(2,1)S(1)}, bf16[16,384]{1,0:T(8,128)(2,1)S(1)}, /*index=5*/bf16[16,384]{1,0:T(8,128)(2,1)S(1)}) custom-call(s32[192]{0:T(256)} %src_in.1, s32[192]{0:T(256)} %lens_in.1, s32[6,80]{1,0:T(8,128)} %table_in.1, ...), custom_call_target="tpu_custom_call" | custom-call | flops 10000000000 | bytes 49152 | tf_op jit(solution)/shard_map/pallas_call | solution.py:136
  2.4 3.7 %collective-permute-start.2 = (f32[32,6]{1,0:T(8,128)S(1)}, f32[32,6]{1,0:T(8,128)S(1)}, u32[]{:S(2)}, u32[]{:S(2)}) collective-permute-start(f32[32,6]{1,0:T(8,128)S(1)} %get-tuple-element.38.gains), channel_id=1, source_target_pairs={{0,1},{1,0},{2,3},{3,2},{4,5},{5,4},{6,7},{7,6},{8,9},{9,8},{10,11... | collective-permute-start | bytes 2312 | tf_op jit(solution)/shard_map/ppermute | solution.py:29
  6.0 2.9 %collective-permute-start = (bf16[16,384]{1,0:T(8,128)(2,1)S(1)}, bf16[16,384]{1,0:T(8,128)(2,1)S(1)}, u32[]{:S(2)}, u32[]{:S(2)}) collective-permute-start(bf16[16,384]{1,0:T(8,128)(2,1)S(1)} %get-tuple-element.36), channel_id=1, source_target_pairs={{0,8},{2,10},{4,12},{6,14},{8,0},{10,2},{12,4},{14,6},{16,24},{18,... | collective-permute-start | bytes 36872 | tf_op jit(solution)/shard_map/ppermute | solution.py:29
  8.9 3.6 %collective-permute-start.1 = (bf16[16,384]{1,0:T(8,128)(2,1)S(1)}, bf16[16,384]{1,0:T(8,128)(2,1)S(1)}, u32[]{:S(2)}, u32[]{:S(2)}) collective-permute-start(bf16[16,384]{1,0:T(8,128)(2,1)S(1)} %get-tuple-element.37), channel_id=1, source_target_pairs={{0,32},{2,34},{4,36},{6,38},{8,40},{10,42},{12,44},{14,46},{16,48}... | collective-permute-start | bytes 36872 | tf_op jit(solution)/shard_map/ppermute | solution.py:29
  12.6 0.5 %collective-permute-start.3 = (bf16[16,8576]{1,0:T(8,128)(2,1)S(1)}, bf16[16,8576]{1,0:T(8,128)(2,1)S(1)}, u32[]{:S(2)}, u32[]{:S(2)}) collective-permute-start(bf16[16,8576]{1,0:T(8,128)(2,1)S(1)} %get-tuple-element.41), channel_id=1, source_target_pairs={{0,4},{2,6},{4,0},{6,2},{8,12},{10,14},{12,8},{14,10},{16,20},{18,... | collective-permute-start | bytes 823304 | tf_op jit(solution)/shard_map/ppermute | solution.py:29
  13.1 0.8 %collective-permute-start.4 = (bf16[16,8576]{1,0:T(8,128)(2,1)S(1)}, bf16[16,8576]{1,0:T(8,128)(2,1)S(1)}, u32[]{:S(2)}, u32[]{:S(2)}) collective-permute-start(bf16[16,8576]{1,0:T(8,128)(2,1)S(1)} %get-tuple-element.42), channel_id=1, source_target_pairs={{0,16},{2,18},{4,20},{6,22},{8,24},{10,26},{12,28},{14,30},{16,0},... | collective-permute-start | bytes 823304 | tf_op jit(solution)/shard_map/ppermute | solution.py:29
  13.8 0.3 collective-permute-start.5
  14.3 1.9 %shard_map.150 = (s32[24]{0:T(128)S(4)}, f32[32,6]{1,0:T(8,128)S(1)}, bf16[32,128]{1,0:T(8,128)(2,1)S(1)}, bf16[16,8448]{1,0:T(8,128)(2,1)S(1)}, bf16[16,8448]{1,0:T(8,128)(2,1)S(1)}) custom-call(s32[24]{0:T(128)S(4)} %get-tuple-element.34.plan, s32[6,80]{1,0:T(8,128)S(4)} %get-tuple-element.35.table, bf16[2,480,16,512]{3,2,1,0:T(8,128)(2,1)S(1)} %bitcast.15, ...), custom_call_target="tpu_custom_call" | custom-call | flops 251658240 | bytes 7864320 | tf_op jit(solution)/shard_map/pallas_call | solution.py:383
  16.1 1.6 %collective-permute-start.6 = (bf16[16,8448]{1,0:T(8,128)(2,1)S(1)}, bf16[16,8448]{1,0:T(8,128)(2,1)S(1)}, u32[]{:S(2)}, u32[]{:S(2)}) collective-permute-start(bf16[16,8448]{1,0:T(8,128)(2,1)S(1)} %get-tuple-element.51), channel_id=1, source_target_pairs={{0,8},{2,10},{4,12},{6,14},{8,0},{10,2},{12,4},{14,6},{16,24},{18,... | collective-permute-start | bytes 811016 | tf_op jit(solution)/shard_map/ppermute | solution.py:29
  17.7 0.9 %collective-permute-start.7 = (bf16[16,8448]{1,0:T(8,128)(2,1)S(1)}, bf16[16,8448]{1,0:T(8,128)(2,1)S(1)}, u32[]{:S(2)}, u32[]{:S(2)}) collective-permute-start(bf16[16,8448]{1,0:T(8,128)(2,1)S(1)} %get-tuple-element.52), channel_id=1, source_target_pairs={{0,32},{2,34},{4,36},{6,38},{8,40},{10,42},{12,44},{14,46},{16,48}... | collective-permute-start | bytes 811016 | tf_op jit(solution)/shard_map/ppermute | solution.py:29
  18.7 0.3 %shard_map.151 = (s32[24]{0:T(128)S(4)}, f32[16,8192]{1,0:T(8,128)S(1)}, f32[6,1,8192]{2,1,0:T(1,128)S(1)}, f32[6,1,8192]{2,1,0:T(1,128)S(1)}, f32[6,8192]{1,0:T(8,128)S(1)}) custom-call(s32[24]{0:T(128)S(4)} %get-tuple-element.39.plan, bf16[6,8192]{1,0:T(8,128)(2,1)S(1)} %bitcast.22, bf16[6,8192]{1,0:T(8,128)(2,1)S(1)} %bitcast.23, ...), custom_call_target="tpu_custom_call" | custom-call | flops 491520 | bytes 524288 | tf_op jit(solution)/shard_map/pallas_call | solution.py:309
  19.2 0.4 %collective-permute-done.4.x1 = bf16[16,8576]{1,0:T(8,128)(2,1)S(1)} collective-permute-done((bf16[16,8576]{1,0:T(8,128)(2,1)S(1)}, bf16[16,8576]{1,0:T(8,128)(2,1)S(1)}, u32[]{:S(2)}, u32[]{:S(2)}) %collective-permute-start.4) | collective-permute-done | bytes 274464 | tf_op jit(solution)/shard_map/ppermute | solution.py:29
  19.6 0.2 collective-permute-done.5.x2
  19.8 1.8 %shard_map.152 = (s32[24]{0:T(128)S(4)}, bf16[32,128]{1,0:T(8,128)(2,1)S(1)}, bf16[32,128]{1,0:T(8,128)(2,1)S(1)}, bf16[32,128]{1,0:T(8,128)(2,1)S(1)}) custom-call(s32[24]{0:T(128)S(4)} %get-tuple-element.40.plan, s32[6,80]{1,0:T(8,128)S(4)} %get-tuple-element.35.table, bf16[2,480,16,512]{3,2,1,0:T(8,128)(2,1)S(1)} %bitcast.16, ...), custom_call_target="tpu_custom_call" | custom-call | flops 251658240 | bytes 7864320 | tf_op jit(solution)/shard_map/pallas_call | solution.py:409
  21.7 4.0 %collective-permute-start.8 = (bf16[32,128]{1,0:T(8,128)(2,1)S(1)}, bf16[32,128]{1,0:T(8,128)(2,1)S(1)}, u32[]{:S(2)}, u32[]{:S(2)}) collective-permute-start(bf16[32,128]{1,0:T(8,128)(2,1)S(1)} %get-tuple-element.53), channel_id=1, source_target_pairs={{0,68},{2,70},{4,64},{6,66},{8,76},{10,78},{12,72},{14,74},{16,84}... | collective-permute-start | bytes 24584 | tf_op jit(solution)/shard_map/ppermute | solution.py:40
  25.7 0.6 %collective-permute-start.9 = (bf16[32,128]{1,0:T(8,128)(2,1)S(1)}, bf16[32,128]{1,0:T(8,128)(2,1)S(1)}, u32[]{:S(2)}, u32[]{:S(2)}) collective-permute-start(bf16[32,128]{1,0:T(8,128)(2,1)S(1)} %get-tuple-element.54), channel_id=1, source_target_pairs={{0,80},{2,82},{4,84},{6,86},{8,88},{10,90},{12,92},{14,94},{16,64}... | collective-permute-start | bytes 24584 | tf_op jit(solution)/shard_map/ppermute | solution.py:40
  26.3 0.6 %collective-permute-start.10 = (bf16[32,128]{1,0:T(8,128)(2,1)S(1)}, bf16[32,128]{1,0:T(8,128)(2,1)S(1)}, u32[]{:S(2)}, u32[]{:S(2)}) collective-permute-start(bf16[32,128]{1,0:T(8,128)(2,1)S(1)} %get-tuple-element.55), channel_id=1, source_target_pairs={{0,66},{2,64},{4,70},{6,68},{8,74},{10,72},{12,78},{14,76},{16,82}... | collective-permute-start | bytes 24584 | tf_op jit(solution)/shard_map/ppermute | solution.py:40
  27.0 0.3 collective-permute-done.8.b0
  27.3 1.4 %collective-permute-done.9.b1 = bf16[32,128]{1,0:T(8,128)(2,1)S(1)} collective-permute-done((bf16[32,128]{1,0:T(8,128)(2,1)S(1)}, bf16[32,128]{1,0:T(8,128)(2,1)S(1)}, u32[]{:S(2)}, u32[]{:S(2)}) %collective-permute-start.9) | collective-permute-done | bytes 8224 | tf_op jit(solution)/shard_map/ppermute | solution.py:40
  28.7 0.7 %collective-permute-done.10.b2 = bf16[32,128]{1,0:T(8,128)(2,1)S(1)} collective-permute-done((bf16[32,128]{1,0:T(8,128)(2,1)S(1)}, bf16[32,128]{1,0:T(8,128)(2,1)S(1)}, u32[]{:S(2)}, u32[]{:S(2)}) %collective-permute-start.10) | collective-permute-done | bytes 8224 | tf_op jit(solution)/shard_map/ppermute | solution.py:40
  29.4 2.2 %shard_map.153 = (f32[6,16,8192]{2,1,0:T(8,128)}, bf16[8,9728]{1,0:T(8,128)(2,1)S(1)}, f32[6,32,128]{2,1,0:T(8,128)S(1)}) custom-call(s32[24]{0:T(128)S(4)} %get-tuple-element.44.plan, f32[32,6]{1,0:T(8,128)S(1)} %get-tuple-element.45.gains, f32[16,8192]{1,0:T(8,128)S(1)} %get-tuple-element.46.rate, f32[6,1,8192]{2,1,0:T(1,128)S(1)} %get-tuple-element.47.step_rows, ...), custom_call_target="tpu_custom_call" | custom-call | flops 6291456 | bytes 4718592 | tf_op jit(solution)/shard_map/pallas_call | solution.py:452
  31.7 0.5 %collective-permute-start.11 = (bf16[8,9728]{1,0:T(8,128)(2,1)S(1)}, bf16[8,9728]{1,0:T(8,128)(2,1)S(1)}, u32[]{:S(2)}, u32[]{:S(2)}) collective-permute-start(bf16[8,9728]{1,0:T(8,128)(2,1)S(1)} %get-tuple-element.56), channel_id=1, source_target_pairs={{0,64},{2,66},{4,68},{6,70},{8,72},{10,74},{12,76},{14,78},{16,80}... | collective-permute-start | bytes 466952 | tf_op jit(solution)/shard_map/ppermute | solution.py:40
  32.2 1.0 %collective-permute-done.11.final = bf16[8,9728]{1,0:T(8,128)(2,1)S(1)} collective-permute-done((bf16[8,9728]{1,0:T(8,128)(2,1)S(1)}, bf16[8,9728]{1,0:T(8,128)(2,1)S(1)}, u32[]{:S(2)}, u32[]{:S(2)}) %collective-permute-start.11) | collective-permute-done | bytes 155680 | tf_op jit(solution)/shard_map/ppermute | solution.py:40
  33.2 0.7 %shard_map.154 = (bf16[6,4096]{1,0:T(8,128)(2,1)}, bf16[6,8192]{1,0:T(8,128)(2,1)}) custom-call(s32[24]{0:T(128)S(4)} %get-tuple-element.44.plan, bf16[8,9728]{1,0:T(8,128)(2,1)S(1)} %collective-permute-done.11.final, f32[6,32,128]{2,1,0:T(8,128)S(1)} %get-tuple-element.57.placed), custom_call_target="tpu_custom_call" | custom-call | tf_op jit(solution)/shard_map/pallas_call | solution.py:498
  (28 shorter events, 0.3 us)
Async XLA Ops:
  0.6 13.5 %slice-start = ((s8[15728640]{0:T(1024)(128)(4,1)}), s8[4194304]{0:T(1024)(128)(4,1)S(1)}, s32[]{:S(2)}) async-start(s8[15728640]{0:T(1024)(128)(4,1)} %bitcast.13), calls=%async_computation | async-start | bytes 8388608
  0.6 11.9 %copy-start = (f32[1,6,16,8192]{3,2,1,0:T(8,128)S(1)}, f32[1,6,16,8192]{3,2,1,0:T(8,128)}, u32[]{:S(2)}) copy-start(f32[1,6,16,8192]{3,2,1,0:T(8,128)} %param.19) | copy-start | bytes 9437188
  0.7 13.5 %slice-start.1 = ((s8[15728640]{0:T(1024)(128)(4,1)}), s8[4194304]{0:T(1024)(128)(4,1)S(1)}, s32[]{:S(2)}) async-start(s8[15728640]{0:T(1024)(128)(4,1)} %bitcast.13), calls=%async_computation.1 | async-start | bytes 8388608
  0.7 13.5 %slice-start.2 = ((s8[15728640]{0:T(1024)(128)(4,1)}), s8[4194304]{0:T(1024)(128)(4,1)S(1)}, s32[]{:S(2)}) async-start(s8[15728640]{0:T(1024)(128)(4,1)} %bitcast.13), calls=%async_computation.2 | async-start | bytes 8388608
  0.7 13.5 %slice-start.3 = ((s8[15728640]{0:T(1024)(128)(4,1)}), s8[3145728]{0:T(1024)(128)(4,1)S(1)}, s32[]{:S(2)}) async-start(s8[15728640]{0:T(1024)(128)(4,1)} %bitcast.13), calls=%async_computation.3 | async-start | bytes 6291456
  2.4 11.5 %collective-permute-start.2 = (f32[32,6]{1,0:T(8,128)S(1)}, f32[32,6]{1,0:T(8,128)S(1)}, u32[]{:S(2)}, u32[]{:S(2)}) collective-permute-start(f32[32,6]{1,0:T(8,128)S(1)} %get-tuple-element.38.gains), channel_id=1, source_target_pairs={{0,1},{1,0},{2,3},{3,2},{4,5},{5,4},{6,7},{7,6},{8,9},{9,8},{10,11... | collective-permute-start | bytes 2312 | tf_op jit(solution)/shard_map/ppermute | solution.py:29
  6.0 8.1 %collective-permute-start = (bf16[16,384]{1,0:T(8,128)(2,1)S(1)}, bf16[16,384]{1,0:T(8,128)(2,1)S(1)}, u32[]{:S(2)}, u32[]{:S(2)}) collective-permute-start(bf16[16,384]{1,0:T(8,128)(2,1)S(1)} %get-tuple-element.36), channel_id=1, source_target_pairs={{0,8},{2,10},{4,12},{6,14},{8,0},{10,2},{12,4},{14,6},{16,24},{18,... | collective-permute-start | bytes 36872 | tf_op jit(solution)/shard_map/ppermute | solution.py:29
  8.9 5.2 %collective-permute-start.1 = (bf16[16,384]{1,0:T(8,128)(2,1)S(1)}, bf16[16,384]{1,0:T(8,128)(2,1)S(1)}, u32[]{:S(2)}, u32[]{:S(2)}) collective-permute-start(bf16[16,384]{1,0:T(8,128)(2,1)S(1)} %get-tuple-element.37), channel_id=1, source_target_pairs={{0,32},{2,34},{4,36},{6,38},{8,40},{10,42},{12,44},{14,46},{16,48}... | collective-permute-start | bytes 36872 | tf_op jit(solution)/shard_map/ppermute | solution.py:29
  12.6 6.6 %collective-permute-start.3 = (bf16[16,8576]{1,0:T(8,128)(2,1)S(1)}, bf16[16,8576]{1,0:T(8,128)(2,1)S(1)}, u32[]{:S(2)}, u32[]{:S(2)}) collective-permute-start(bf16[16,8576]{1,0:T(8,128)(2,1)S(1)} %get-tuple-element.41), channel_id=1, source_target_pairs={{0,4},{2,6},{4,0},{6,2},{8,12},{10,14},{12,8},{14,10},{16,20},{18,... | collective-permute-start | bytes 823304 | tf_op jit(solution)/shard_map/ppermute | solution.py:29
  13.1 6.5 %collective-permute-start.4 = (bf16[16,8576]{1,0:T(8,128)(2,1)S(1)}, bf16[16,8576]{1,0:T(8,128)(2,1)S(1)}, u32[]{:S(2)}, u32[]{:S(2)}) collective-permute-start(bf16[16,8576]{1,0:T(8,128)(2,1)S(1)} %get-tuple-element.42), channel_id=1, source_target_pairs={{0,16},{2,18},{4,20},{6,22},{8,24},{10,26},{12,28},{14,30},{16,0},... | collective-permute-start | bytes 823304 | tf_op jit(solution)/shard_map/ppermute | solution.py:29
  13.8 6.0 %collective-permute-start.5 = (bf16[16,8576]{1,0:T(8,128)(2,1)S(1)}, bf16[16,8576]{1,0:T(8,128)(2,1)S(1)}, u32[]{:S(2)}, u32[]{:S(2)}) collective-permute-start(bf16[16,8576]{1,0:T(8,128)(2,1)S(1)} %get-tuple-element.43), channel_id=1, source_target_pairs={{0,2},{2,0},{4,6},{6,4},{8,10},{10,8},{12,14},{14,12},{16,18},{18,... | collective-permute-start | bytes 823304 | tf_op jit(solution)/shard_map/ppermute | solution.py:29
  14.2 4.5 %copy-start.1 = (f32[1,16,8192]{2,1,0:T(8,128)S(1)}, f32[1,16,8192]{2,1,0:T(8,128)}, u32[]{:S(2)}) copy-start(f32[1,16,8192]{2,1,0:T(8,128)} %param.23) | copy-start | bytes 1572868
  14.2 4.5 %copy-start.2 = (bf16[1,6,8192]{2,1,0:T(8,128)(2,1)S(1)}, bf16[1,6,8192]{2,1,0:T(8,128)(2,1)}, u32[]{:S(2)}) copy-start(bf16[1,6,8192]{2,1,0:T(8,128)(2,1)} %param.20) | copy-start | bytes 294916
  14.2 4.4 %copy-start.3 = (bf16[1,6,8192]{2,1,0:T(8,128)(2,1)S(1)}, bf16[1,6,8192]{2,1,0:T(8,128)(2,1)}, u32[]{:S(2)}) copy-start(bf16[1,6,8192]{2,1,0:T(8,128)(2,1)} %param.21) | copy-start | bytes 294916
  14.2 4.4 %copy-start.4 = (f32[1,8192]{1,0:T(1,128)S(1)}, f32[1,8192]{1,0:T(1,128)}, u32[]{:S(2)}) copy-start(f32[1,8192]{1,0:T(1,128)} %bias.1) | copy-start | bytes 98308
  14.2 4.4 %copy-start.5 = (f32[1,8192]{1,0:T(1,128)S(1)}, f32[1,8192]{1,0:T(1,128)}, u32[]{:S(2)}) copy-start(f32[1,8192]{1,0:T(1,128)} %skip.1) | copy-start | bytes 98308
  16.1 10.8 %collective-permute-start.6 = (bf16[16,8448]{1,0:T(8,128)(2,1)S(1)}, bf16[16,8448]{1,0:T(8,128)(2,1)S(1)}, u32[]{:S(2)}, u32[]{:S(2)}) collective-permute-start(bf16[16,8448]{1,0:T(8,128)(2,1)S(1)} %get-tuple-element.51), channel_id=1, source_target_pairs={{0,8},{2,10},{4,12},{6,14},{8,0},{10,2},{12,4},{14,6},{16,24},{18,... | collective-permute-start | bytes 811016 | tf_op jit(solution)/shard_map/ppermute | solution.py:29
  17.7 9.2 %collective-permute-start.7 = (bf16[16,8448]{1,0:T(8,128)(2,1)S(1)}, bf16[16,8448]{1,0:T(8,128)(2,1)S(1)}, u32[]{:S(2)}, u32[]{:S(2)}) collective-permute-start(bf16[16,8448]{1,0:T(8,128)(2,1)S(1)} %get-tuple-element.52), channel_id=1, source_target_pairs={{0,32},{2,34},{4,36},{6,38},{8,40},{10,42},{12,44},{14,46},{16,48}... | collective-permute-start | bytes 811016 | tf_op jit(solution)/shard_map/ppermute | solution.py:29
  21.7 5.6 %collective-permute-start.8 = (bf16[32,128]{1,0:T(8,128)(2,1)S(1)}, bf16[32,128]{1,0:T(8,128)(2,1)S(1)}, u32[]{:S(2)}, u32[]{:S(2)}) collective-permute-start(bf16[32,128]{1,0:T(8,128)(2,1)S(1)} %get-tuple-element.53), channel_id=1, source_target_pairs={{0,68},{2,70},{4,64},{6,66},{8,76},{10,78},{12,72},{14,74},{16,84}... | collective-permute-start | bytes 24584 | tf_op jit(solution)/shard_map/ppermute | solution.py:40
  25.7 3.1 %collective-permute-start.9 = (bf16[32,128]{1,0:T(8,128)(2,1)S(1)}, bf16[32,128]{1,0:T(8,128)(2,1)S(1)}, u32[]{:S(2)}, u32[]{:S(2)}) collective-permute-start(bf16[32,128]{1,0:T(8,128)(2,1)S(1)} %get-tuple-element.54), channel_id=1, source_target_pairs={{0,80},{2,82},{4,84},{6,86},{8,88},{10,90},{12,92},{14,94},{16,64}... | collective-permute-start | bytes 24584 | tf_op jit(solution)/shard_map/ppermute | solution.py:40
  26.3 3.1 %collective-permute-start.10 = (bf16[32,128]{1,0:T(8,128)(2,1)S(1)}, bf16[32,128]{1,0:T(8,128)(2,1)S(1)}, u32[]{:S(2)}, u32[]{:S(2)}) collective-permute-start(bf16[32,128]{1,0:T(8,128)(2,1)S(1)} %get-tuple-element.55), channel_id=1, source_target_pairs={{0,66},{2,64},{4,70},{6,68},{8,74},{10,72},{12,78},{14,76},{16,82}... | collective-permute-start | bytes 24584 | tf_op jit(solution)/shard_map/ppermute | solution.py:40
  31.7 1.5 %collective-permute-start.11 = (bf16[8,9728]{1,0:T(8,128)(2,1)S(1)}, bf16[8,9728]{1,0:T(8,128)(2,1)S(1)}, u32[]{:S(2)}, u32[]{:S(2)}) collective-permute-start(bf16[8,9728]{1,0:T(8,128)(2,1)S(1)} %get-tuple-element.56), channel_id=1, source_target_pairs={{0,64},{2,66},{4,68},{6,70},{8,72},{10,74},{12,76},{14,78},{16,80}... | collective-permute-start | bytes 466952 | tf_op jit(solution)/shard_map/ppermute | solution.py:40

commit v5 on v4

--- a/solution.py
+++ b/solution.py
@@ -14,7 +14,7 @@
 FAR = (2, 4)
 NEAR = (1, 3, 0)
 FIRST = (BITS,) + FAR
-BLOCK = 256
+BLOCK = 640
 LOG2E = 1.4426950408889634
 WEIGHT = 10**10
 

time: 34 us -> 33.9 us (level)
  Pallas kernels: 8.78 us -> 8.43 us
  transfers between devices with their start and end apart: 12 -> 12, of which waited for: 7 -> 7; matrix products, arithmetic and copies ran while one was open for 0% -> 0% of each run, Pallas kernels for 12% -> 11%
where the time goes in v5:
time: 33.9 us; the launch traced here: 33.8 us
  starting transfers between devices  20 us (59%)
  Pallas kernels  8.43 us (25%)
  waiting for transfers between devices  4.46 us (13%)
  between operations  0.8 us (2%)
    ppermute x8, starting transfers between devices, swapped(): return lax.ppermute(value, axis, pairs)  14.2 us
    ppermute x4, starting transfers between devices, across(): return lax.ppermute(value, ('section', 'replica'), pairs)  5.78 us
    ppermute x4, waiting for transfers between devices, across(): return lax.ppermute(value, ('section', 'replica'), pairs)  3.49 us
    pallas_call x1, Pallas kernels, last(): pl.pallas_call(last_kernel, out_shape=(pltpu.HBM(held.shape, f32), pltpu....  2.24 us
    pallas_call x1, Pallas kernels, first(): pl.pallas_call(first_kernel, out_shape=(pltpu.SMEM(plan.shape, jnp.int32)...  1.69 us
    pallas_call x1, Pallas kernels, load(): pl.pallas_call(load_kernel, out_shape=(pltpu.SMEM((24,), jnp.int32), pltp...  1.68 us
    pallas_call x1, Pallas kernels, near(): pl.pallas_call(near_kernel, out_shape=(pltpu.SMEM(plan.shape, jnp.int32),...  1.65 us
    ppermute x8, waiting for transfers between devices, swapped(): return lax.ppermute(value, axis, pairs)  0.96 us
  transfers between devices with their start and end apart: 12, of which 7 were waited for; matrix products, arithmetic and copies ran while one was open for 0% of the time, Pallas kernels for 11%

profile of v5, /device:TPU:1, one launch (start us, length us, event | category | flops | bytes accessed | tf_op | source)
XLA Modules:
  0.0 33.8 jit_solution(17685152362468029208)
XLA Ops:
  0.7 1.7 %shard_map.148 = (s32[24]{0:T(128)S(4)}, s32[6,80]{1,0:T(8,128)S(4)}, f32[32,6]{1,0:T(8,128)S(1)}, bf16[6,16,384]{2,1,0:T(8,128)(2,1)S(1)}, bf16[16,384]{1,0:T(8,128)(2,1)S(1)}, /*index=5*/bf16[16,384]{1,0:T(8,128)(2,1)S(1)}) custom-call(s32[192]{0:T(256)} %src_in.1, s32[192]{0:T(256)} %lens_in.1, s32[6,80]{1,0:T(8,128)} %table_in.1, ...), custom_call_target="tpu_custom_call" | custom-call | flops 10000000000 | bytes 49152 | tf_op jit(solution)/shard_map/pallas_call | solution.py:136
  2.4 3.7 %collective-permute-start.2 = (f32[32,6]{1,0:T(8,128)S(1)}, f32[32,6]{1,0:T(8,128)S(1)}, u32[]{:S(2)}, u32[]{:S(2)}) collective-permute-start(f32[32,6]{1,0:T(8,128)S(1)} %get-tuple-element.38.gains), channel_id=1, source_target_pairs={{0,1},{1,0},{2,3},{3,2},{4,5},{5,4},{6,7},{7,6},{8,9},{9,8},{10,11... | collective-permute-start | bytes 2312 | tf_op jit(solution)/shard_map/ppermute | solution.py:29
  6.0 2.9 %collective-permute-start = (bf16[16,384]{1,0:T(8,128)(2,1)S(1)}, bf16[16,384]{1,0:T(8,128)(2,1)S(1)}, u32[]{:S(2)}, u32[]{:S(2)}) collective-permute-start(bf16[16,384]{1,0:T(8,128)(2,1)S(1)} %get-tuple-element.36), channel_id=1, source_target_pairs={{0,8},{2,10},{4,12},{6,14},{8,0},{10,2},{12,4},{14,6},{16,24},{18,... | collective-permute-start | bytes 36872 | tf_op jit(solution)/shard_map/ppermute | solution.py:29
  8.9 3.6 %collective-permute-start.1 = (bf16[16,384]{1,0:T(8,128)(2,1)S(1)}, bf16[16,384]{1,0:T(8,128)(2,1)S(1)}, u32[]{:S(2)}, u32[]{:S(2)}) collective-permute-start(bf16[16,384]{1,0:T(8,128)(2,1)S(1)} %get-tuple-element.37), channel_id=1, source_target_pairs={{0,32},{2,34},{4,36},{6,38},{8,40},{10,42},{12,44},{14,46},{16,48}... | collective-permute-start | bytes 36872 | tf_op jit(solution)/shard_map/ppermute | solution.py:29
  12.6 0.5 %collective-permute-start.3 = (bf16[16,8576]{1,0:T(8,128)(2,1)S(1)}, bf16[16,8576]{1,0:T(8,128)(2,1)S(1)}, u32[]{:S(2)}, u32[]{:S(2)}) collective-permute-start(bf16[16,8576]{1,0:T(8,128)(2,1)S(1)} %get-tuple-element.41), channel_id=1, source_target_pairs={{0,4},{2,6},{4,0},{6,2},{8,12},{10,14},{12,8},{14,10},{16,20},{18,... | collective-permute-start | bytes 823304 | tf_op jit(solution)/shard_map/ppermute | solution.py:29
  13.1 0.8 %collective-permute-start.4 = (bf16[16,8576]{1,0:T(8,128)(2,1)S(1)}, bf16[16,8576]{1,0:T(8,128)(2,1)S(1)}, u32[]{:S(2)}, u32[]{:S(2)}) collective-permute-start(bf16[16,8576]{1,0:T(8,128)(2,1)S(1)} %get-tuple-element.42), channel_id=1, source_target_pairs={{0,16},{2,18},{4,20},{6,22},{8,24},{10,26},{12,28},{14,30},{16,0},... | collective-permute-start | bytes 823304 | tf_op jit(solution)/shard_map/ppermute | solution.py:29
  13.8 0.3 collective-permute-start.5
  14.3 1.7 %shard_map.150 = (s32[24]{0:T(128)S(4)}, f32[32,6]{1,0:T(8,128)S(1)}, bf16[32,128]{1,0:T(8,128)(2,1)S(1)}, bf16[16,8448]{1,0:T(8,128)(2,1)S(1)}, bf16[16,8448]{1,0:T(8,128)(2,1)S(1)}) custom-call(s32[24]{0:T(128)S(4)} %get-tuple-element.34.plan, s32[6,80]{1,0:T(8,128)S(4)} %get-tuple-element.35.table, bf16[2,480,16,512]{3,2,1,0:T(8,128)(2,1)S(1)} %bitcast.15, ...), custom_call_target="tpu_custom_call" | custom-call | flops 251658240 | bytes 7864320 | tf_op jit(solution)/shard_map/pallas_call | solution.py:383
  15.9 1.6 %collective-permute-start.6 = (bf16[16,8448]{1,0:T(8,128)(2,1)S(1)}, bf16[16,8448]{1,0:T(8,128)(2,1)S(1)}, u32[]{:S(2)}, u32[]{:S(2)}) collective-permute-start(bf16[16,8448]{1,0:T(8,128)(2,1)S(1)} %get-tuple-element.51), channel_id=1, source_target_pairs={{0,8},{2,10},{4,12},{6,14},{8,0},{10,2},{12,4},{14,6},{16,24},{18,... | collective-permute-start | bytes 811016 | tf_op jit(solution)/shard_map/ppermute | solution.py:29
  17.6 0.9 %collective-permute-start.7 = (bf16[16,8448]{1,0:T(8,128)(2,1)S(1)}, bf16[16,8448]{1,0:T(8,128)(2,1)S(1)}, u32[]{:S(2)}, u32[]{:S(2)}) collective-permute-start(bf16[16,8448]{1,0:T(8,128)(2,1)S(1)} %get-tuple-element.52), channel_id=1, source_target_pairs={{0,32},{2,34},{4,36},{6,38},{8,40},{10,42},{12,44},{14,46},{16,48}... | collective-permute-start | bytes 811016 | tf_op jit(solution)/shard_map/ppermute | solution.py:29
  18.5 0.3 %shard_map.151 = (s32[24]{0:T(128)S(4)}, f32[16,8192]{1,0:T(8,128)S(1)}, f32[6,1,8192]{2,1,0:T(1,128)S(1)}, f32[6,1,8192]{2,1,0:T(1,128)S(1)}, f32[6,8192]{1,0:T(8,128)S(1)}) custom-call(s32[24]{0:T(128)S(4)} %get-tuple-element.39.plan, bf16[6,8192]{1,0:T(8,128)(2,1)S(1)} %bitcast.22, bf16[6,8192]{1,0:T(8,128)(2,1)S(1)} %bitcast.23, ...), custom_call_target="tpu_custom_call" | custom-call | flops 491520 | bytes 524288 | tf_op jit(solution)/shard_map/pallas_call | solution.py:309
  18.9 0.3 collective-permute-done.3.x0
  19.2 0.4 %collective-permute-done.4.x1 = bf16[16,8576]{1,0:T(8,128)(2,1)S(1)} collective-permute-done((bf16[16,8576]{1,0:T(8,128)(2,1)S(1)}, bf16[16,8576]{1,0:T(8,128)(2,1)S(1)}, u32[]{:S(2)}, u32[]{:S(2)}) %collective-permute-start.4) | collective-permute-done | bytes 274464 | tf_op jit(solution)/shard_map/ppermute | solution.py:29
  19.8 1.7 %shard_map.152 = (s32[24]{0:T(128)S(4)}, bf16[32,128]{1,0:T(8,128)(2,1)S(1)}, bf16[32,128]{1,0:T(8,128)(2,1)S(1)}, bf16[32,128]{1,0:T(8,128)(2,1)S(1)}) custom-call(s32[24]{0:T(128)S(4)} %get-tuple-element.40.plan, s32[6,80]{1,0:T(8,128)S(4)} %get-tuple-element.35.table, bf16[2,480,16,512]{3,2,1,0:T(8,128)(2,1)S(1)} %bitcast.16, ...), custom_call_target="tpu_custom_call" | custom-call | flops 251658240 | bytes 7864320 | tf_op jit(solution)/shard_map/pallas_call | solution.py:409
  21.5 4.2 %collective-permute-start.8 = (bf16[32,128]{1,0:T(8,128)(2,1)S(1)}, bf16[32,128]{1,0:T(8,128)(2,1)S(1)}, u32[]{:S(2)}, u32[]{:S(2)}) collective-permute-start(bf16[32,128]{1,0:T(8,128)(2,1)S(1)} %get-tuple-element.53), channel_id=1, source_target_pairs={{0,68},{2,70},{4,64},{6,66},{8,76},{10,78},{12,72},{14,74},{16,84}... | collective-permute-start | bytes 24584 | tf_op jit(solution)/shard_map/ppermute | solution.py:40
  25.7 0.5 %collective-permute-start.9 = (bf16[32,128]{1,0:T(8,128)(2,1)S(1)}, bf16[32,128]{1,0:T(8,128)(2,1)S(1)}, u32[]{:S(2)}, u32[]{:S(2)}) collective-permute-start(bf16[32,128]{1,0:T(8,128)(2,1)S(1)} %get-tuple-element.54), channel_id=1, source_target_pairs={{0,80},{2,82},{4,84},{6,86},{8,88},{10,90},{12,92},{14,94},{16,64}... | collective-permute-start | bytes 24584 | tf_op jit(solution)/shard_map/ppermute | solution.py:40
  26.2 0.6 %collective-permute-start.10 = (bf16[32,128]{1,0:T(8,128)(2,1)S(1)}, bf16[32,128]{1,0:T(8,128)(2,1)S(1)}, u32[]{:S(2)}, u32[]{:S(2)}) collective-permute-start(bf16[32,128]{1,0:T(8,128)(2,1)S(1)} %get-tuple-element.55), channel_id=1, source_target_pairs={{0,66},{2,64},{4,70},{6,68},{8,74},{10,72},{12,78},{14,76},{16,82}... | collective-permute-start | bytes 24584 | tf_op jit(solution)/shard_map/ppermute | solution.py:40
  26.8 0.5 %collective-permute-done.8.b0 = bf16[32,128]{1,0:T(8,128)(2,1)S(1)} collective-permute-done((bf16[32,128]{1,0:T(8,128)(2,1)S(1)}, bf16[32,128]{1,0:T(8,128)(2,1)S(1)}, u32[]{:S(2)}, u32[]{:S(2)}) %collective-permute-start.8) | collective-permute-done | bytes 8224 | tf_op jit(solution)/shard_map/ppermute | solution.py:40
  27.3 1.4 %collective-permute-done.9.b1 = bf16[32,128]{1,0:T(8,128)(2,1)S(1)} collective-permute-done((bf16[32,128]{1,0:T(8,128)(2,1)S(1)}, bf16[32,128]{1,0:T(8,128)(2,1)S(1)}, u32[]{:S(2)}, u32[]{:S(2)}) %collective-permute-start.9) | collective-permute-done | bytes 8224 | tf_op jit(solution)/shard_map/ppermute | solution.py:40
  28.7 0.5 %collective-permute-done.10.b2 = bf16[32,128]{1,0:T(8,128)(2,1)S(1)} collective-permute-done((bf16[32,128]{1,0:T(8,128)(2,1)S(1)}, bf16[32,128]{1,0:T(8,128)(2,1)S(1)}, u32[]{:S(2)}, u32[]{:S(2)}) %collective-permute-start.10) | collective-permute-done | bytes 8224 | tf_op jit(solution)/shard_map/ppermute | solution.py:40
  29.3 2.2 %shard_map.153 = (f32[6,16,8192]{2,1,0:T(8,128)}, bf16[8,9728]{1,0:T(8,128)(2,1)S(1)}, f32[6,32,128]{2,1,0:T(8,128)S(1)}) custom-call(s32[24]{0:T(128)S(4)} %get-tuple-element.44.plan, f32[32,6]{1,0:T(8,128)S(1)} %get-tuple-element.45.gains, f32[16,8192]{1,0:T(8,128)S(1)} %get-tuple-element.46.rate, f32[6,1,8192]{2,1,0:T(1,128)S(1)} %get-tuple-element.47.step_rows, ...), custom_call_target="tpu_custom_call" | custom-call | flops 6291456 | bytes 4718592 | tf_op jit(solution)/shard_map/pallas_call | solution.py:452
  31.5 0.5 %collective-permute-start.11 = (bf16[8,9728]{1,0:T(8,128)(2,1)S(1)}, bf16[8,9728]{1,0:T(8,128)(2,1)S(1)}, u32[]{:S(2)}, u32[]{:S(2)}) collective-permute-start(bf16[8,9728]{1,0:T(8,128)(2,1)S(1)} %get-tuple-element.56), channel_id=1, source_target_pairs={{0,64},{2,66},{4,68},{6,70},{8,72},{10,74},{12,76},{14,78},{16,80}... | collective-permute-start | bytes 466952 | tf_op jit(solution)/shard_map/ppermute | solution.py:40
  32.0 1.0 %collective-permute-done.11.final = bf16[8,9728]{1,0:T(8,128)(2,1)S(1)} collective-permute-done((bf16[8,9728]{1,0:T(8,128)(2,1)S(1)}, bf16[8,9728]{1,0:T(8,128)(2,1)S(1)}, u32[]{:S(2)}, u32[]{:S(2)}) %collective-permute-start.11) | collective-permute-done | bytes 155680 | tf_op jit(solution)/shard_map/ppermute | solution.py:40
  33.0 0.7 %shard_map.154 = (bf16[6,4096]{1,0:T(8,128)(2,1)}, bf16[6,8192]{1,0:T(8,128)(2,1)}) custom-call(s32[24]{0:T(128)S(4)} %get-tuple-element.44.plan, bf16[8,9728]{1,0:T(8,128)(2,1)S(1)} %collective-permute-done.11.final, f32[6,32,128]{2,1,0:T(8,128)S(1)} %get-tuple-element.57.placed), custom_call_target="tpu_custom_call" | custom-call | tf_op jit(solution)/shard_map/pallas_call | solution.py:498
  (28 shorter events, 0.4 us)
Async XLA Ops:
  0.6 13.5 %slice-start = ((s8[15728640]{0:T(1024)(128)(4,1)}), s8[4194304]{0:T(1024)(128)(4,1)S(1)}, s32[]{:S(2)}) async-start(s8[15728640]{0:T(1024)(128)(4,1)} %bitcast.13), calls=%async_computation | async-start | bytes 8388608
  0.6 11.9 %copy-start = (f32[1,6,16,8192]{3,2,1,0:T(8,128)S(1)}, f32[1,6,16,8192]{3,2,1,0:T(8,128)}, u32[]{:S(2)}) copy-start(f32[1,6,16,8192]{3,2,1,0:T(8,128)} %param.19) | copy-start | bytes 9437188
  0.7 13.5 %slice-start.1 = ((s8[15728640]{0:T(1024)(128)(4,1)}), s8[4194304]{0:T(1024)(128)(4,1)S(1)}, s32[]{:S(2)}) async-start(s8[15728640]{0:T(1024)(128)(4,1)} %bitcast.13), calls=%async_computation.1 | async-start | bytes 8388608
  0.7 13.5 %slice-start.2 = ((s8[15728640]{0:T(1024)(128)(4,1)}), s8[4194304]{0:T(1024)(128)(4,1)S(1)}, s32[]{:S(2)}) async-start(s8[15728640]{0:T(1024)(128)(4,1)} %bitcast.13), calls=%async_computation.2 | async-start | bytes 8388608
  0.7 13.5 %slice-start.3 = ((s8[15728640]{0:T(1024)(128)(4,1)}), s8[3145728]{0:T(1024)(128)(4,1)S(1)}, s32[]{:S(2)}) async-start(s8[15728640]{0:T(1024)(128)(4,1)} %bitcast.13), calls=%async_computation.3 | async-start | bytes 6291456
  2.4 11.5 %collective-permute-start.2 = (f32[32,6]{1,0:T(8,128)S(1)}, f32[32,6]{1,0:T(8,128)S(1)}, u32[]{:S(2)}, u32[]{:S(2)}) collective-permute-start(f32[32,6]{1,0:T(8,128)S(1)} %get-tuple-element.38.gains), channel_id=1, source_target_pairs={{0,1},{1,0},{2,3},{3,2},{4,5},{5,4},{6,7},{7,6},{8,9},{9,8},{10,11... | collective-permute-start | bytes 2312 | tf_op jit(solution)/shard_map/ppermute | solution.py:29
  6.0 8.1 %collective-permute-start = (bf16[16,384]{1,0:T(8,128)(2,1)S(1)}, bf16[16,384]{1,0:T(8,128)(2,1)S(1)}, u32[]{:S(2)}, u32[]{:S(2)}) collective-permute-start(bf16[16,384]{1,0:T(8,128)(2,1)S(1)} %get-tuple-element.36), channel_id=1, source_target_pairs={{0,8},{2,10},{4,12},{6,14},{8,0},{10,2},{12,4},{14,6},{16,24},{18,... | collective-permute-start | bytes 36872 | tf_op jit(solution)/shard_map/ppermute | solution.py:29
  8.9 5.2 %collective-permute-start.1 = (bf16[16,384]{1,0:T(8,128)(2,1)S(1)}, bf16[16,384]{1,0:T(8,128)(2,1)S(1)}, u32[]{:S(2)}, u32[]{:S(2)}) collective-permute-start(bf16[16,384]{1,0:T(8,128)(2,1)S(1)} %get-tuple-element.37), channel_id=1, source_target_pairs={{0,32},{2,34},{4,36},{6,38},{8,40},{10,42},{12,44},{14,46},{16,48}... | collective-permute-start | bytes 36872 | tf_op jit(solution)/shard_map/ppermute | solution.py:29
  12.6 6.6 %collective-permute-start.3 = (bf16[16,8576]{1,0:T(8,128)(2,1)S(1)}, bf16[16,8576]{1,0:T(8,128)(2,1)S(1)}, u32[]{:S(2)}, u32[]{:S(2)}) collective-permute-start(bf16[16,8576]{1,0:T(8,128)(2,1)S(1)} %get-tuple-element.41), channel_id=1, source_target_pairs={{0,4},{2,6},{4,0},{6,2},{8,12},{10,14},{12,8},{14,10},{16,20},{18,... | collective-permute-start | bytes 823304 | tf_op jit(solution)/shard_map/ppermute | solution.py:29
  13.1 6.5 %collective-permute-start.4 = (bf16[16,8576]{1,0:T(8,128)(2,1)S(1)}, bf16[16,8576]{1,0:T(8,128)(2,1)S(1)}, u32[]{:S(2)}, u32[]{:S(2)}) collective-permute-start(bf16[16,8576]{1,0:T(8,128)(2,1)S(1)} %get-tuple-element.42), channel_id=1, source_target_pairs={{0,16},{2,18},{4,20},{6,22},{8,24},{10,26},{12,28},{14,30},{16,0},... | collective-permute-start | bytes 823304 | tf_op jit(solution)/shard_map/ppermute | solution.py:29
  13.8 6.0 %collective-permute-start.5 = (bf16[16,8576]{1,0:T(8,128)(2,1)S(1)}, bf16[16,8576]{1,0:T(8,128)(2,1)S(1)}, u32[]{:S(2)}, u32[]{:S(2)}) collective-permute-start(bf16[16,8576]{1,0:T(8,128)(2,1)S(1)} %get-tuple-element.43), channel_id=1, source_target_pairs={{0,2},{2,0},{4,6},{6,4},{8,10},{10,8},{12,14},{14,12},{16,18},{18,... | collective-permute-start | bytes 823304 | tf_op jit(solution)/shard_map/ppermute | solution.py:29
  14.2 4.3 %copy-start.1 = (f32[1,16,8192]{2,1,0:T(8,128)S(1)}, f32[1,16,8192]{2,1,0:T(8,128)}, u32[]{:S(2)}) copy-start(f32[1,16,8192]{2,1,0:T(8,128)} %param.23) | copy-start | bytes 1572868
  14.2 4.3 %copy-start.2 = (bf16[1,6,8192]{2,1,0:T(8,128)(2,1)S(1)}, bf16[1,6,8192]{2,1,0:T(8,128)(2,1)}, u32[]{:S(2)}) copy-start(bf16[1,6,8192]{2,1,0:T(8,128)(2,1)} %param.20) | copy-start | bytes 294916
  14.2 4.3 %copy-start.3 = (bf16[1,6,8192]{2,1,0:T(8,128)(2,1)S(1)}, bf16[1,6,8192]{2,1,0:T(8,128)(2,1)}, u32[]{:S(2)}) copy-start(bf16[1,6,8192]{2,1,0:T(8,128)(2,1)} %param.21) | copy-start | bytes 294916
  14.2 4.3 %copy-start.4 = (f32[1,8192]{1,0:T(1,128)S(1)}, f32[1,8192]{1,0:T(1,128)}, u32[]{:S(2)}) copy-start(f32[1,8192]{1,0:T(1,128)} %bias.1) | copy-start | bytes 98308
  14.2 4.3 %copy-start.5 = (f32[1,8192]{1,0:T(1,128)S(1)}, f32[1,8192]{1,0:T(1,128)}, u32[]{:S(2)}) copy-start(f32[1,8192]{1,0:T(1,128)} %skip.1) | copy-start | bytes 98308
  15.9 10.8 %collective-permute-start.6 = (bf16[16,8448]{1,0:T(8,128)(2,1)S(1)}, bf16[16,8448]{1,0:T(8,128)(2,1)S(1)}, u32[]{:S(2)}, u32[]{:S(2)}) collective-permute-start(bf16[16,8448]{1,0:T(8,128)(2,1)S(1)} %get-tuple-element.51), channel_id=1, source_target_pairs={{0,8},{2,10},{4,12},{6,14},{8,0},{10,2},{12,4},{14,6},{16,24},{18,... | collective-permute-start | bytes 811016 | tf_op jit(solution)/shard_map/ppermute | solution.py:29
  17.6 9.2 %collective-permute-start.7 = (bf16[16,8448]{1,0:T(8,128)(2,1)S(1)}, bf16[16,8448]{1,0:T(8,128)(2,1)S(1)}, u32[]{:S(2)}, u32[]{:S(2)}) collective-permute-start(bf16[16,8448]{1,0:T(8,128)(2,1)S(1)} %get-tuple-element.52), channel_id=1, source_target_pairs={{0,32},{2,34},{4,36},{6,38},{8,40},{10,42},{12,44},{14,46},{16,48}... | collective-permute-start | bytes 811016 | tf_op jit(solution)/shard_map/ppermute | solution.py:29
  21.5 5.8 %collective-permute-start.8 = (bf16[32,128]{1,0:T(8,128)(2,1)S(1)}, bf16[32,128]{1,0:T(8,128)(2,1)S(1)}, u32[]{:S(2)}, u32[]{:S(2)}) collective-permute-start(bf16[32,128]{1,0:T(8,128)(2,1)S(1)} %get-tuple-element.53), channel_id=1, source_target_pairs={{0,68},{2,70},{4,64},{6,66},{8,76},{10,78},{12,72},{14,74},{16,84}... | collective-permute-start | bytes 24584 | tf_op jit(solution)/shard_map/ppermute | solution.py:40
  25.7 3.1 %collective-permute-start.9 = (bf16[32,128]{1,0:T(8,128)(2,1)S(1)}, bf16[32,128]{1,0:T(8,128)(2,1)S(1)}, u32[]{:S(2)}, u32[]{:S(2)}) collective-permute-start(bf16[32,128]{1,0:T(8,128)(2,1)S(1)} %get-tuple-element.54), channel_id=1, source_target_pairs={{0,80},{2,82},{4,84},{6,86},{8,88},{10,90},{12,92},{14,94},{16,64}... | collective-permute-start | bytes 24584 | tf_op jit(solution)/shard_map/ppermute | solution.py:40
  26.2 3.1 %collective-permute-start.10 = (bf16[32,128]{1,0:T(8,128)(2,1)S(1)}, bf16[32,128]{1,0:T(8,128)(2,1)S(1)}, u32[]{:S(2)}, u32[]{:S(2)}) collective-permute-start(bf16[32,128]{1,0:T(8,128)(2,1)S(1)} %get-tuple-element.55), channel_id=1, source_target_pairs={{0,66},{2,64},{4,70},{6,68},{8,74},{10,72},{12,78},{14,76},{16,82}... | collective-permute-start | bytes 24584 | tf_op jit(solution)/shard_map/ppermute | solution.py:40
  31.5 1.5 %collective-permute-start.11 = (bf16[8,9728]{1,0:T(8,128)(2,1)S(1)}, bf16[8,9728]{1,0:T(8,128)(2,1)S(1)}, u32[]{:S(2)}, u32[]{:S(2)}) collective-permute-start(bf16[8,9728]{1,0:T(8,128)(2,1)S(1)} %get-tuple-element.56), channel_id=1, source_target_pairs={{0,64},{2,66},{4,68},{6,70},{8,72},{10,74},{12,76},{14,78},{16,80}... | collective-permute-start | bytes 466952 | tf_op jit(solution)/shard_map/ppermute | solution.py:40
